TPU v7x, 512 devices: a whole 4x8x8 slice. The times are simulated.
512 devices in a mesh: node: 16 (over z, core), local: 32 (over y, x).
Axes of the slice: x: 4, y: 8, z: 8, core: 2. Of those that a mesh axis runs over, the one named last changes fastest.
Arguments:
- tokens: bfloat16 [8192, 2048], P(('node', 'local')), may hold values from -6 to 6
- grad_out: bfloat16 [8192, 2048], P(('node', 'local')), may hold values from -6 to 6
- expert_ids: int32 [8192, 8], P(('node', 'local')), may hold values from 0 to 127, all different within a row; in each aligned block of 16 rows (0 to 15, 16 to 31, ...) at most 2 rows name the same one
- scores: bfloat16 [8192, 8], P(('node', 'local')), may hold values from 0.049804688 to 0.5
- gate_weight: bfloat16 [16, 32, 192, 2048], P('node', 'local'), may hold values from -0.125 to 0.125
- up_weight: bfloat16 [16, 32, 192, 2048], P('node', 'local'), may hold values from -0.125 to 0.125
- down_weight: bfloat16 [16, 32, 192, 2048], P('node', 'local'), may hold values from -0.21875 to 0.21875
Outputs:
- d_tokens: bfloat16 [8192, 2048], P(('node', 'local'))
- d_scores: bfloat16 [8192, 8], P(('node', 'local'))
- d_gate_weight: bfloat16 [16, 32, 192, 2048], P('node', 'local')
- d_up_weight: bfloat16 [16, 32, 192, 2048], P('node', 'local')
- d_down_weight: bfloat16 [16, 32, 192, 2048], P('node', 'local')
Inputs may be any that keep to these rules, and one draw needn't show every extreme that they name: `expert_ids`: each row names 8 different experts. Among the 16 rows of one device (aligned blocks of rows) no expert is named more than 2 times, and in every draw some expert is named exactly 2 times in some block.
All inputs are finite; a program needn't handle non-finite values.
Results may differ from a plain program's by a relative error of at most 0.017.
Values may be sent and summed in bfloat16 or wider, within the bound.
No kernel may reach another device: no remote copies, remote signals or barrier semaphores. Data moves between devices by JAX's collectives and lax.ppermute only.
A program may use at most 64 MiB of HBM per device.

v0:
```python
import jax
import jax.numpy as jnp
from jax import lax
from jax.sharding import PartitionSpec as P

TOP = 8
EXP_NODE = 8


def for_sending(shard):

    def short(part):
        return part.astype(jnp.bfloat16) if part.dtype == jnp.float32 else part

    return jax.tree.map(short, shard)


def on_device(tokens, grad_out, expert_ids, scores, gate_weight, up_weight, down_weight):
    node_count = lax.axis_size("node")
    local_count = lax.axis_size("local")
    expert_count = EXP_NODE * node_count
    shards = local_count // EXP_NODE
    tok_count = tokens.shape[0]
    width = tokens.shape[1]
    capacity = max(2, 2 * tok_count * TOP // expert_count)
    slot_count = expert_count * capacity
    flat_ids = expert_ids.reshape(-1)
    expert_iota = jnp.arange(expert_count, dtype=jnp.int32)
    matches = (flat_ids[:, None] == expert_iota[None, :]).astype(jnp.int32)
    rank_within = jnp.sum((jnp.cumsum(matches, axis=0) - matches) * matches, axis=1)
    slot_index = (flat_ids % EXP_NODE * node_count + flat_ids // EXP_NODE) * capacity + rank_within
    placed = jnp.arange(slot_count, dtype=jnp.int32)[:, None] == slot_index[None, :]
    token_map = placed.reshape(slot_count, tok_count, TOP).sum(axis=2).astype(jnp.bfloat16)
    send_x = jnp.dot(token_map, tokens, preferred_element_type=jnp.float32).astype(jnp.bfloat16)
    send_dy = jnp.dot(token_map, grad_out, preferred_element_type=jnp.float32).astype(jnp.bfloat16)
    send_s = jnp.sum(jnp.where(placed, scores.reshape(-1)[None, :], 0), axis=1)
    outgoing = (
        send_x.reshape(EXP_NODE, node_count, capacity, width),
        send_dy.reshape(EXP_NODE, node_count, capacity, width),
        send_s.reshape(EXP_NODE, node_count, capacity),
    )
    at_nodes = (
        lax.all_to_all(outgoing[0], "node", split_axis=1, concat_axis=1, tiled=True),
        lax.all_to_all(outgoing[1], "node", split_axis=1, concat_axis=1, tiled=True),
        lax.all_to_all(outgoing[2], "node", split_axis=1, concat_axis=1, tiled=True),
    )
    spread = tuple(
        (
            jnp.broadcast_to(member[:, None], (EXP_NODE, shards) + member.shape[1:]).reshape(
                (local_count,) + member.shape[1:]
            )
            for member in at_nodes
        )
    )
    rows_x, rows_dy, rows_s = jax.tree.map(
        lambda part, own: part.astype(own.dtype),
        lax.all_to_all(for_sending(spread), "local", split_axis=0, concat_axis=0, tiled=True),
        spread,
    )
    block_lead = 1
    x_rows = rows_x.reshape(-1, width)
    dy_rows = rows_dy.reshape(-1, width)
    s_rows = rows_s.reshape(-1).astype(jnp.float32)
    w_gate = gate_weight[0, 0]
    w_up = up_weight[0, 0]
    w_down = down_weight[0, 0]
    contract_cols = (((1,), (1,)), ((), ()))
    contract_rows = (((0,), (0,)), ((), ()))
    pre_gate = lax.dot_general(x_rows, w_gate, contract_cols, preferred_element_type=jnp.float32)
    pre_up = lax.dot_general(x_rows, w_up, contract_cols, preferred_element_type=jnp.float32)
    logistic = jax.nn.sigmoid(pre_gate)
    act = (pre_gate * logistic * pre_up).astype(jnp.bfloat16)
    back = lax.dot_general(dy_rows, w_down, contract_cols, preferred_element_type=jnp.float32)
    score_part = jnp.sum(act.astype(jnp.float32) * back, axis=1).astype(jnp.bfloat16)
    scaled = (s_rows[:, None] * dy_rows).astype(jnp.bfloat16)
    d_act = s_rows[:, None] * back
    d_pre_gate = (d_act * pre_up * logistic * (1.0 + pre_gate * (1.0 - logistic))).astype(
        jnp.bfloat16
    )
    d_pre_up = (d_act * pre_gate * logistic).astype(jnp.bfloat16)
    partial_rows = (
        jnp.dot(d_pre_gate, w_gate, preferred_element_type=jnp.float32)
        + jnp.dot(d_pre_up, w_up, preferred_element_type=jnp.float32)
    ).astype(jnp.bfloat16)
    d_gate_weight = lax.dot_general(
        d_pre_gate, x_rows, contract_rows, preferred_element_type=jnp.float32
    ).astype(jnp.bfloat16)[None, None]
    d_up_weight = lax.dot_general(
        d_pre_up, x_rows, contract_rows, preferred_element_type=jnp.float32
    ).astype(jnp.bfloat16)[None, None]
    d_down_weight = lax.dot_general(
        act, scaled, contract_rows, preferred_element_type=jnp.float32
    ).astype(jnp.bfloat16)[None, None]
    returning = (
        partial_rows.reshape(block_lead, local_count, -1, capacity, width),
        score_part.reshape(block_lead, local_count, -1, capacity),
    )
    came_x, came_s = (
        lax.all_to_all(returning[0], "local", split_axis=1, concat_axis=0, tiled=True),
        lax.all_to_all(returning[1], "local", split_axis=1, concat_axis=0, tiled=True),
    )
    slot_grad = jnp.sum(
        came_x.reshape(EXP_NODE, shards, node_count, capacity, width).astype(jnp.float32), axis=1
    ).astype(jnp.bfloat16)
    slot_score = jnp.sum(
        came_s.reshape(EXP_NODE, shards, node_count, capacity).astype(jnp.float32), axis=1
    ).astype(jnp.bfloat16)
    home_x, home_s = (
        lax.all_to_all(slot_grad, "node", split_axis=1, concat_axis=1, tiled=True),
        lax.all_to_all(slot_score, "node", split_axis=1, concat_axis=1, tiled=True),
    )
    home_flat = home_x.reshape(slot_count, width)
    d_tokens = lax.dot_general(
        token_map, home_flat, contract_rows, preferred_element_type=jnp.float32
    ).astype(jnp.bfloat16)
    score_flat = home_s.reshape(slot_count).astype(jnp.float32)
    d_scores = (
        jnp.sum(jnp.where(placed, score_flat[:, None], 0.0), axis=0)
        .reshape(tok_count, TOP)
        .astype(jnp.bfloat16)
    )
    return (d_tokens, d_scores, d_gate_weight, d_up_weight, d_down_weight)


def solution(mesh):
    return jax.shard_map(
        on_device,
        mesh=mesh,
        in_specs=(
            P(("node", "local"), None),
            P(("node", "local"), None),
            P(("node", "local"), None),
            P(("node", "local"), None),
            P("node", "local", None, None),
            P("node", "local", None, None),
            P("node", "local", None, None),
        ),
        out_specs=(
            P(("node", "local"), None),
            P(("node", "local"), None),
            P("node", "local", None, None),
            P("node", "local", None, None),
            P("node", "local", None, None),
        ),
        check_vma=False,
    )
```

profile of v0, /device:TPU:1, one launch (start us, length us, event | category | flops | bytes accessed | tf_op | source)
XLA Modules:
  0.0 508.0 jit_solution(12981022623738255920)
XLA Ops:
  0.7 0.9 copy.106
  1.6 0.8 copy.101
  3.2 0.8 copy.107
  4.0 11.8 %all-to-all-start = ((bf16[8,16,2]{0,2,1:T(2,128)(2,1)}), bf16[8,16,2]{0,2,1:T(2,128)(2,1)S(1)}, u32[]{:S(2)}, u32[]{:S(2)}) async-start(bf16[8,16,2]{0,2,1:T(2,128)(2,1)} %copy.107), calls=%async_computation | async-start | bytes 16384 | tf_op jit(solution)/shard_map/all_to_all | solution.py:45
  16.1 6.7 %all-to-all-done = bf16[8,16,2]{0,2,1:T(2,128)(2,1)S(1)} async-done(((bf16[8,16,2]{0,2,1:T(2,128)(2,1)}), bf16[8,16,2]{0,2,1:T(2,128)(2,1)S(1)}, u32[]{:S(2)}, u32[]{:S(2)}) %all-to-all-start) | async-done | bytes 544 | tf_op jit(solution)/shard_map/all_to_all | solution.py:45
  23.5 9.7 %all-to-all-start.1 = ((bf16[32,16,2]{1,2,0:T(2,128)(2,1)}), bf16[32,16,2]{1,2,0:T(2,128)(2,1)S(1)}, u32[]{:S(2)}, u32[]{:S(2)}) async-start(bf16[32,16,2]{1,2,0:T(2,128)(2,1)} %bitcast), calls=%async_computation.1 | async-start | bytes 32768 | tf_op jit(solution)/shard_map/all_to_all | solution.py:57
  33.2 1.3 convolution_convert_fusion
  34.5 0.7 reshape.159
  35.2 2.0 copy.113
  37.2 4.5 all-to-all-done.1
  41.7 5.5 %all-to-all-start.4 = ((bf16[8,16,2,2048]{3,2,0,1:T(2,128)(2,1)}), bf16[8,16,2,2048]{3,2,0,1:T(2,128)(2,1)S(1)}, u32[]{:S(2)}, u32[]{:S(2)}) async-start(bf16[8,16,2,2048]{3,2,0,1:T(2,128)(2,1)} %copy.113), calls=%async_computation.4 | async-start | bytes 2097152 | tf_op jit(solution)/shard_map/all_to_all | solution.py:43
  47.2 1.5 convolution_convert_fusion.1
  48.7 1.7 reshape.156
  50.4 2.0 copy.111
  52.5 22.7 %all-to-all-done.4 = bf16[8,16,2,2048]{3,2,0,1:T(2,128)(2,1)S(1)} async-done(((bf16[8,16,2,2048]{3,2,0,1:T(2,128)(2,1)}), bf16[8,16,2,2048]{3,2,0,1:T(2,128)(2,1)S(1)}, u32[]{:S(2)}, u32[]{:S(2)}) %all-to-all-start.4) | async-done | bytes 1048608 | tf_op jit(solution)/shard_map/all_to_all | solution.py:43
  75.2 4.2 all-to-all-start.2
  79.4 0.8 copy.114
  80.3 26.5 %all-to-all-done.2 = bf16[8,16,2,2048]{3,2,0,1:T(2,128)(2,1)} async-done(((bf16[8,16,2,2048]{3,2,0,1:T(2,128)(2,1)}), bf16[8,16,2,2048]{3,2,0,1:T(2,128)(2,1)}, u32[]{:S(2)}, u32[]{:S(2)}) %all-to-all-start.2) | async-done | bytes 1048608 | tf_op jit(solution)/shard_map/all_to_all | solution.py:44
  106.7 5.9 %broadcast_in_dim.64 = bf16[8,4,16,2,2048]{4,3,2,1,0:T(2,128)(2,1)} broadcast(bf16[8,16,2,2048]{3,2,1,0:T(2,128)(2,1)S(1)} %copy.114), dimensions={0,2,3,4} | broadcast | bytes 5242880 | tf_op jit(solution)/shard_map/broadcast_in_dim | solution.py:49
  112.6 4.9 all-to-all-start.5
  117.5 2.1 copy.112
  119.5 91.0 %all-to-all-done.5 = bf16[32,16,2,2048]{3,2,1,0:T(2,128)(2,1)} async-done(((bf16[32,16,2,2048]{3,2,1,0:T(2,128)(2,1)}), bf16[32,16,2,2048]{3,2,1,0:T(2,128)(2,1)}, u32[]{:S(2)}, u32[]{:S(2)}) %all-to-all-start.5) | async-done | bytes 4194336 | tf_op jit(solution)/shard_map/all_to_all | solution.py:57
  210.6 5.8 %broadcast_in_dim.63 = bf16[8,4,16,2,2048]{4,3,2,1,0:T(2,128)(2,1)} broadcast(bf16[8,16,2,2048]{3,2,1,0:T(2,128)(2,1)S(1)} %copy.112), dimensions={0,2,3,4} | broadcast | bytes 5242880 | tf_op jit(solution)/shard_map/broadcast_in_dim | solution.py:49
  216.4 9.1 %all-to-all-start.3 = ((bf16[32,16,2,2048]{3,2,1,0:T(2,128)(2,1)}), bf16[32,16,2,2048]{3,2,1,0:T(2,128)(2,1)}, u32[]{:S(2)}, u32[]{:S(2)}) async-start(bf16[32,16,2,2048]{3,2,1,0:T(2,128)(2,1)} %bitcast.40), calls=%async_computation.3 | async-start | bytes 8388608 | tf_op jit(solution)/shard_map/all_to_all | solution.py:57
  225.9 7.2 %reshape.161 = bf16[1024,2048]{1,0:T(8,128)(2,1)} reshape(bf16[32,16,2,2048]{3,2,1,0:T(2,128)(2,1)} %all-to-all-done.5) | data formatting | bytes 8388608 | tf_op jit(solution)/shard_map/reshape | solution.py:61
  233.1 4.7 fusion.8
  237.9 2.5 fusion.11
  240.3 78.3 %all-to-all-done.3 = bf16[32,16,2,2048]{3,2,1,0:T(2,128)(2,1)} async-done(((bf16[32,16,2,2048]{3,2,1,0:T(2,128)(2,1)}), bf16[32,16,2,2048]{3,2,1,0:T(2,128)(2,1)}, u32[]{:S(2)}, u32[]{:S(2)}) %all-to-all-start.3) | async-done | bytes 4194336 | tf_op jit(solution)/shard_map/all_to_all | solution.py:57
  318.6 7.2 %reshape.158 = bf16[1024,2048]{1,0:T(8,128)(2,1)} reshape(bf16[32,16,2,2048]{3,2,1,0:T(2,128)(2,1)} %all-to-all-done.3) | data formatting | bytes 8388608 | tf_op jit(solution)/shard_map/reshape | solution.py:62
  325.8 4.7 multiply_reduce_fusion
  330.8 0.9 copy.118
  331.7 8.3 %all-to-all-start.8 = ((bf16[1,32,16,2]{2,3,0,1:T(2,128)(2,1)}), bf16[1,32,16,2]{2,3,0,1:T(2,128)(2,1)S(1)}, u32[]{:S(2)}, u32[]{:S(2)}) async-start(bf16[1,32,16,2]{2,3,0,1:T(2,128)(2,1)} %copy.118), calls=%async_computation.8 | async-start | bytes 32768 | tf_op jit(solution)/shard_map/all_to_all | solution.py:100
  340.0 1.3 fusion.6
  341.3 3.3 add_convert_fusion
  344.6 7.7 %reshape.162 = bf16[1,32,16,2,2048]{4,3,2,1,0:T(2,128)(2,1)} reshape(bf16[1024,2048]{1,0:T(8,128)(2,1)} %add_convert_fusion) | data formatting | bytes 8388608 | tf_op jit(solution)/shard_map/reshape | solution.py:95
  352.3 9.3 %all-to-all-start.6 = ((bf16[1,32,16,2,2048]{4,3,2,0,1:T(2,128)(2,1)}), bf16[1,32,16,2,2048]{4,3,2,0,1:T(2,128)(2,1)}, u32[]{:S(2)}, u32[]{:S(2)}) async-start(bf16[1,32,16,2,2048]{4,3,2,0,1:T(2,128)(2,1)} %bitcast.42), calls=%async_computation.6 | async-start | bytes 8388608 | tf_op jit(solution)/shard_map/all_to_all | solution.py:99
  361.7 0.7 copy.119
  362.3 91.4 %all-to-all-done.6 = bf16[1,32,16,2,2048]{4,3,2,0,1:T(2,128)(2,1)} async-done(((bf16[1,32,16,2,2048]{4,3,2,0,1:T(2,128)(2,1)}), bf16[1,32,16,2,2048]{4,3,2,0,1:T(2,128)(2,1)}, u32[]{:S(2)}, u32[]{:S(2)}) %all-to-all-start.6) | async-done | bytes 4194336 | tf_op jit(solution)/shard_map/all_to_all | solution.py:99
  453.7 7.6 %all-to-all-start.9 = ((bf16[8,16,2]{0,2,1:T(2,128)(2,1)}), bf16[8,16,2]{0,2,1:T(2,128)(2,1)S(1)}, u32[]{:S(2)}, u32[]{:S(2)}) async-start(bf16[8,16,2]{0,2,1:T(2,128)(2,1)} %copy.119), calls=%async_computation.9 | async-start | bytes 16384 | tf_op jit(solution)/shard_map/all_to_all | solution.py:110
  461.3 7.3 %reduce_sum.78 = bf16[8,16,2,2048]{3,2,1,0:T(2,128)(2,1)S(1)} reduce(bf16[8,4,16,2,2048]{4,3,2,1,0:T(2,128)(2,1)} %bitcast.7, bf16[]{:T(256)} %constant.43.clone.1), dimensions={1}, to_apply=%region_4.5 | reduce | flops 1572864 | bytes 5242882 | tf_op jit(solution)/shard_map/reduce_sum | solution.py:102
  468.6 2.1 copy.116
  470.7 7.2 %all-to-all-start.7 = ((bf16[8,16,2,2048]{3,2,0,1:T(2,128)(2,1)}), bf16[8,16,2,2048]{3,2,0,1:T(2,128)(2,1)S(1)}, u32[]{:S(2)}, u32[]{:S(2)}) async-start(bf16[8,16,2,2048]{3,2,0,1:T(2,128)(2,1)} %copy.116), calls=%async_computation.7 | async-start | bytes 2097152 | tf_op jit(solution)/shard_map/all_to_all | solution.py:109
  477.9 4.2 fusion.3
  482.1 1.9 fusion.4
  484.0 2.0 fusion.5
  487.3 18.5 %all-to-all-done.7 = bf16[8,16,2,2048]{3,2,0,1:T(2,128)(2,1)S(1)} async-done(((bf16[8,16,2,2048]{3,2,0,1:T(2,128)(2,1)}), bf16[8,16,2,2048]{3,2,0,1:T(2,128)(2,1)S(1)}, u32[]{:S(2)}, u32[]{:S(2)}) %all-to-all-start.7) | async-done | bytes 1048608 | tf_op jit(solution)/shard_map/all_to_all | solution.py:109
  505.9 0.8 copy.117
  507.2 0.9 convolution_convert_fusion.4
  (41 shorter events, 4.3 us)
Async XLA Ops:
  0.6 232.5 %copy-start = (bf16[1,1,192,2048]{3,2,1,0:T(8,128)(2,1)S(1)}, bf16[1,1,192,2048]{3,2,1,0:T(8,128)(2,1)}, u32[]{:S(2)}) copy-start(bf16[1,1,192,2048]{3,2,1,0:T(8,128)(2,1)} %param.11) | copy-start | bytes 2359300
  0.6 46.6 %copy-start.6 = (bf16[16,2048]{1,0:T(8,128)(2,1)S(1)}, bf16[16,2048]{1,0:T(8,128)(2,1)}, u32[]{:S(2)}) copy-start(bf16[16,2048]{1,0:T(8,128)(2,1)} %param.8) | copy-start | bytes 196612
  4.0 18.8 %all-to-all-start = ((bf16[8,16,2]{0,2,1:T(2,128)(2,1)}), bf16[8,16,2]{0,2,1:T(2,128)(2,1)S(1)}, u32[]{:S(2)}, u32[]{:S(2)}) async-start(bf16[8,16,2]{0,2,1:T(2,128)(2,1)} %copy.107), calls=%async_computation | async-start | bytes 16384 | tf_op jit(solution)/shard_map/all_to_all | solution.py:45
  23.5 18.2 %all-to-all-start.1 = ((bf16[32,16,2]{1,2,0:T(2,128)(2,1)}), bf16[32,16,2]{1,2,0:T(2,128)(2,1)S(1)}, u32[]{:S(2)}, u32[]{:S(2)}) async-start(bf16[32,16,2]{1,2,0:T(2,128)(2,1)} %bitcast), calls=%async_computation.1 | async-start | bytes 32768 | tf_op jit(solution)/shard_map/all_to_all | solution.py:57
  41.7 33.5 %all-to-all-start.4 = ((bf16[8,16,2,2048]{3,2,0,1:T(2,128)(2,1)}), bf16[8,16,2,2048]{3,2,0,1:T(2,128)(2,1)S(1)}, u32[]{:S(2)}, u32[]{:S(2)}) async-start(bf16[8,16,2,2048]{3,2,0,1:T(2,128)(2,1)} %copy.113), calls=%async_computation.4 | async-start | bytes 2097152 | tf_op jit(solution)/shard_map/all_to_all | solution.py:43
  75.2 31.6 %all-to-all-start.2 = ((bf16[8,16,2,2048]{3,2,0,1:T(2,128)(2,1)}), bf16[8,16,2,2048]{3,2,0,1:T(2,128)(2,1)}, u32[]{:S(2)}, u32[]{:S(2)}) async-start(bf16[8,16,2,2048]{3,2,0,1:T(2,128)(2,1)} %copy.111), calls=%async_computation.2 | async-start | bytes 2097152 | tf_op jit(solution)/shard_map/all_to_all | solution.py:44
  112.6 98.0 %all-to-all-start.5 = ((bf16[32,16,2,2048]{3,2,1,0:T(2,128)(2,1)}), bf16[32,16,2,2048]{3,2,1,0:T(2,128)(2,1)}, u32[]{:S(2)}, u32[]{:S(2)}) async-start(bf16[32,16,2,2048]{3,2,1,0:T(2,128)(2,1)} %bitcast.41), calls=%async_computation.5 | async-start | bytes 8388608 | tf_op jit(solution)/shard_map/all_to_all | solution.py:57
  216.4 102.2 %all-to-all-start.3 = ((bf16[32,16,2,2048]{3,2,1,0:T(2,128)(2,1)}), bf16[32,16,2,2048]{3,2,1,0:T(2,128)(2,1)}, u32[]{:S(2)}, u32[]{:S(2)}) async-start(bf16[32,16,2,2048]{3,2,1,0:T(2,128)(2,1)} %bitcast.40), calls=%async_computation.3 | async-start | bytes 8388608 | tf_op jit(solution)/shard_map/all_to_all | solution.py:57
  233.1 4.8 copy-start.2
  233.1 4.8 copy-start.5
  331.7 20.6 %all-to-all-start.8 = ((bf16[1,32,16,2]{2,3,0,1:T(2,128)(2,1)}), bf16[1,32,16,2]{2,3,0,1:T(2,128)(2,1)S(1)}, u32[]{:S(2)}, u32[]{:S(2)}) async-start(bf16[1,32,16,2]{2,3,0,1:T(2,128)(2,1)} %copy.118), calls=%async_computation.8 | async-start | bytes 32768 | tf_op jit(solution)/shard_map/all_to_all | solution.py:100
  352.3 101.4 %all-to-all-start.6 = ((bf16[1,32,16,2,2048]{4,3,2,0,1:T(2,128)(2,1)}), bf16[1,32,16,2,2048]{4,3,2,0,1:T(2,128)(2,1)}, u32[]{:S(2)}, u32[]{:S(2)}) async-start(bf16[1,32,16,2,2048]{4,3,2,0,1:T(2,128)(2,1)} %bitcast.42), calls=%async_computation.6 | async-start | bytes 8388608 | tf_op jit(solution)/shard_map/all_to_all | solution.py:99
  453.7 17.0 %all-to-all-start.9 = ((bf16[8,16,2]{0,2,1:T(2,128)(2,1)}), bf16[8,16,2]{0,2,1:T(2,128)(2,1)S(1)}, u32[]{:S(2)}, u32[]{:S(2)}) async-start(bf16[8,16,2]{0,2,1:T(2,128)(2,1)} %copy.119), calls=%async_computation.9 | async-start | bytes 16384 | tf_op jit(solution)/shard_map/all_to_all | solution.py:110
  470.7 35.2 %all-to-all-start.7 = ((bf16[8,16,2,2048]{3,2,0,1:T(2,128)(2,1)}), bf16[8,16,2,2048]{3,2,0,1:T(2,128)(2,1)S(1)}, u32[]{:S(2)}, u32[]{:S(2)}) async-start(bf16[8,16,2,2048]{3,2,0,1:T(2,128)(2,1)} %copy.116), calls=%async_computation.7 | async-start | bytes 2097152 | tf_op jit(solution)/shard_map/all_to_all | solution.py:109
  477.9 4.2 copy-start.3
  477.9 6.1 %copy-start.4 = (bf16[1024,2048]{1,0:T(8,128)(2,1)S(1)}, bf16[1024,2048]{1,0:T(8,128)(2,1)}, u32[]{:S(2)}) copy-start(bf16[1024,2048]{1,0:T(8,128)(2,1)} %reshape.158) | copy-start | bytes 12582916
  484.0 24.0 %copy-start.1 = (bf16[1,1,192,2048]{3,2,1,0:T(8,128)(2,1)S(1)}, bf16[1,1,192,2048]{3,2,1,0:T(8,128)(2,1)}, u32[]{:S(2)}) copy-start(bf16[1,1,192,2048]{3,2,1,0:T(8,128)(2,1)} %param.11) | copy-start | bytes 2359300
where the time goes:
time: 509 us; the launch traced here: 508 us
  waiting for transfers between devices  340 us (67%)
  starting transfers between devices  77.7 us (15%)
  local copies, waits for them, and re-layouts  53.5 us (11%)
  matrix products  28.3 us (6%)
  other arithmetic  8.18 us (2%)
    all_to_all x3, waiting for transfers between devices, on_device(): lax.all_to_all(for_sending(spread), 'local', split_axis=0, concat_axis=0,...  174 us
    all_to_all x1, waiting for transfers between devices, on_device(): lax.all_to_all(returning[0], 'local', split_axis=1, concat_axis=0, tiled=...  91.4 us
    all_to_all x1, waiting for transfers between devices, on_device(): lax.all_to_all(outgoing[1], 'node', split_axis=1, concat_axis=1, tiled=True)  26.5 us
    all_to_all x3, starting transfers between devices, on_device(): lax.all_to_all(for_sending(spread), 'local', split_axis=0, concat_axis=0,...  23.6 us
    all_to_all x1, waiting for transfers between devices, on_device(): lax.all_to_all(outgoing[0], 'node', split_axis=1, concat_axis=1, tiled=True)  22.7 us
    all_to_all x1, waiting for transfers between devices, on_device(): lax.all_to_all(slot_grad, 'node', split_axis=1, concat_axis=1, tiled=True)  18.5 us
    broadcast_in_dim x3, local copies, waits for them, and re-layouts, on_device(): jnp.broadcast_to(member[:, None], (EXP_NODE, shards) + member.shape[1:])  12.3 us
    all_to_all x1, starting transfers between devices, on_device(): lax.all_to_all(outgoing[2], 'node', split_axis=1, concat_axis=1, tiled=True)  11.8 us
  transfers between devices with their start and end apart: 10, of which 8 were waited for; matrix products, arithmetic and copies ran while one was open for 12% of the time, Pallas kernels for 0%

commit v1 on v0

v1 whole, which is shorter than its diff:
```python
import functools

import jax
import jax.numpy as jnp
from jax import lax
from jax.experimental import pallas as pl
from jax.experimental.pallas import tpu as pltpu
from jax.sharding import Mesh
from jax.sharding import PartitionSpec as P

TOP = 8
EXP_NODE = 8
CAP = 2
LANES = 128
SUBLANES = 8
VMEM_BYTES = 40 << 20
FLOPS_TOTAL = 0

COLS = (((1,), (1,)), ((), ()))
ROWS = (((0,), (0,)), ((), ()))
PLAIN = (((1,), (0,)), ((), ()))


def dot(a, b, dims):
    return lax.dot_general(a, b, dims, preferred_element_type=jnp.float32)


def right(part, ring):
    return lax.ppermute(part, "block", [(i, (i + 1) % ring) for i in range(ring)])


def left(part, ring):
    return lax.ppermute(part, "block", [(i, (i - 1) % ring) for i in range(ring)])


def on_core(body, outs, flops, *operands):
    size = sum(v.size * v.dtype.itemsize for v in (*operands, *outs))
    return pl.pallas_call(
        body,
        out_shape=outs,
        in_specs=[pl.BlockSpec(memory_space=pltpu.VMEM)] * len(operands),
        out_specs=[pl.BlockSpec(memory_space=pltpu.VMEM)] * len(outs),
        compiler_params=pltpu.CompilerParams(vmem_limit_bytes=VMEM_BYTES),
        cost_estimate=pl.CostEstimate(flops=int(flops), bytes_accessed=size, transcendentals=0),
    )(*operands)


def halves(refs):
    if len(refs) == 2:
        return [ref[...] for ref in refs]
    half = refs[0].shape[1] // 2
    return [refs[0][:, :half], refs[0][:, half:]]


def prepare_body(width, rows_ref, scaled_ref, s_ref):
    s_lanes = rows_ref[:, 2 * width :].astype(jnp.float32)
    dy = rows_ref[:, width : 2 * width].astype(jnp.float32)
    scaled_ref[...] = (s_lanes[:, :1] * dy).astype(jnp.bfloat16)
    s_ref[...] = s_lanes.T[:SUBLANES]


def block_body(width, units, parts, rows_ref, scaled_ref, s_ref, *refs):
    weights, (grad_a, grad_b, d_pre_ref, d_s_ref) = halves(refs[:parts]), refs[parts:]
    half = width // 2
    x = [rows_ref[:, :half], rows_ref[:, half:width]]
    dy = [rows_ref[:, width : width + half], rows_ref[:, width + half : 2 * width]]
    pre = sum(dot(w[: 2 * units], v, COLS) for w, v in zip(weights, x))
    back = sum(dot(w[2 * units :], v, COLS) for w, v in zip(weights, dy))
    pre_gate, pre_up = pre[:units], pre[units:]
    logistic = 1.0 / (1.0 + jnp.exp(-pre_gate))
    act = (pre_gate * logistic * pre_up).astype(jnp.bfloat16)
    d_s = jnp.sum(act.astype(jnp.float32) * back, axis=0, keepdims=True)
    d_s_ref[...] = jnp.broadcast_to(d_s, d_s_ref.shape)
    d_act = s_ref[:1] * back
    d_gate = d_act * pre_up * logistic * (1.0 + pre_gate * (1.0 - logistic))
    d_up = d_act * pre_gate * logistic
    d_pre = jnp.concatenate([d_gate, d_up], axis=0)
    d_pre_ref[...] = d_pre.T.astype(jnp.bfloat16)
    d_pre = d_pre.astype(jnp.bfloat16)
    for i, grad in enumerate((grad_a, grad_b)):
        grad[: 2 * units] = dot(d_pre, x[i], PLAIN).astype(grad.dtype)
        grad[2 * units :] = dot(
            act, scaled_ref[:, i * half : (i + 1) * half], PLAIN
        ).astype(grad.dtype)


def input_body(width, units, parts, *refs):
    count = len(parts)
    d_pre, d_s, refs = refs[:count], refs[count : 2 * count], refs[2 * count :]
    weights, at = [], 0
    for part in parts:
        weights.append(halves(refs[at : at + part]))
        at += part
    out_ref = refs[at]
    half = width // 2
    for i in range(2):
        total = sum(dot(d_pre[b][...], weights[b][i][: 2 * units], PLAIN) for b in range(count))
        out_ref[:, i * half : (i + 1) * half] = total.astype(jnp.bfloat16)
    scores = sum(ref[...] for ref in d_s)[:1]
    scores = jnp.broadcast_to(scores, (LANES, scores.shape[1])).T
    out_ref[:, width:] = scores.astype(jnp.bfloat16)


def total_body(units, mine_a, mine_b, left_a, left_b, right_a, right_b, *outs):
    half = mine_a.shape[1]
    for j, out in enumerate(outs):
        rows = slice(j * units, (j + 1) * units)
        for i, three in enumerate(((mine_a, left_a, right_a), (mine_b, left_b, right_b))):
            out[:, i * half : (i + 1) * half] = sum(
                ref[rows].astype(jnp.float32) for ref in three
            ).astype(jnp.bfloat16)


def on_device(tokens, grad_out, expert_ids, scores, gate_weight, up_weight, down_weight):
    ring = lax.axis_size("block")
    expert_count = lax.axis_size("node") * lax.axis_size("expert")
    tok_count, width = tokens.shape
    units = gate_weight.shape[2]
    half = width // 2
    slot_count = expert_count * CAP
    bf16, f32 = jnp.bfloat16, jnp.float32
    shape = jax.ShapeDtypeStruct

    own = jnp.concatenate([gate_weight[0, 0], up_weight[0, 0], down_weight[0, 0]], axis=0)
    before = right(own, ring)
    after = left(own, ring)
    far_a = right(before[:, :half], ring)
    far_b = left(after[:, half:], ring)

    flat_ids = expert_ids.reshape(-1)
    expert_iota = jnp.arange(expert_count, dtype=jnp.int32)
    matches = (flat_ids[:, None] == expert_iota[None, :]).astype(jnp.int32)
    rank_within = jnp.sum((jnp.cumsum(matches, axis=0) - matches) * matches, axis=1)
    slot_index = flat_ids * CAP + rank_within
    placed = jnp.arange(slot_count, dtype=jnp.int32)[:, None] == slot_index[None, :]
    token_map = placed.reshape(slot_count, tok_count, TOP).sum(axis=2).astype(bf16)
    rows = dot(token_map, jnp.concatenate([tokens, grad_out], axis=1), PLAIN)
    slot_s = jnp.sum(jnp.where(placed, scores.reshape(-1)[None, :], 0), axis=1)
    outgoing = jnp.concatenate(
        [rows.astype(bf16), jnp.broadcast_to(slot_s[:, None], (slot_count, LANES))], axis=1
    )
    rows = lax.all_to_all(
        outgoing.reshape(expert_count, CAP, 2 * width + LANES), ("node", "expert"), 0, 0, tiled=True
    ).reshape(slot_count, 2 * width + LANES)
    scaled, s_rows = on_core(
        functools.partial(prepare_body, width),
        [shape((slot_count, width), bf16), shape((SUBLANES, slot_count), f32)],
        0,
        rows,
    )

    def block(weights, kinds):
        return on_core(
            functools.partial(block_body, width, units, len(weights)),
            [
                shape((3 * units, half), kinds[0]),
                shape((3 * units, half), kinds[1]),
                shape((slot_count, 2 * units), bf16),
                shape((SUBLANES, slot_count), f32),
            ],
            12 * slot_count * units * width,
            rows,
            scaled,
            s_rows,
            *weights,
        )

    blocks = ((far_a, far_b), (after,), (before,), (own,))
    far = block(blocks[0], (bf16, bf16))
    passing_a = right(far[0], ring)
    passing_b = left(far[1], ring)
    nxt = block(blocks[1], (f32, bf16))
    prev = block(blocks[2], (bf16, f32))
    left_b = right(nxt[1], ring)
    right_a = left(prev[0], ring)
    left_a = right((nxt[0] + passing_a.astype(f32)).astype(bf16), ring)
    right_b = left((prev[1] + passing_b.astype(f32)).astype(bf16), ring)
    mine = block(blocks[3], (f32, f32))
    d_gate, d_up, d_down = on_core(
        functools.partial(total_body, units),
        [shape((units, width), bf16)] * 3,
        FLOPS_TOTAL,
        *mine[:2],
        left_a,
        left_b,
        right_a,
        right_b,
    )

    terms = (far, nxt, prev, mine)
    (returning,) = on_core(
        functools.partial(input_body, width, units, [len(w) for w in blocks]),
        [shape((slot_count, width + LANES), bf16)],
        16 * slot_count * units * width,
        *[t[2] for t in terms],
        *[t[3] for t in terms],
        *[w for ws in blocks for w in ws],
    )
    home = lax.all_to_all(
        returning.reshape(expert_count, CAP, width + LANES), ("node", "expert"), 0, 0, tiled=True
    ).reshape(slot_count, width + LANES)
    d_tokens = dot(token_map, home[:, :width], ROWS).astype(bf16)
    d_scores = (
        jnp.sum(jnp.where(placed, home[:, width].astype(f32)[:, None], 0.0), axis=0)
        .reshape(tok_count, TOP)
        .astype(bf16)
    )
    return (d_tokens, d_scores, d_gate[None, None], d_up[None, None], d_down[None, None])


def solution(mesh):
    node_count, local_count = mesh.devices.shape
    mesh = Mesh(
        mesh.devices.reshape(node_count, EXP_NODE, local_count // EXP_NODE),
        ("node", "expert", "block"),
    )
    by_token = P(("node", "expert", "block"), None)
    by_block = P("node", ("expert", "block"), None, None)
    return jax.shard_map(
        on_device,
        mesh=mesh,
        in_specs=(by_token,) * 4 + (by_block,) * 3,
        out_specs=(by_token,) * 2 + (by_block,) * 3,
        check_vma=False,
    )
```

time: 509 us -> 224 us (0.44)
  waiting for transfers between devices: 340 us -> 96.3 us
  local copies, waits for them, and re-layouts: 53.5 us -> 24.6 us
  matrix products: 28.3 us -> 3.71 us
  Pallas kernels: 0 us -> 19.4 us
  starting transfers between devices: 77.7 us -> 68 us
    all_to_all x10 -> x2, waiting for transfers between devices: 340 us -> 15 us  [the longest x1 15 us: on_device(): lax.all_to_all(returning.reshape(expert_count, CAP, width + LANES), ('nod...]
    ppermute x0 -> x10, waiting for transfers between devices: none -> 81.4 us  [the longest x5 70.6 us: left(): lax.ppermute(part, 'block', [(i, (i - 1) % ring) for i in range(ring)])]
    all_to_all x10 -> x2, starting transfers between devices: 77.7 us -> 37 us  [the longest x1 19 us: on_device(): lax.all_to_all(outgoing.reshape(expert_count, CAP, 2 * width + LANES), ('...]
    ppermute x0 -> x10, starting transfers between devices: none -> 31 us  [the longest x5 19.6 us: left(): lax.ppermute(part, 'block', [(i, (i - 1) % ring) for i in range(ring)])]
    dot_general x11 -> x2, matrix products: 28.3 us -> 3.71 us  [dot(): return lax.dot_general(a, b, dims, preferred_element_type=jnp.float32)]
    reshape x10 -> x4, local copies, waits for them, and re-layouts: 29.9 us -> 8.54 us  [the longest x1 2.78 us: on_device(): rows = lax.all_to_all(outgoing.reshape(expert_count, CAP, 2 * width + LAN...]
    pallas_call x0 -> x7, Pallas kernels: none -> 19.4 us  [on_core(): pl.pallas_call(body, out_shape=outs, in_specs=[pl.BlockSpec(memory_space=...]
    broadcast_in_dim x4 -> x2, local copies, waits for them, and re-layouts: 12.4 us -> 0.19 us  [the longest x1 0.1 us: on_device(): jnp.broadcast_to(slot_s[:, None], (slot_count, LANES))]
  transfers between devices with their start and end apart: 10 -> 12, of which waited for: 8 -> 6; matrix products, arithmetic and copies ran while one was open for 12% -> 10% of each run, Pallas kernels for 0% -> 5%
where the time goes in v1:
time: 224 us; the launch traced here: 222 us
  waiting for transfers between devices  96.3 us (43%)
  starting transfers between devices  68 us (30%)
  local copies, waits for them, and re-layouts  24.6 us (11%)
  Pallas kernels  19.4 us (9%)
  other arithmetic  9.06 us (4%)
  matrix products  3.71 us (2%)
    ppermute x5, waiting for transfers between devices, left(): lax.ppermute(part, 'block', [(i, (i - 1) % ring) for i in range(ring)])  70.6 us
    ppermute x5, starting transfers between devices, left(): lax.ppermute(part, 'block', [(i, (i - 1) % ring) for i in range(ring)])  19.6 us
    pallas_call x7, Pallas kernels, on_core(): pl.pallas_call(body, out_shape=outs, in_specs=[pl.BlockSpec(memory_space=...  19.4 us
    all_to_all x1, starting transfers between devices, on_device(): lax.all_to_all(outgoing.reshape(expert_count, CAP, 2 * width + LANES), ('...  19 us
    all_to_all x1, starting transfers between devices, on_device(): lax.all_to_all(returning.reshape(expert_count, CAP, width + LANES), ('nod...  18.1 us
    all_to_all x1, waiting for transfers between devices, on_device(): lax.all_to_all(returning.reshape(expert_count, CAP, width + LANES), ('nod...  15 us
    unnamed x41, local copies, waits for them, and re-layouts  12 us
    ppermute x5, starting transfers between devices, right(): lax.ppermute(part, 'block', [(i, (i + 1) % ring) for i in range(ring)])  11.4 us
  transfers between devices with their start and end apart: 12, of which 6 were waited for; matrix products, arithmetic and copies ran while one was open for 10% of the time, Pallas kernels for 5%

profile of v1, /device:TPU:1, one launch (start us, length us, event | category | flops | bytes accessed | tf_op | source)
XLA Modules:
  0.0 222.2 jit_solution(239271974850261742)
XLA Ops:
  0.6 0.8 copy.25
  2.0 0.8 copy.27
  3.1 1.6 convolution_convert_fusion
  5.0 2.2 %reshape.46 = bf16[128,2,4224]{2,1,0:T(2,128)(2,1)} reshape(bf16[256,4224]{1,0:T(8,128)(2,1)S(1)} %pad_maximum_fusion.1) | data formatting | bytes 4325376 | tf_op jit(solution)/shard_map/reshape | solution.py:143
  7.3 19.0 %all-to-all-start = ((bf16[128,2,4224]{2,1,0:T(2,128)(2,1)}), bf16[128,2,4224]{2,1,0:T(2,128)(2,1)}, u32[]{:S(2)}, u32[]{:S(2)}) async-start(bf16[128,2,4224]{2,1,0:T(2,128)(2,1)} %reshape.46), calls=%async_computation | async-start | bytes 4325376 | tf_op jit(solution)/shard_map/all_to_all | solution.py:142
  26.3 0.3 pad_maximum_fusion.refs_0_.refs_12_
  26.6 4.4 %collective-permute-start.2 = (bf16[576,2048]{1,0:T(8,128)(2,1)S(1)}, bf16[576,2048]{1,0:T(8,128)(2,1)S(1)}, u32[]{:S(2)}, u32[]{:S(2)}) collective-permute-start(bf16[576,2048]{1,0:T(8,128)(2,1)S(1)} %pad_maximum_fusion.refs_0_.refs_12_), channel_id=1, source_target_pairs={{0,3},{1,0},{2,1},{3,2},{4,7},{5,4},{6,5},{7,6},{8,11},{9,8},{10,9... | collective-permute-start | bytes 7077896 | tf_op jit(solution)/shard_map/ppermute | solution.py:33
  31.0 1.9 collective-permute-start
  32.9 47.6 %collective-permute-done.2.refs_0_.refs_10_ = bf16[576,2048]{1,0:T(8,128)(2,1)S(1)} collective-permute-done((bf16[576,2048]{1,0:T(8,128)(2,1)S(1)}, bf16[576,2048]{1,0:T(8,128)(2,1)S(1)}, u32[]{:S(2)}, u32[]{:S(2)}) %collective-permute-start.2) | collective-permute-done | bytes 2359328 | tf_op jit(solution)/shard_map/ppermute | solution.py:33
  80.6 1.2 slice.17
  81.8 5.3 %collective-permute-start.3 = (bf16[576,1024]{1,0:T(8,128)(2,1)}, bf16[576,1024]{1,0:T(8,128)(2,1)S(1)}, u32[]{:S(2)}, u32[]{:S(2)}) collective-permute-start(bf16[576,1024]{1,0:T(8,128)(2,1)} %slice.17), channel_id=1, source_target_pairs={{0,3},{1,0},{2,1},{3,2},{4,7},{5,4},{6,5},{7,6},{8,11},{9,8},{10,9... | collective-permute-start | bytes 3538952 | tf_op jit(solution)/shard_map/ppermute | solution.py:33
  87.1 1.2 slice.16
  88.3 1.4 copy-done.5
  89.7 1.9 collective-permute-start.1
  91.6 2.8 %reshape.47.rows_ref = bf16[256,4224]{1,0:T(8,128)(2,1)S(1)} reshape(bf16[128,2,4224]{2,1,0:T(2,128)(2,1)} %all-to-all-done) | data formatting | bytes 4325376 | tf_op jit(solution)/shard_map/reshape | solution.py:144
  94.4 0.2 shard_map.110
  94.7 1.7 copy-done.1
  96.3 1.9 shard_map.114
  98.3 1.4 copy-done.11
  99.7 1.4 copy-done.13
  101.1 9.7 %collective-permute-done.3.refs_1_.refs_9_ = bf16[576,1024]{1,0:T(8,128)(2,1)S(1)} collective-permute-done((bf16[576,1024]{1,0:T(8,128)(2,1)}, bf16[576,1024]{1,0:T(8,128)(2,1)S(1)}, u32[]{:S(2)}, u32[]{:S(2)}) %collective-permute-start.3) | collective-permute-done | bytes 1179680 | tf_op jit(solution)/shard_map/ppermute | solution.py:33
  110.8 7.6 %collective-permute-done.1.refs_0_.refs_8_ = bf16[576,1024]{1,0:T(8,128)(2,1)} collective-permute-done((bf16[576,1024]{1,0:T(8,128)(2,1)}, bf16[576,1024]{1,0:T(8,128)(2,1)}, u32[]{:S(2)}, u32[]{:S(2)}) %collective-permute-start.1) | collective-permute-done | bytes 1179680 | tf_op jit(solution)/shard_map/ppermute | solution.py:29
  118.4 4.3 %shard_map.111 = (bf16[576,1024]{1,0:T(8,128)(2,1)}, bf16[576,1024]{1,0:T(8,128)(2,1)}, bf16[256,384]{1,0:T(8,128)(2,1)S(1)}, f32[8,256]{1,0:T(8,128)S(1)}) custom-call(bf16[256,4224]{1,0:T(8,128)(2,1)S(1)} %reshape.47.rows_ref, bf16[256,2048]{1,0:T(8,128)(2,1)S(1)} %get-tuple-element.26.scaled_ref, f32[8,256]{1,0:T(8,128)S(1)} %get-tuple-element.27.s_ref, ...), custom_call_target="tpu_custom_call" | custom-call | flops 1207959552 | bytes 8142848 | tf_op jit(solution)/shard_map/pallas_call | solution.py:38
  122.7 1.9 collective-permute-start.4
  124.7 4.9 %collective-permute-start.8 = (bf16[576,1024]{1,0:T(8,128)(2,1)}, bf16[576,1024]{1,0:T(8,128)(2,1)}, u32[]{:S(2)}, u32[]{:S(2)}) collective-permute-start(bf16[576,1024]{1,0:T(8,128)(2,1)} %get-tuple-element.43), channel_id=1, source_target_pairs={{0,3},{1,0},{2,1},{3,2},{4,7},{5,4},{6,5},{7,6},{8,11},{9,8},{10,9... | collective-permute-start | bytes 3538952 | tf_op jit(solution)/shard_map/ppermute | solution.py:33
  129.6 2.7 %shard_map.113 = (bf16[576,1024]{1,0:T(8,128)(2,1)}, f32[576,1024]{1,0:T(8,128)S(1)}, bf16[256,384]{1,0:T(8,128)(2,1)S(1)}, f32[8,256]{1,0:T(8,128)S(1)}) custom-call(bf16[256,4224]{1,0:T(8,128)(2,1)S(1)} %reshape.47.rows_ref, bf16[256,2048]{1,0:T(8,128)(2,1)S(1)} %get-tuple-element.26.scaled_ref, f32[8,256]{1,0:T(8,128)S(1)} %get-tuple-element.27.s_ref, ...), custom_call_target="tpu_custom_call" | custom-call | flops 1207959552 | bytes 9322496 | tf_op jit(solution)/shard_map/pallas_call | solution.py:38
  132.3 2.9 %shard_map.112 = (f32[576,1024]{1,0:T(8,128)S(1)}, bf16[576,1024]{1,0:T(8,128)(2,1)}, bf16[256,384]{1,0:T(8,128)(2,1)S(1)}, f32[8,256]{1,0:T(8,128)S(1)}) custom-call(bf16[256,4224]{1,0:T(8,128)(2,1)S(1)} %reshape.47.rows_ref, bf16[256,2048]{1,0:T(8,128)(2,1)S(1)} %get-tuple-element.26.scaled_ref, f32[8,256]{1,0:T(8,128)S(1)} %get-tuple-element.27.s_ref, ...), custom_call_target="tpu_custom_call" | custom-call | flops 1207959552 | bytes 9322496 | tf_op jit(solution)/shard_map/pallas_call | solution.py:38
  135.2 1.5 copy-done.7
  136.7 3.6 %shard_map.115 = bf16[256,2176]{1,0:T(8,128)(2,1)S(1)} custom-call(bf16[256,384]{1,0:T(8,128)(2,1)S(1)} %get-tuple-element.28.refs_0_, bf16[256,384]{1,0:T(8,128)(2,1)S(1)} %get-tuple-element.29.refs_1_, bf16[256,384]{1,0:T(8,128)(2,1)S(1)} %get-tuple-element.30.refs_2_, bf16[256,384]{1,0:T(8,128)(2,1)S(1)} %get-tuple-element.31.refs_3_, ...), custom_call_target="tpu_custom_call" | custom-call | flops 1610612736 | bytes 11370496 | tf_op jit(solution)/shard_map/pallas_call | solution.py:38
  140.3 1.2 reshape.48
  141.6 18.1 %all-to-all-start.1 = ((bf16[128,2,2176]{2,1,0:T(2,128)(2,1)}), bf16[128,2,2176]{2,1,0:T(2,128)(2,1)}, u32[]{:S(2)}, u32[]{:S(2)}) async-start(bf16[128,2,2176]{2,1,0:T(2,128)(2,1)} %reshape.48), calls=%async_computation.1 | async-start | bytes 2228224 | tf_op jit(solution)/shard_map/all_to_all | solution.py:199
  159.7 1.9 collective-permute-start.7
  161.6 3.4 %collective-permute-start.6 = (bf16[576,1024]{1,0:T(8,128)(2,1)}, bf16[576,1024]{1,0:T(8,128)(2,1)}, u32[]{:S(2)}, u32[]{:S(2)}) collective-permute-start(bf16[576,1024]{1,0:T(8,128)(2,1)} %get-tuple-element.40), channel_id=1, source_target_pairs={{0,1},{1,2},{2,3},{3,0},{4,5},{5,6},{6,7},{7,4},{8,9},{9,10},{10,1... | collective-permute-start | bytes 3538952 | tf_op jit(solution)/shard_map/ppermute | solution.py:29
  165.0 2.9 %add_convert_fusion = bf16[576,1024]{1,0:T(8,128)(2,1)} fusion(f32[576,1024]{1,0:T(8,128)S(1)} %copy-done.10, bf16[576,1024]{1,0:T(8,128)(2,1)} %collective-permute-done.8), kind=kLoop, calls=%fused_computation.2 | loop fusion | flops 1769472 | bytes 4718592 | tf_op jit(solution)/shard_map/convert_element_type | solution.py:177
  167.9 3.1 %collective-permute-start.9 = (bf16[576,1024]{1,0:T(8,128)(2,1)}, bf16[576,1024]{1,0:T(8,128)(2,1)S(1)}, u32[]{:S(2)}, u32[]{:S(2)}) collective-permute-start(bf16[576,1024]{1,0:T(8,128)(2,1)} %add_convert_fusion), channel_id=1, source_target_pairs={{0,3},{1,0},{2,1},{3,2},{4,7},{5,4},{6,5},{7,6},{8,11},{9,8},{10,9... | collective-permute-start | bytes 3538952 | tf_op jit(solution)/shard_map/ppermute | solution.py:33
  171.0 2.8 %add_convert_fusion.1 = bf16[576,1024]{1,0:T(8,128)(2,1)} fusion(f32[576,1024]{1,0:T(8,128)S(1)} %copy-done.8, bf16[576,1024]{1,0:T(8,128)(2,1)} %collective-permute-done.4), kind=kLoop, calls=%fused_computation.3 | loop fusion | flops 1769472 | bytes 4718592 | tf_op jit(solution)/shard_map/convert_element_type | solution.py:176
  173.8 2.3 %collective-permute-start.5 = (bf16[576,1024]{1,0:T(8,128)(2,1)}, bf16[576,1024]{1,0:T(8,128)(2,1)}, u32[]{:S(2)}, u32[]{:S(2)}) collective-permute-start(bf16[576,1024]{1,0:T(8,128)(2,1)} %add_convert_fusion.1), channel_id=1, source_target_pairs={{0,1},{1,2},{2,3},{3,0},{4,5},{5,6},{6,7},{7,4},{8,9},{9,10},{10,1... | collective-permute-start | bytes 3538952 | tf_op jit(solution)/shard_map/ppermute | solution.py:29
  176.1 15.0 %all-to-all-done.1 = bf16[128,2,2176]{2,1,0:T(2,128)(2,1)} async-done(((bf16[128,2,2176]{2,1,0:T(2,128)(2,1)}), bf16[128,2,2176]{2,1,0:T(2,128)(2,1)}, u32[]{:S(2)}, u32[]{:S(2)}) %all-to-all-start.1) | async-done | bytes 1114144 | tf_op jit(solution)/shard_map/all_to_all | solution.py:199
  191.1 2.3 %reshape.49 = bf16[256,2176]{1,0:T(8,128)(2,1)} reshape(bf16[128,2,2176]{2,1,0:T(2,128)(2,1)} %all-to-all-done.1) | data formatting | bytes 2228224 | tf_op jit(solution)/shard_map/reshape | solution.py:201
  193.4 0.9 convert_reduce_fusion
  194.3 1.3 select_reduce_fusion
  195.6 1.3 convert_element_type.45
  196.9 1.3 copy.28
  198.3 2.1 convolution_convert_fusion.1
  200.4 13.3 %collective-permute-done.9.right_b = bf16[576,1024]{1,0:T(8,128)(2,1)S(1)} collective-permute-done((bf16[576,1024]{1,0:T(8,128)(2,1)}, bf16[576,1024]{1,0:T(8,128)(2,1)S(1)}, u32[]{:S(2)}, u32[]{:S(2)}) %collective-permute-start.9) | collective-permute-done | bytes 1179680 | tf_op jit(solution)/shard_map/ppermute | solution.py:33
  213.7 3.1 %collective-permute-done.5.left_a = bf16[576,1024]{1,0:T(8,128)(2,1)} collective-permute-done((bf16[576,1024]{1,0:T(8,128)(2,1)}, bf16[576,1024]{1,0:T(8,128)(2,1)}, u32[]{:S(2)}, u32[]{:S(2)}) %collective-permute-start.5) | collective-permute-done | bytes 1179680 | tf_op jit(solution)/shard_map/ppermute | solution.py:29
  216.8 1.7 copy-done.14
  218.5 3.7 %shard_map.116 = (bf16[192,2048]{1,0:T(8,128)(2,1)}, bf16[192,2048]{1,0:T(8,128)(2,1)}, bf16[192,2048]{1,0:T(8,128)(2,1)}) custom-call(f32[576,1024]{1,0:T(8,128)S(1)} %copy-done.12, f32[576,1024]{1,0:T(8,128)S(1)} %copy-done.14, bf16[576,1024]{1,0:T(8,128)(2,1)} %collective-permute-done.5.left_a, bf16[576,1024]{1,0:T(8,128)(2,1)} %collective-permute-done.6.left_b, ...), custom_call_target="tpu_custom_call" | custom-call | bytes 11796480 | tf_op jit(solution)/shard_map/pallas_call | solution.py:38
  (50 shorter events, 1.3 us)
Async XLA Ops:
  1.9 2.8 %copy-start.18 = (s32[128]{0:T(128)}, s32[128]{0:T(128)S(1)}, u32[]{:S(2)}) copy-start(s32[128]{0:T(128)S(1)} %multiply_add_fusion.1) | copy-start | bytes 1540
  7.3 19.0 %copy-start.15 = (bf16[1,1,192,2048]{3,2,1,0:T(8,128)(2,1)S(1)}, bf16[1,1,192,2048]{3,2,1,0:T(8,128)(2,1)}, u32[]{:S(2)}) copy-start(bf16[1,1,192,2048]{3,2,1,0:T(8,128)(2,1)} %param.13) | copy-start | bytes 2359300
  7.3 19.0 %copy-start.16 = (bf16[1,1,192,2048]{3,2,1,0:T(8,128)(2,1)S(1)}, bf16[1,1,192,2048]{3,2,1,0:T(8,128)(2,1)}, u32[]{:S(2)}) copy-start(bf16[1,1,192,2048]{3,2,1,0:T(8,128)(2,1)} %param.12) | copy-start | bytes 2359300
  7.3 19.0 %copy-start.17 = (bf16[1,1,192,2048]{3,2,1,0:T(8,128)(2,1)S(1)}, bf16[1,1,192,2048]{3,2,1,0:T(8,128)(2,1)}, u32[]{:S(2)}) copy-start(bf16[1,1,192,2048]{3,2,1,0:T(8,128)(2,1)} %param.11) | copy-start | bytes 2359300
  7.3 84.3 %all-to-all-start = ((bf16[128,2,4224]{2,1,0:T(2,128)(2,1)}), bf16[128,2,4224]{2,1,0:T(2,128)(2,1)}, u32[]{:S(2)}, u32[]{:S(2)}) async-start(bf16[128,2,4224]{2,1,0:T(2,128)(2,1)} %reshape.46), calls=%async_computation | async-start | bytes 4325376 | tf_op jit(solution)/shard_map/all_to_all | solution.py:142
  26.6 61.7 %copy-start = (bf16[576,2048]{1,0:T(8,128)(2,1)}, bf16[576,2048]{1,0:T(8,128)(2,1)S(1)}, u32[]{:S(2)}) copy-start(bf16[576,2048]{1,0:T(8,128)(2,1)S(1)} %pad_maximum_fusion.refs_0_.refs_12_) | copy-start | bytes 7077892
  26.6 54.0 %collective-permute-start.2 = (bf16[576,2048]{1,0:T(8,128)(2,1)S(1)}, bf16[576,2048]{1,0:T(8,128)(2,1)S(1)}, u32[]{:S(2)}, u32[]{:S(2)}) collective-permute-start(bf16[576,2048]{1,0:T(8,128)(2,1)S(1)} %pad_maximum_fusion.refs_0_.refs_12_), channel_id=1, source_target_pairs={{0,3},{1,0},{2,1},{3,2},{4,7},{5,4},{6,5},{7,6},{8,11},{9,8},{10,9... | collective-permute-start | bytes 7077896 | tf_op jit(solution)/shard_map/ppermute | solution.py:33
  31.0 56.1 %collective-permute-start = (bf16[576,2048]{1,0:T(8,128)(2,1)S(1)}, bf16[576,2048]{1,0:T(8,128)(2,1)S(1)}, u32[]{:S(2)}, u32[]{:S(2)}) collective-permute-start(bf16[576,2048]{1,0:T(8,128)(2,1)S(1)} %pad_maximum_fusion.refs_0_.refs_12_), channel_id=1, source_target_pairs={{0,1},{1,2},{2,3},{3,0},{4,5},{5,6},{6,7},{7,4},{8,9},{9,10},{10,1... | collective-permute-start | bytes 7077896 | tf_op jit(solution)/shard_map/ppermute | solution.py:29
  80.5 7.7 %copy-start.3 = (bf16[576,2048]{1,0:T(8,128)(2,1)}, bf16[576,2048]{1,0:T(8,128)(2,1)S(1)}, u32[]{:S(2)}) copy-start(bf16[576,2048]{1,0:T(8,128)(2,1)S(1)} %collective-permute-done.2.refs_0_.refs_10_) | copy-start | bytes 7077892
  81.8 29.0 %collective-permute-start.3 = (bf16[576,1024]{1,0:T(8,128)(2,1)}, bf16[576,1024]{1,0:T(8,128)(2,1)S(1)}, u32[]{:S(2)}, u32[]{:S(2)}) collective-permute-start(bf16[576,1024]{1,0:T(8,128)(2,1)} %slice.17), channel_id=1, source_target_pairs={{0,3},{1,0},{2,1},{3,2},{4,7},{5,4},{6,5},{7,6},{8,11},{9,8},{10,9... | collective-permute-start | bytes 3538952 | tf_op jit(solution)/shard_map/ppermute | solution.py:33
  88.3 1.4 copy-start.5
  89.7 28.7 %collective-permute-start.1 = (bf16[576,1024]{1,0:T(8,128)(2,1)}, bf16[576,1024]{1,0:T(8,128)(2,1)}, u32[]{:S(2)}, u32[]{:S(2)}) collective-permute-start(bf16[576,1024]{1,0:T(8,128)(2,1)} %slice.16), channel_id=1, source_target_pairs={{0,1},{1,2},{2,3},{3,0},{4,5},{5,6},{6,7},{7,4},{8,9},{9,10},{10,1... | collective-permute-start | bytes 3538952 | tf_op jit(solution)/shard_map/ppermute | solution.py:29
  94.7 1.7 copy-start.1
  98.2 1.4 copy-start.11
  99.7 1.4 copy-start.13
  101.1 28.4 %copy-start.6 = (bf16[576,2048]{1,0:T(8,128)(2,1)S(1)}, bf16[576,2048]{1,0:T(8,128)(2,1)}, u32[]{:S(2)}) copy-start(bf16[576,2048]{1,0:T(8,128)(2,1)} %copy-done.5) | copy-start | bytes 7077892
  122.7 48.3 %collective-permute-start.4 = (bf16[576,1024]{1,0:T(8,128)(2,1)}, bf16[576,1024]{1,0:T(8,128)(2,1)}, u32[]{:S(2)}, u32[]{:S(2)}) collective-permute-start(bf16[576,1024]{1,0:T(8,128)(2,1)} %get-tuple-element.39), channel_id=1, source_target_pairs={{0,1},{1,2},{2,3},{3,0},{4,5},{5,6},{6,7},{7,4},{8,9},{9,10},{10,1... | collective-permute-start | bytes 3538952 | tf_op jit(solution)/shard_map/ppermute | solution.py:29
  124.6 7.6 %copy-start.4 = (bf16[576,2048]{1,0:T(8,128)(2,1)S(1)}, bf16[576,2048]{1,0:T(8,128)(2,1)}, u32[]{:S(2)}) copy-start(bf16[576,2048]{1,0:T(8,128)(2,1)} %copy-done.3) | copy-start | bytes 7077892
  124.7 40.3 %collective-permute-start.8 = (bf16[576,1024]{1,0:T(8,128)(2,1)}, bf16[576,1024]{1,0:T(8,128)(2,1)}, u32[]{:S(2)}, u32[]{:S(2)}) collective-permute-start(bf16[576,1024]{1,0:T(8,128)(2,1)} %get-tuple-element.43), channel_id=1, source_target_pairs={{0,3},{1,0},{2,1},{3,2},{4,7},{5,4},{6,5},{7,6},{8,11},{9,8},{10,9... | collective-permute-start | bytes 3538952 | tf_op jit(solution)/shard_map/ppermute | solution.py:33
  132.3 2.9 %copy-start.9 = (f32[576,1024]{1,0:T(8,128)}, f32[576,1024]{1,0:T(8,128)S(1)}, u32[]{:S(2)}) copy-start(f32[576,1024]{1,0:T(8,128)S(1)} %get-tuple-element.42) | copy-start | bytes 7077892
  132.3 4.4 %copy-start.2 = (bf16[576,2048]{1,0:T(8,128)(2,1)S(1)}, bf16[576,2048]{1,0:T(8,128)(2,1)}, u32[]{:S(2)}) copy-start(bf16[576,2048]{1,0:T(8,128)(2,1)} %copy-done) | copy-start | bytes 7077892
  135.2 1.5 copy-start.7
  140.3 24.7 %copy-start.10 = (f32[576,1024]{1,0:T(8,128)S(1)}, f32[576,1024]{1,0:T(8,128)}, u32[]{:S(2)}) copy-start(f32[576,1024]{1,0:T(8,128)} %copy-done.9) | copy-start | bytes 7077892
  141.6 49.5 %all-to-all-start.1 = ((bf16[128,2,2176]{2,1,0:T(2,128)(2,1)}), bf16[128,2,2176]{2,1,0:T(2,128)(2,1)}, u32[]{:S(2)}, u32[]{:S(2)}) async-start(bf16[128,2,2176]{2,1,0:T(2,128)(2,1)} %reshape.48), calls=%async_computation.1 | async-start | bytes 2228224 | tf_op jit(solution)/shard_map/all_to_all | solution.py:199
  159.7 40.7 %collective-permute-start.7 = (bf16[576,1024]{1,0:T(8,128)(2,1)}, bf16[576,1024]{1,0:T(8,128)(2,1)}, u32[]{:S(2)}, u32[]{:S(2)}) collective-permute-start(bf16[576,1024]{1,0:T(8,128)(2,1)} %get-tuple-element.41), channel_id=1, source_target_pairs={{0,3},{1,0},{2,1},{3,2},{4,7},{5,4},{6,5},{7,6},{8,11},{9,8},{10,9... | collective-permute-start | bytes 3538952 | tf_op jit(solution)/shard_map/ppermute | solution.py:33
  161.6 38.8 %collective-permute-start.6 = (bf16[576,1024]{1,0:T(8,128)(2,1)}, bf16[576,1024]{1,0:T(8,128)(2,1)}, u32[]{:S(2)}, u32[]{:S(2)}) collective-permute-start(bf16[576,1024]{1,0:T(8,128)(2,1)} %get-tuple-element.40), channel_id=1, source_target_pairs={{0,1},{1,2},{2,3},{3,0},{4,5},{5,6},{6,7},{7,4},{8,9},{9,10},{10,1... | collective-permute-start | bytes 3538952 | tf_op jit(solution)/shard_map/ppermute | solution.py:29
  165.0 6.0 %copy-start.8 = (f32[576,1024]{1,0:T(8,128)S(1)}, f32[576,1024]{1,0:T(8,128)}, u32[]{:S(2)}) copy-start(f32[576,1024]{1,0:T(8,128)} %copy-done.7) | copy-start | bytes 7077892
  167.9 45.8 %collective-permute-start.9 = (bf16[576,1024]{1,0:T(8,128)(2,1)}, bf16[576,1024]{1,0:T(8,128)(2,1)S(1)}, u32[]{:S(2)}, u32[]{:S(2)}) collective-permute-start(bf16[576,1024]{1,0:T(8,128)(2,1)} %add_convert_fusion), channel_id=1, source_target_pairs={{0,3},{1,0},{2,1},{3,2},{4,7},{5,4},{6,5},{7,6},{8,11},{9,8},{10,9... | collective-permute-start | bytes 3538952 | tf_op jit(solution)/shard_map/ppermute | solution.py:33
  173.8 43.0 %copy-start.12 = (f32[576,1024]{1,0:T(8,128)S(1)}, f32[576,1024]{1,0:T(8,128)}, u32[]{:S(2)}) copy-start(f32[576,1024]{1,0:T(8,128)} %copy-done.11) | copy-start | bytes 7077892
  173.8 43.0 %collective-permute-start.5 = (bf16[576,1024]{1,0:T(8,128)(2,1)}, bf16[576,1024]{1,0:T(8,128)(2,1)}, u32[]{:S(2)}, u32[]{:S(2)}) collective-permute-start(bf16[576,1024]{1,0:T(8,128)(2,1)} %add_convert_fusion.1), channel_id=1, source_target_pairs={{0,1},{1,2},{2,3},{3,0},{4,5},{5,6},{6,7},{7,4},{8,9},{9,10},{10,1... | collective-permute-start | bytes 3538952 | tf_op jit(solution)/shard_map/ppermute | solution.py:29
  216.8 1.7 copy-start.14

commit v2 on v1

v2 whole, which is shorter than its diff:
```python
import functools

import jax
import jax.numpy as jnp
from jax import lax
from jax.experimental import pallas as pl
from jax.experimental.pallas import tpu as pltpu
from jax.sharding import Mesh
from jax.sharding import PartitionSpec as P

TOP = 8
EXP_NODE = 8
CAP = 2
LANES = 128
SUBLANES = 8
VMEM_BYTES = 56 << 20
FLOPS_CUT = 2 * 10**10
FLOPS_PART = 3 * 10**10

COLS = (((1,), (1,)), ((), ()))
ROWS = (((0,), (0,)), ((), ()))
PLAIN = (((1,), (0,)), ((), ()))


def dot(a, b, dims):
    return lax.dot_general(a, b, dims, preferred_element_type=jnp.float32)


def right(part, ring):
    return lax.ppermute(part, "block", [(i, (i + 1) % ring) for i in range(ring)])


def left(part, ring):
    return lax.ppermute(part, "block", [(i, (i - 1) % ring) for i in range(ring)])


def on_core(body, far_ins, near_ins, far_outs, near_outs, flops):
    n_in, n_near, n_out = len(far_ins), len(near_ins), len(far_outs)
    size = sum(v.size * v.dtype.itemsize for v in (*far_ins, *near_ins, *far_outs, *near_outs))

    def kernel(*refs):
        ends = [n_in, n_near, n_out, len(near_outs), n_in, n_out, 1, 1]
        groups, at = [], 0
        for count in ends:
            groups.append(refs[at : at + count])
            at += count
        source, near_in, target, near_out, held_in, held_out, (in_sem,), (out_sem,) = groups
        incoming = [
            pltpu.make_async_copy(src, held, in_sem.at[i])
            for i, (src, held) in enumerate(zip(source, held_in))
        ]
        outgoing = [
            pltpu.make_async_copy(held, dst, out_sem.at[i])
            for i, (held, dst) in enumerate(zip(held_out, target))
        ]
        for copy in incoming:
            copy.start()
        body(
            [(copy.wait, held) for copy, held in zip(incoming, held_in)],
            near_in,
            [(copy.start, held) for copy, held in zip(outgoing, held_out)],
            near_out,
        )
        for copy in outgoing:
            copy.wait()

    hbm, vmem = pl.BlockSpec(memory_space=pltpu.HBM), pl.BlockSpec(memory_space=pltpu.VMEM)
    return pl.pallas_call(
        kernel,
        out_shape=[*far_outs, *near_outs],
        in_specs=[hbm] * n_in + [vmem] * n_near,
        out_specs=[hbm] * n_out + [vmem] * len(near_outs),
        scratch_shapes=[
            *[pltpu.VMEM(v.shape, v.dtype) for v in (*far_ins, *far_outs)],
            pltpu.SemaphoreType.DMA((n_in,)),
            pltpu.SemaphoreType.DMA((n_out,)),
        ],
        compiler_params=pltpu.CompilerParams(vmem_limit_bytes=VMEM_BYTES),
        cost_estimate=pl.CostEstimate(flops=int(flops), bytes_accessed=size, transcendentals=0),
    )(*far_ins, *near_ins)


def cut(whole, side):
    rows, columns = whole.shape
    half = columns // 2

    def kernel(whole_ref, half_ref, held, sem):
        for src, dst in (
            (whole_ref.at[:, side * half : (side + 1) * half], held),
            (held, half_ref),
        ):
            copy = pltpu.make_async_copy(src, dst, sem)
            copy.start()
            copy.wait()

    hbm = pl.BlockSpec(memory_space=pltpu.HBM)
    return pl.pallas_call(
        kernel,
        out_shape=jax.ShapeDtypeStruct((rows, half), whole.dtype),
        in_specs=[hbm],
        out_specs=hbm,
        scratch_shapes=[pltpu.VMEM((rows, half), whole.dtype), pltpu.SemaphoreType.DMA],
        compiler_params=pltpu.CompilerParams(vmem_limit_bytes=VMEM_BYTES),
        cost_estimate=pl.CostEstimate(flops=FLOPS_CUT, bytes_accessed=0, transcendentals=0),
    )(whole)


def halves(refs, rows):
    if len(refs) == 2:
        return [ref[rows] for ref in refs]
    half = refs[0].shape[1] // 2
    return [refs[0][rows, :half], refs[0][rows, half:]]


def split_parts(parts, items):
    out, at = [], 0
    for part in parts:
        out.append(items[at : at + part])
        at += part
    return out


def block_grads(width, units, rows_ref, weights, emits):
    half = width // 2
    gates, downs = slice(0, 2 * units), slice(2 * units, 3 * units)
    x = [rows_ref[:, :half], rows_ref[:, half:width]]
    dy = [rows_ref[:, width : width + half], rows_ref[:, width + half :]]
    pre = sum(dot(w, v, COLS) for w, v in zip(halves(weights, gates), x))
    d_act = sum(dot(w, v, COLS) for w, v in zip(halves(weights, downs), dy))
    pre_gate, pre_up = pre[:units], pre[units:]
    logistic = 1.0 / (1.0 + jnp.exp(-pre_gate))
    act = (pre_gate * logistic * pre_up).astype(jnp.bfloat16)
    d_s = jnp.sum(act.astype(jnp.float32) * d_act, axis=0, keepdims=True)
    d_gate = d_act * pre_up * logistic * (1.0 + pre_gate * (1.0 - logistic))
    d_up = d_act * pre_gate * logistic
    d_pre = jnp.concatenate([d_gate, d_up], axis=0)
    d_pre_low = d_pre.astype(jnp.bfloat16)
    for i, (send, grad) in enumerate(emits):
        grad[gates] = dot(d_pre_low, x[i], PLAIN).astype(grad.dtype)
        grad[downs] = dot(act, dy[i], PLAIN).astype(grad.dtype)
        send()
    return d_pre.T.astype(jnp.bfloat16), d_s


def blocks_body(width, units, parts, fetches, near_in, emits, near_out):
    (wait_rows, rows_ref), weights = fetches[0], split_parts(parts, fetches[1:])
    count = len(parts)
    wait_rows()
    total = sum(ref[:1] for ref in near_in)
    for b in range(count):
        for wait, _ in weights[b]:
            wait()
        refs = [ref for _, ref in weights[b]]
        out = emits[2 * b : 2 * b + 2]
        d_pre, d_s = block_grads(width, units, rows_ref, refs, out)
        near_out[b][...] = d_pre
        total = total + d_s
    near_out[count][...] = jnp.broadcast_to(total, near_out[count].shape)


def own_body(width, units, parts, fetches, near_in, emits, near_out):
    (wait_rows, rows_ref), weights = fetches[0], split_parts(parts, fetches[1:])
    count, half = len(parts), width // 2
    wait_rows()
    for wait, _ in weights[0]:
        wait()
    refs = [[ref for _, ref in pairs] for pairs in weights]
    d_pre, d_s = block_grads(width, units, rows_ref, refs[0], emits[:2])
    d_pre = [d_pre] + [ref[...] for ref in near_in[: count - 1]]
    d_s = d_s + near_in[count - 1][:1]
    for pairs in weights[1:]:
        for wait, _ in pairs:
            wait()
    send, out_ref = emits[2]
    gates = slice(0, 2 * units)
    for i in range(2):
        total = sum(dot(d_pre[b], halves(refs[b], gates)[i], PLAIN) for b in range(count))
        out_ref[:, i * half : (i + 1) * half] = total.astype(jnp.bfloat16)
    scores = jnp.broadcast_to(d_s, (LANES, d_s.shape[1])).T
    out_ref[:, width:] = scores.astype(jnp.bfloat16)
    send()


def add_body(fetches, near_in, emits, near_out):
    for i, (send, out) in enumerate(emits):
        (wait_a, a), (wait_b, b) = fetches[2 * i : 2 * i + 2]
        wait_a()
        wait_b()
        out[...] = (a[...].astype(jnp.float32) + b[...].astype(jnp.float32)).astype(out.dtype)
        send()


def added(*pairs, flops=0):
    outs = [jax.ShapeDtypeStruct(a.shape, a.dtype) for a, _ in pairs]
    return on_core(add_body, [v for pair in pairs for v in pair], [], outs, [], flops)


def total_body(units, fetches, near_in, emits, near_out):
    half = fetches[0][1].shape[1]
    for i in range(2):
        pair = fetches[2 * i : 2 * i + 2]
        for wait, _ in pair:
            wait()
        for j, (send, out) in enumerate(emits):
            rows = slice(j * units, (j + 1) * units)
            out[:, i * half : (i + 1) * half] = sum(
                ref[rows].astype(jnp.float32) for _, ref in pair
            ).astype(jnp.bfloat16)
            if i == 1:
                send()


def on_device(tokens, grad_out, expert_ids, scores, gate_weight, up_weight, down_weight):
    ring = lax.axis_size("block")
    expert_count = lax.axis_size("node") * lax.axis_size("expert")
    tok_count, width = tokens.shape
    units = gate_weight.shape[2]
    half = width // 2
    slot_count = expert_count * CAP
    bf16, f32 = jnp.bfloat16, jnp.float32
    shape = jax.ShapeDtypeStruct

    own = jnp.concatenate([gate_weight[0, 0], up_weight[0, 0], down_weight[0, 0]], axis=0)
    before = right(own, ring)
    after = left(own, ring)
    far_a = right(cut(before, 0), ring)
    far_b = left(cut(after, 1), ring)

    flat_ids = expert_ids.reshape(-1)
    expert_iota = jnp.arange(expert_count, dtype=jnp.int32)
    matches = (flat_ids[:, None] == expert_iota[None, :]).astype(jnp.int32)
    rank_within = jnp.sum((jnp.cumsum(matches, axis=0) - matches) * matches, axis=1)
    slot_index = flat_ids * CAP + rank_within
    placed = jnp.arange(slot_count, dtype=jnp.int32)[:, None] == slot_index[None, :]
    token_map = placed.reshape(slot_count, tok_count, TOP).sum(axis=2).astype(bf16)
    slot_s = jnp.sum(jnp.where(placed, scores.reshape(-1)[None, :].astype(f32), 0.0), axis=1)
    rows = dot(token_map, jnp.concatenate([tokens, grad_out], axis=1), PLAIN)
    by_slot = jnp.where(jnp.arange(2 * width)[None, :] < width, 1.0, slot_s[:, None])
    outgoing = (rows * by_slot).astype(bf16)
    rows = lax.all_to_all(
        outgoing.reshape(expert_count, CAP, 2 * width), ("node", "expert"), 0, 0, tiled=True
    ).reshape(slot_count, 2 * width)
    half_grad = shape((3 * units, half), bf16)
    near = [shape((slot_count, 2 * units), bf16), shape((SUBLANES, slot_count), f32)]

    def blocks(weights, so_far):
        count = len(weights)
        results = on_core(
            functools.partial(blocks_body, width, units, [len(w) for w in weights]),
            [rows, *[w for ws in weights for w in ws]],
            so_far,
            [half_grad] * (2 * count),
            [near[0]] * count + [near[1]],
            count * 12 * slot_count * units * width,
        )
        return results[: 2 * count], results[2 * count : 3 * count], results[3 * count :]

    (far_grad_a, far_grad_b), far_pre, far_s = blocks([(far_a, far_b)], [])
    passing_a = right(far_grad_a, ring)
    passing_b = left(far_grad_b, ring)
    (nxt_a, nxt_b, prev_a, prev_b), near_pre, near_s = blocks([(after,), (before,)], far_s)
    left_b = right(nxt_b, ring)
    right_a = left(prev_a, ring)
    left_a = right(added((nxt_a, passing_a))[0], ring)
    right_b = left(added((prev_b, passing_b))[0], ring)
    mine_a, mine_b, returning = on_core(
        functools.partial(own_body, width, units, [1, 2, 1, 1]),
        [rows, own, far_a, far_b, after, before],
        [*far_pre, *near_pre, *near_s],
        [half_grad, half_grad, shape((slot_count, width + LANES), bf16)],
        [],
        28 * slot_count * units * width,
    )
    part_a, part_b = added((mine_a, right_a), (mine_b, left_b), flops=FLOPS_PART)
    d_gate, d_up, d_down = on_core(
        functools.partial(total_body, units),
        [part_a, left_a, part_b, right_b],
        [],
        [shape((units, width), bf16)] * 3,
        [],
        0,
    )

    home = lax.all_to_all(
        returning.reshape(expert_count, CAP, width + LANES), ("node", "expert"), 0, 0, tiled=True
    ).reshape(slot_count, width + LANES)
    d_tokens = dot(token_map, home[:, :width], ROWS).astype(bf16)
    scaled_sums = jnp.sum(jnp.where(placed, home[:, width].astype(f32)[:, None], 0.0), axis=0)
    d_scores = (scaled_sums.reshape(tok_count, TOP) / scores.astype(f32)).astype(bf16)
    return (d_tokens, d_scores, d_gate[None, None], d_up[None, None], d_down[None, None])


def solution(mesh):
    node_count, local_count = mesh.devices.shape
    mesh = Mesh(
        mesh.devices.reshape(node_count, EXP_NODE, local_count // EXP_NODE),
        ("node", "expert", "block"),
    )
    by_token = P(("node", "expert", "block"), None)
    by_block = P("node", ("expert", "block"), None, None)
    return jax.shard_map(
        on_device,
        mesh=mesh,
        in_specs=(by_token,) * 4 + (by_block,) * 3,
        out_specs=(by_token,) * 2 + (by_block,) * 3,
        check_vma=False,
    )
```

time: 224 us -> 202 us (0.902)
  waiting for transfers between devices: 96.3 us -> 58 us
  Pallas kernels: 19.4 us -> 41.8 us
  starting transfers between devices: 68 us -> 75.3 us
  local copies, waits for them, and re-layouts: 24.6 us -> 17.5 us
  other arithmetic: 9.06 us -> 2.7 us
    ppermute x5, waiting for transfers between devices: 70.6 us -> 23.3 us  [left(): lax.ppermute(part, 'block', [(i, (i - 1) % ring) for i in range(ring)])]
    pallas_call x7 -> x9, Pallas kernels: 19.4 us -> 41.8 us  [the longest x7 37.2 us: on_core(): pl.pallas_call(kernel, out_shape=[*far_outs, *near_outs], in_specs=[hbm]...]
    all_to_all x1, waiting for transfers between devices: 0.01 us -> 21.3 us  [on_device(): lax.all_to_all(outgoing.reshape(expert_count, CAP, 2 * width), ('node', '...]
    ppermute x5, waiting for transfers between devices: 10.8 us -> 0.01 us  [right(): lax.ppermute(part, 'block', [(i, (i + 1) % ring) for i in range(ring)])]
    unnamed x41 -> x31, local copies, waits for them, and re-layouts: 12 us -> 5.8 us
    convert_element_type x2 -> x1, other arithmetic: 5.7 us -> 0.01 us  [on_device(): (scaled_sums.reshape(tok_count, TOP) / scores.astype(f32)).astype(bf16)]
    all_to_all x1, starting transfers between devices: 18.1 us -> 23.5 us  [on_device(): lax.all_to_all(returning.reshape(expert_count, CAP, width + LANES), ('nod...]
    reshape x2 -> x3, local copies, waits for them, and re-layouts: 5.01 us -> 8.7 us  [the longest x1 4.45 us: on_device(): outgoing.reshape(expert_count, CAP, 2 * width)]
  transfers between devices with their start and end apart: 12 -> 12, of which waited for: 6 -> 4; matrix products, arithmetic and copies ran while one was open for 10% -> 8% of each run, Pallas kernels for 5% -> 16%
where the time goes in v2:
time: 202 us; the launch traced here: 199 us
  starting transfers between devices  75.3 us (37%)
  waiting for transfers between devices  58 us (29%)
  Pallas kernels  41.8 us (21%)
  local copies, waits for them, and re-layouts  17.5 us (9%)
  matrix products  2.93 us (1%)
  other arithmetic  2.7 us (1%)
    pallas_call x7, Pallas kernels, on_core(): pl.pallas_call(kernel, out_shape=[*far_outs, *near_outs], in_specs=[hbm]...  37.2 us
    all_to_all x1, starting transfers between devices, on_device(): lax.all_to_all(returning.reshape(expert_count, CAP, width + LANES), ('nod...  23.5 us
    ppermute x5, waiting for transfers between devices, left(): lax.ppermute(part, 'block', [(i, (i - 1) % ring) for i in range(ring)])  23.3 us
    ppermute x5, starting transfers between devices, left(): lax.ppermute(part, 'block', [(i, (i - 1) % ring) for i in range(ring)])  23 us
    all_to_all x1, waiting for transfers between devices, on_device(): lax.all_to_all(outgoing.reshape(expert_count, CAP, 2 * width), ('node', '...  21.3 us
    all_to_all x1, starting transfers between devices, on_device(): lax.all_to_all(outgoing.reshape(expert_count, CAP, 2 * width), ('node', '...  18.3 us
    all_to_all x1, waiting for transfers between devices, on_device(): lax.all_to_all(returning.reshape(expert_count, CAP, width + LANES), ('nod...  13.4 us
    ppermute x5, starting transfers between devices, right(): lax.ppermute(part, 'block', [(i, (i + 1) % ring) for i in range(ring)])  10.4 us
  transfers between devices with their start and end apart: 12, of which 4 were waited for; matrix products, arithmetic and copies ran while one was open for 8% of the time, Pallas kernels for 16%

profile of v2, /device:TPU:1, one launch (start us, length us, event | category | flops | bytes accessed | tf_op | source)
XLA Modules:
  0.0 199.5 jit_solution(4121730611932077094)
XLA Ops:
  0.7 1.8 pad_maximum_fusion.refs_1_
  2.5 5.2 %collective-permute-start.2 = (bf16[576,2048]{1,0:T(8,128)(2,1)S(1)}, bf16[576,2048]{1,0:T(8,128)(2,1)}, u32[]{:S(2)}, u32[]{:S(2)}) collective-permute-start(bf16[576,2048]{1,0:T(8,128)(2,1)S(1)} %pad_maximum_fusion.refs_1_), channel_id=1, source_target_pairs={{0,3},{1,0},{2,1},{3,2},{4,7},{5,4},{6,5},{7,6},{8,11},{9,8},{10,9... | collective-permute-start | bytes 7077896 | tf_op jit(solution)/shard_map/ppermute | solution.py:34
  7.7 1.9 collective-permute-start
  9.7 0.1 copy.27
  9.7 0.1 reshape.65
  9.9 0.1 eq.36
  10.0 0.3 copy-done.6
  10.4 0.2 reduce_window_sum.11
  10.6 0.2 select_reduce_fusion.2
  10.9 0.5 copy-done.10
  11.4 0.1 select_reduce_fusion.1
  11.5 0.1 convert_reduce_fusion.1
  11.7 2.0 %fusion = bf16[256,4096]{1,0:T(8,128)(2,1)} fusion(f32[256]{0:T(256)S(1)} %select_reduce_fusion.1, pred[4096]{0:T(1024)(128)(4,1)S(1)} %iota_compare_fusion.3, bf16[16,2048]{1,0:T(8,128)(2,1)S(1)} %copy-done.12, bf16[16,2048]{1,0:T(8,128)(2,1)S(1)} %copy-done.13, s32[256,16]{0,1:T(8,128)S(1)} %convert_reduce_fusion.1), kind=kOutput, calls=%fused_computation.1 | convolution fusion | flops 36966400 | bytes 2249728 | tf_op jit(solution)/shard_map/dot_general | solution.py:26
  13.7 4.4 %reshape.60 = bf16[128,2,4096]{2,1,0:T(2,128)(2,1)} reshape(bf16[256,4096]{1,0:T(8,128)(2,1)} %fusion) | data formatting | bytes 4194304 | tf_op jit(solution)/shard_map/reshape | solution.py:241
  18.2 18.3 %all-to-all-start = ((bf16[128,2,4096]{2,1,0:T(2,128)(2,1)}), bf16[128,2,4096]{2,1,0:T(2,128)(2,1)}, u32[]{:S(2)}, u32[]{:S(2)}) async-start(bf16[128,2,4096]{2,1,0:T(2,128)(2,1)} %reshape.60), calls=%async_computation | async-start | bytes 4194304 | tf_op jit(solution)/shard_map/all_to_all | solution.py:240
  36.5 18.4 %collective-permute-done.2.whole_ref.refs_1_.refs_4_ = bf16[576,2048]{1,0:T(8,128)(2,1)} collective-permute-done((bf16[576,2048]{1,0:T(8,128)(2,1)S(1)}, bf16[576,2048]{1,0:T(8,128)(2,1)}, u32[]{:S(2)}, u32[]{:S(2)}) %collective-permute-start.2) | collective-permute-done | bytes 2359328 | tf_op jit(solution)/shard_map/ppermute | solution.py:34
  54.9 2.4 %shard_map.111 = bf16[576,1024]{1,0:T(8,128)(2,1)} custom-call(bf16[576,2048]{1,0:T(8,128)(2,1)} %collective-permute-done.2.whole_ref.refs_1_.refs_4_), custom_call_target="tpu_custom_call" | custom-call | flops 20000000000 | tf_op jit(solution)/shard_map/pallas_call | solution.py:97
  57.3 5.4 %collective-permute-start.3 = (bf16[576,1024]{1,0:T(8,128)(2,1)}, bf16[576,1024]{1,0:T(8,128)(2,1)S(1)}, u32[]{:S(2)}, u32[]{:S(2)}) collective-permute-start(bf16[576,1024]{1,0:T(8,128)(2,1)} %shard_map.111), channel_id=1, source_target_pairs={{0,3},{1,0},{2,1},{3,2},{4,7},{5,4},{6,5},{7,6},{8,11},{9,8},{10,9... | collective-permute-start | bytes 3538952 | tf_op jit(solution)/shard_map/ppermute | solution.py:34
  62.7 2.3 %shard_map.110 = bf16[576,1024]{1,0:T(8,128)(2,1)} custom-call(bf16[576,2048]{1,0:T(8,128)(2,1)} %collective-permute-done.whole_ref.refs_2_.refs_5_), custom_call_target="tpu_custom_call" | custom-call | flops 20000000000 | tf_op jit(solution)/shard_map/pallas_call | solution.py:97
  65.1 2.1 %collective-permute-start.1 = (bf16[576,1024]{1,0:T(8,128)(2,1)}, bf16[576,1024]{1,0:T(8,128)(2,1)S(1)}, u32[]{:S(2)}, u32[]{:S(2)}) collective-permute-start(bf16[576,1024]{1,0:T(8,128)(2,1)} %shard_map.110), channel_id=1, source_target_pairs={{0,1},{1,2},{2,3},{3,0},{4,5},{5,6},{6,7},{7,4},{8,9},{9,10},{10,1... | collective-permute-start | bytes 3538952 | tf_op jit(solution)/shard_map/ppermute | solution.py:30
  67.2 21.3 %all-to-all-done = bf16[128,2,4096]{2,1,0:T(2,128)(2,1)} async-done(((bf16[128,2,4096]{2,1,0:T(2,128)(2,1)}), bf16[128,2,4096]{2,1,0:T(2,128)(2,1)}, u32[]{:S(2)}, u32[]{:S(2)}) %all-to-all-start) | async-done | bytes 2097184 | tf_op jit(solution)/shard_map/all_to_all | solution.py:240
  88.5 4.2 %reshape.61.refs_0_ = bf16[256,4096]{1,0:T(8,128)(2,1)} reshape(bf16[128,2,4096]{2,1,0:T(2,128)(2,1)} %all-to-all-done) | data formatting | bytes 4194304 | tf_op jit(solution)/shard_map/reshape | solution.py:242
  92.6 1.0 copy-done.4
  93.7 1.0 copy-done.5
  94.7 6.0 %shard_map.112 = (bf16[576,1024]{1,0:T(8,128)(2,1)}, bf16[576,1024]{1,0:T(8,128)(2,1)}, bf16[256,384]{1,0:T(8,128)(2,1)}, f32[8,256]{1,0:T(8,128)}) custom-call(bf16[256,4096]{1,0:T(8,128)(2,1)} %reshape.61.refs_0_, bf16[576,1024]{1,0:T(8,128)(2,1)} %copy-done.5, bf16[576,1024]{1,0:T(8,128)(2,1)} %copy-done.4), custom_call_target="tpu_custom_call" | custom-call | flops 1207959552 | bytes 7020544 | tf_op jit(solution)/shard_map/pallas_call | solution.py:68
  100.7 2.4 %collective-permute-start.6 = (bf16[576,1024]{1,0:T(8,128)(2,1)}, bf16[576,1024]{1,0:T(8,128)(2,1)S(1)}, u32[]{:S(2)}, u32[]{:S(2)}) collective-permute-start(bf16[576,1024]{1,0:T(8,128)(2,1)} %get-tuple-element.36), channel_id=1, source_target_pairs={{0,1},{1,2},{2,3},{3,0},{4,5},{5,6},{6,7},{7,4},{8,9},{9,10},{10,1... | collective-permute-start | bytes 3538952 | tf_op jit(solution)/shard_map/ppermute | solution.py:30
  103.1 4.4 %collective-permute-start.8 = (bf16[576,1024]{1,0:T(8,128)(2,1)}, bf16[576,1024]{1,0:T(8,128)(2,1)S(1)}, u32[]{:S(2)}, u32[]{:S(2)}) collective-permute-start(bf16[576,1024]{1,0:T(8,128)(2,1)} %get-tuple-element.39), channel_id=1, source_target_pairs={{0,3},{1,0},{2,1},{3,2},{4,7},{5,4},{6,5},{7,6},{8,11},{9,8},{10,9... | collective-permute-start | bytes 3538952 | tf_op jit(solution)/shard_map/ppermute | solution.py:34
  107.5 8.8 %shard_map.113 = (bf16[576,1024]{1,0:T(8,128)(2,1)}, bf16[576,1024]{1,0:T(8,128)(2,1)}, bf16[576,1024]{1,0:T(8,128)(2,1)}, bf16[576,1024]{1,0:T(8,128)(2,1)}, bf...) custom-call(bf16[256,4096]{1,0:T(8,128)(2,1)} %reshape.61.refs_0_, ...), custom_call_target="tpu_custom_call" | custom-call | flops 2415919104 | bytes 11943936 | tf_op jit(solution)/shard_map/pallas_call | solution.py:68
  116.3 3.4 %collective-permute-start.4 = (bf16[576,1024]{1,0:T(8,128)(2,1)}, bf16[576,1024]{1,0:T(8,128)(2,1)}, u32[]{:S(2)}, u32[]{:S(2)}) collective-permute-start(bf16[576,1024]{1,0:T(8,128)(2,1)} %get-tuple-element.31), channel_id=1, source_target_pairs={{0,3},{1,0},{2,1},{3,2},{4,7},{5,4},{6,5},{7,6},{8,11},{9,8},{10,9... | collective-permute-start | bytes 3538952 | tf_op jit(solution)/shard_map/ppermute | solution.py:34
  119.6 2.1 %collective-permute-start.5 = (bf16[576,1024]{1,0:T(8,128)(2,1)}, bf16[576,1024]{1,0:T(8,128)(2,1)}, u32[]{:S(2)}, u32[]{:S(2)}) collective-permute-start(bf16[576,1024]{1,0:T(8,128)(2,1)} %get-tuple-element.33), channel_id=1, source_target_pairs={{0,1},{1,2},{2,3},{3,0},{4,5},{5,6},{6,7},{7,4},{8,9},{9,10},{10,1... | collective-permute-start | bytes 3538952 | tf_op jit(solution)/shard_map/ppermute | solution.py:30
  121.8 8.9 %shard_map.114 = (bf16[576,1024]{1,0:T(8,128)(2,1)}, bf16[576,1024]{1,0:T(8,128)(2,1)}, bf16[256,2176]{1,0:T(8,128)(2,1)}) custom-call(bf16[256,4096]{1,0:T(8,128)(2,1)} %reshape.61.refs_0_, bf16[576,2048]{1,0:T(8,128)(2,1)} %copy-done, bf16[576,1024]{1,0:T(8,128)(2,1)} %copy-done.5, bf16[576,1024]{1,0:T(8,128)(2,1)} %copy-done.4, ...), custom_call_target="tpu_custom_call" | custom-call | flops 2818572288 | bytes 15605760 | tf_op jit(solution)/shard_map/pallas_call | solution.py:68
  130.7 2.3 %reshape.62 = bf16[128,2,2176]{2,1,0:T(2,128)(2,1)} reshape(bf16[256,2176]{1,0:T(8,128)(2,1)} %get-tuple-element.29) | data formatting | bytes 2228224 | tf_op jit(solution)/shard_map/reshape | solution.py:285
  132.9 23.5 %all-to-all-start.1 = ((bf16[128,2,2176]{2,1,0:T(2,128)(2,1)}), bf16[128,2,2176]{2,1,0:T(2,128)(2,1)S(1)}, u32[]{:S(2)}, u32[]{:S(2)}) async-start(bf16[128,2,2176]{2,1,0:T(2,128)(2,1)} %reshape.62), calls=%async_computation.1 | async-start | bytes 2228224 | tf_op jit(solution)/shard_map/all_to_all | solution.py:284
  156.5 1.0 copy-done.2
  157.5 3.0 %shard_map.116 = bf16[576,1024]{1,0:T(8,128)(2,1)} custom-call(bf16[576,1024]{1,0:T(8,128)(2,1)} %get-tuple-element.35.refs_0_, bf16[576,1024]{1,0:T(8,128)(2,1)} %copy-done.2), custom_call_target="tpu_custom_call" | custom-call | bytes 3538944 | tf_op jit(solution)/shard_map/pallas_call | solution.py:68
  160.5 1.9 collective-permute-start.7
  162.5 1.0 copy-done.1
  163.5 3.0 %shard_map.117 = bf16[576,1024]{1,0:T(8,128)(2,1)} custom-call(bf16[576,1024]{1,0:T(8,128)(2,1)} %get-tuple-element.38.refs_0_, bf16[576,1024]{1,0:T(8,128)(2,1)} %copy-done.1), custom_call_target="tpu_custom_call" | custom-call | bytes 3538944 | tf_op jit(solution)/shard_map/pallas_call | solution.py:68
  166.4 4.6 %collective-permute-start.9 = (bf16[576,1024]{1,0:T(8,128)(2,1)}, bf16[576,1024]{1,0:T(8,128)(2,1)}, u32[]{:S(2)}, u32[]{:S(2)}) collective-permute-start(bf16[576,1024]{1,0:T(8,128)(2,1)} %shard_map.117), channel_id=1, source_target_pairs={{0,3},{1,0},{2,1},{3,2},{4,7},{5,4},{6,5},{7,6},{8,11},{9,8},{10,9... | collective-permute-start | bytes 3538952 | tf_op jit(solution)/shard_map/ppermute | solution.py:34
  171.0 3.7 %shard_map.115 = (bf16[576,1024]{1,0:T(8,128)(2,1)}, bf16[576,1024]{1,0:T(8,128)(2,1)}) custom-call(bf16[576,1024]{1,0:T(8,128)(2,1)} %get-tuple-element.30.refs_0_, bf16[576,1024]{1,0:T(8,128)(2,1)} %collective-permute-done.4.refs_1_, bf16[576,1024]{1,0:T(8,128)(2,1)} %get-tuple-element.32.refs_2_, bf16[576,1024]{1,0:T(8,128)(2,1)} %collective-permute-done.5.refs_3_), custom_call_target="tpu_custom_call" | custom-call | flops 30000001024 | bytes 7077888 | tf_op jit(solution)/shard_map/pallas_call | solution.py:68
  174.8 13.4 %all-to-all-done.1 = bf16[128,2,2176]{2,1,0:T(2,128)(2,1)S(1)} async-done(((bf16[128,2,2176]{2,1,0:T(2,128)(2,1)}), bf16[128,2,2176]{2,1,0:T(2,128)(2,1)S(1)}, u32[]{:S(2)}, u32[]{:S(2)}) %all-to-all-start.1) | async-done | bytes 1114144 | tf_op jit(solution)/shard_map/all_to_all | solution.py:284
  188.2 0.4 reshape.63
  188.7 0.1 convert_reduce_fusion
  188.8 0.1 select_reduce_fusion
  189.0 0.7 copy.28
  189.7 0.9 convolution_convert_fusion
  190.6 4.8 %collective-permute-done.9.refs_3_ = bf16[576,1024]{1,0:T(8,128)(2,1)} collective-permute-done((bf16[576,1024]{1,0:T(8,128)(2,1)}, bf16[576,1024]{1,0:T(8,128)(2,1)}, u32[]{:S(2)}, u32[]{:S(2)}) %collective-permute-start.9) | collective-permute-done | bytes 1179680 | tf_op jit(solution)/shard_map/ppermute | solution.py:34
  195.4 3.9 %shard_map.118 = (bf16[192,2048]{1,0:T(8,128)(2,1)}, bf16[192,2048]{1,0:T(8,128)(2,1)}, bf16[192,2048]{1,0:T(8,128)(2,1)}) custom-call(bf16[576,1024]{1,0:T(8,128)(2,1)} %get-tuple-element.34.refs_0_, bf16[576,1024]{1,0:T(8,128)(2,1)} %copy-done.3, bf16[576,1024]{1,0:T(8,128)(2,1)} %get-tuple-element.37.refs_2_, bf16[576,1024]{1,0:T(8,128)(2,1)} %collective-permute-done.9.refs_3_), custom_call_target="tpu_custom_call" | custom-call | bytes 7077888 | tf_op jit(solution)/shard_map/pallas_call | solution.py:68
  (38 shorter events, 0.4 us)
Async XLA Ops:
  0.6 9.0 %copy-start.9 = (bf16[16,8]{0,1:T(8,128)(2,1)S(1)}, bf16[16,8]{0,1:T(8,128)(2,1)}, u32[]{:S(2)}) copy-start(bf16[16,8]{0,1:T(8,128)(2,1)} %param.10) | copy-start | bytes 772
  0.6 9.2 %copy-start.8 = (s32[16,8]{0,1:T(8,128)S(1)}, s32[16,8]{0,1:T(8,128)}, u32[]{:S(2)}) copy-start(s32[16,8]{0,1:T(8,128)} %param.9) | copy-start | bytes 1540
  0.7 11.0 %copy-start.12 = (bf16[16,2048]{1,0:T(8,128)(2,1)S(1)}, bf16[16,2048]{1,0:T(8,128)(2,1)}, u32[]{:S(2)}) copy-start(bf16[16,2048]{1,0:T(8,128)(2,1)} %param.8) | copy-start | bytes 196612
  0.7 11.0 %copy-start.13 = (bf16[16,2048]{1,0:T(8,128)(2,1)S(1)}, bf16[16,2048]{1,0:T(8,128)(2,1)}, u32[]{:S(2)}) copy-start(bf16[16,2048]{1,0:T(8,128)(2,1)} %param.7) | copy-start | bytes 196612
  2.5 11.2 %copy-start = (bf16[576,2048]{1,0:T(8,128)(2,1)}, bf16[576,2048]{1,0:T(8,128)(2,1)S(1)}, u32[]{:S(2)}) copy-start(bf16[576,2048]{1,0:T(8,128)(2,1)S(1)} %pad_maximum_fusion.refs_1_) | copy-start | bytes 7077892
  2.5 52.4 %collective-permute-start.2 = (bf16[576,2048]{1,0:T(8,128)(2,1)S(1)}, bf16[576,2048]{1,0:T(8,128)(2,1)}, u32[]{:S(2)}, u32[]{:S(2)}) collective-permute-start(bf16[576,2048]{1,0:T(8,128)(2,1)S(1)} %pad_maximum_fusion.refs_1_), channel_id=1, source_target_pairs={{0,3},{1,0},{2,1},{3,2},{4,7},{5,4},{6,5},{7,6},{8,11},{9,8},{10,9... | collective-permute-start | bytes 7077896 | tf_op jit(solution)/shard_map/ppermute | solution.py:34
  7.7 55.0 %collective-permute-start = (bf16[576,2048]{1,0:T(8,128)(2,1)S(1)}, bf16[576,2048]{1,0:T(8,128)(2,1)}, u32[]{:S(2)}, u32[]{:S(2)}) collective-permute-start(bf16[576,2048]{1,0:T(8,128)(2,1)S(1)} %pad_maximum_fusion.refs_1_), channel_id=1, source_target_pairs={{0,1},{1,2},{2,3},{3,0},{4,5},{5,6},{6,7},{7,4},{8,9},{9,10},{10,1... | collective-permute-start | bytes 7077896 | tf_op jit(solution)/shard_map/ppermute | solution.py:30
  9.7 0.6 copy-start.6
  10.9 0.5 copy-start.10
  18.2 70.3 %all-to-all-start = ((bf16[128,2,4096]{2,1,0:T(2,128)(2,1)}), bf16[128,2,4096]{2,1,0:T(2,128)(2,1)}, u32[]{:S(2)}, u32[]{:S(2)}) async-start(bf16[128,2,4096]{2,1,0:T(2,128)(2,1)} %reshape.60), calls=%async_computation | async-start | bytes 4194304 | tf_op jit(solution)/shard_map/all_to_all | solution.py:240
  57.3 35.3 %collective-permute-start.3 = (bf16[576,1024]{1,0:T(8,128)(2,1)}, bf16[576,1024]{1,0:T(8,128)(2,1)S(1)}, u32[]{:S(2)}, u32[]{:S(2)}) collective-permute-start(bf16[576,1024]{1,0:T(8,128)(2,1)} %shard_map.111), channel_id=1, source_target_pairs={{0,3},{1,0},{2,1},{3,2},{4,7},{5,4},{6,5},{7,6},{8,11},{9,8},{10,9... | collective-permute-start | bytes 3538952 | tf_op jit(solution)/shard_map/ppermute | solution.py:34
  65.1 27.6 %collective-permute-start.1 = (bf16[576,1024]{1,0:T(8,128)(2,1)}, bf16[576,1024]{1,0:T(8,128)(2,1)S(1)}, u32[]{:S(2)}, u32[]{:S(2)}) collective-permute-start(bf16[576,1024]{1,0:T(8,128)(2,1)} %shard_map.110), channel_id=1, source_target_pairs={{0,1},{1,2},{2,3},{3,0},{4,5},{5,6},{6,7},{7,4},{8,9},{9,10},{10,1... | collective-permute-start | bytes 3538952 | tf_op jit(solution)/shard_map/ppermute | solution.py:30
  92.6 1.0 copy-start.4
  93.7 1.0 copy-start.5
  100.7 55.8 %collective-permute-start.6 = (bf16[576,1024]{1,0:T(8,128)(2,1)}, bf16[576,1024]{1,0:T(8,128)(2,1)S(1)}, u32[]{:S(2)}, u32[]{:S(2)}) collective-permute-start(bf16[576,1024]{1,0:T(8,128)(2,1)} %get-tuple-element.36), channel_id=1, source_target_pairs={{0,1},{1,2},{2,3},{3,0},{4,5},{5,6},{6,7},{7,4},{8,9},{9,10},{10,1... | collective-permute-start | bytes 3538952 | tf_op jit(solution)/shard_map/ppermute | solution.py:30
  103.1 59.3 %collective-permute-start.8 = (bf16[576,1024]{1,0:T(8,128)(2,1)}, bf16[576,1024]{1,0:T(8,128)(2,1)S(1)}, u32[]{:S(2)}, u32[]{:S(2)}) collective-permute-start(bf16[576,1024]{1,0:T(8,128)(2,1)} %get-tuple-element.39), channel_id=1, source_target_pairs={{0,3},{1,0},{2,1},{3,2},{4,7},{5,4},{6,5},{7,6},{8,11},{9,8},{10,9... | collective-permute-start | bytes 3538952 | tf_op jit(solution)/shard_map/ppermute | solution.py:34
  116.3 54.8 %collective-permute-start.4 = (bf16[576,1024]{1,0:T(8,128)(2,1)}, bf16[576,1024]{1,0:T(8,128)(2,1)}, u32[]{:S(2)}, u32[]{:S(2)}) collective-permute-start(bf16[576,1024]{1,0:T(8,128)(2,1)} %get-tuple-element.31), channel_id=1, source_target_pairs={{0,3},{1,0},{2,1},{3,2},{4,7},{5,4},{6,5},{7,6},{8,11},{9,8},{10,9... | collective-permute-start | bytes 3538952 | tf_op jit(solution)/shard_map/ppermute | solution.py:34
  119.6 51.4 %collective-permute-start.5 = (bf16[576,1024]{1,0:T(8,128)(2,1)}, bf16[576,1024]{1,0:T(8,128)(2,1)}, u32[]{:S(2)}, u32[]{:S(2)}) collective-permute-start(bf16[576,1024]{1,0:T(8,128)(2,1)} %get-tuple-element.33), channel_id=1, source_target_pairs={{0,1},{1,2},{2,3},{3,0},{4,5},{5,6},{6,7},{7,4},{8,9},{9,10},{10,1... | collective-permute-start | bytes 3538952 | tf_op jit(solution)/shard_map/ppermute | solution.py:30
  132.9 55.3 %all-to-all-start.1 = ((bf16[128,2,2176]{2,1,0:T(2,128)(2,1)}), bf16[128,2,2176]{2,1,0:T(2,128)(2,1)S(1)}, u32[]{:S(2)}, u32[]{:S(2)}) async-start(bf16[128,2,2176]{2,1,0:T(2,128)(2,1)} %reshape.62), calls=%async_computation.1 | async-start | bytes 2228224 | tf_op jit(solution)/shard_map/all_to_all | solution.py:284
  156.5 1.0 copy-start.2
  160.5 30.0 %collective-permute-start.7 = (bf16[576,1024]{1,0:T(8,128)(2,1)}, bf16[576,1024]{1,0:T(8,128)(2,1)S(1)}, u32[]{:S(2)}, u32[]{:S(2)}) collective-permute-start(bf16[576,1024]{1,0:T(8,128)(2,1)} %shard_map.116), channel_id=1, source_target_pairs={{0,1},{1,2},{2,3},{3,0},{4,5},{5,6},{6,7},{7,4},{8,9},{9,10},{10,1... | collective-permute-start | bytes 3538952 | tf_op jit(solution)/shard_map/ppermute | solution.py:30
  162.4 1.0 copy-start.1
  166.4 29.0 %collective-permute-start.9 = (bf16[576,1024]{1,0:T(8,128)(2,1)}, bf16[576,1024]{1,0:T(8,128)(2,1)}, u32[]{:S(2)}, u32[]{:S(2)}) collective-permute-start(bf16[576,1024]{1,0:T(8,128)(2,1)} %shard_map.117), channel_id=1, source_target_pairs={{0,3},{1,0},{2,1},{3,2},{4,7},{5,4},{6,5},{7,6},{8,11},{9,8},{10,9... | collective-permute-start | bytes 3538952 | tf_op jit(solution)/shard_map/ppermute | solution.py:34
  174.8 14.0 %copy-start.11 = (s32[128]{0:T(128)S(1)}, s32[128]{0:T(128)}, u32[]{:S(2)}) copy-start(s32[128]{0:T(128)} %copy-done.10) | copy-start | bytes 1540
  174.8 14.2 %copy-start.7 = (bf16[16,8]{1,0:T(8,128)(2,1)S(1)}, bf16[16,8]{1,0:T(8,128)(2,1)}, u32[]{:S(2)}) copy-start(bf16[16,8]{1,0:T(8,128)(2,1)} %copy-done.6) | copy-start | bytes 772
  190.6 4.9 %copy-start.3 = (bf16[576,1024]{1,0:T(8,128)(2,1)}, bf16[576,1024]{1,0:T(8,128)(2,1)S(1)}, u32[]{:S(2)}) copy-start(bf16[576,1024]{1,0:T(8,128)(2,1)S(1)} %collective-permute-done.7.refs_1_) | copy-start | bytes 3538948

commit v3 on v2

--- a/solution.py
+++ b/solution.py
@@ -13,7 +13,8 @@
 CAP = 2
 LANES = 128
 SUBLANES = 8
-VMEM_BYTES = 56 << 20
+PIECES = 4
+VMEM_BYTES = 58 << 20
 FLOPS_CUT = 2 * 10**10
 FLOPS_PART = 3 * 10**10
 
@@ -32,6 +33,20 @@
 
 def left(part, ring):
     return lax.ppermute(part, "block", [(i, (i - 1) % ring) for i in range(ring)])
+
+
+def pieces(src, dst, sems):
+    rows = src.shape[0] // PIECES
+    spans = [pl.ds(i * rows, rows) for i in range(PIECES)]
+    return [
+        pltpu.make_async_copy(src.at[span], dst.at[span], sems.at[i])
+        for i, span in enumerate(spans)
+    ]
+
+
+def each(copies, what):
+    for copy in copies:
+        getattr(copy, what)()
 
 
 def on_core(body, far_ins, near_ins, far_outs, near_outs, flops):
@@ -45,24 +60,20 @@
             groups.append(refs[at : at + count])
             at += count
         source, near_in, target, near_out, held_in, held_out, (in_sem,), (out_sem,) = groups
-        incoming = [
-            pltpu.make_async_copy(src, held, in_sem.at[i])
-            for i, (src, held) in enumerate(zip(source, held_in))
+        incoming = [pieces(src, held, in_sem.at[i]) for i, (src, held) in enumerate(zip(source, held_in))]
+        outgoing = [
+            pieces(held, dst, out_sem.at[i]) for i, (held, dst) in enumerate(zip(held_out, target))
         ]
-        outgoing = [
-            pltpu.make_async_copy(held, dst, out_sem.at[i])
-            for i, (held, dst) in enumerate(zip(held_out, target))
-        ]
-        for copy in incoming:
-            copy.start()
+        for copies in incoming:
+            each(copies, "start")
         body(
-            [(copy.wait, held) for copy, held in zip(incoming, held_in)],
+            [(functools.partial(each, c, "wait"), held) for c, held in zip(incoming, held_in)],
             near_in,
-            [(copy.start, held) for copy, held in zip(outgoing, held_out)],
+            [(functools.partial(each, c, "start"), held) for c, held in zip(outgoing, held_out)],
             near_out,
         )
-        for copy in outgoing:
-            copy.wait()
+        for copies in outgoing:
+            each(copies, "wait")
 
     hbm, vmem = pl.BlockSpec(memory_space=pltpu.HBM), pl.BlockSpec(memory_space=pltpu.VMEM)
     return pl.pallas_call(
@@ -72,37 +83,25 @@
         out_specs=[hbm] * n_out + [vmem] * len(near_outs),
         scratch_shapes=[
             *[pltpu.VMEM(v.shape, v.dtype) for v in (*far_ins, *far_outs)],
-            pltpu.SemaphoreType.DMA((n_in,)),
-            pltpu.SemaphoreType.DMA((n_out,)),
+            pltpu.SemaphoreType.DMA((n_in, PIECES)),
+            pltpu.SemaphoreType.DMA((n_out, PIECES)),
         ],
         compiler_params=pltpu.CompilerParams(vmem_limit_bytes=VMEM_BYTES),
         cost_estimate=pl.CostEstimate(flops=int(flops), bytes_accessed=size, transcendentals=0),
     )(*far_ins, *near_ins)
 
 
-def cut(whole, side):
-    rows, columns = whole.shape
-    half = columns // 2
-
-    def kernel(whole_ref, half_ref, held, sem):
-        for src, dst in (
-            (whole_ref.at[:, side * half : (side + 1) * half], held),
-            (held, half_ref),
-        ):
-            copy = pltpu.make_async_copy(src, dst, sem)
-            copy.start()
-            copy.wait()
-
+def hold(part):
     hbm = pl.BlockSpec(memory_space=pltpu.HBM)
     return pl.pallas_call(
-        kernel,
-        out_shape=jax.ShapeDtypeStruct((rows, half), whole.dtype),
+        lambda part_ref, same_ref: None,
+        out_shape=jax.ShapeDtypeStruct(part.shape, part.dtype),
         in_specs=[hbm],
         out_specs=hbm,
-        scratch_shapes=[pltpu.VMEM((rows, half), whole.dtype), pltpu.SemaphoreType.DMA],
-        compiler_params=pltpu.CompilerParams(vmem_limit_bytes=VMEM_BYTES),
+        input_output_aliases={0: 0},
+        compiler_params=pltpu.CompilerParams(vmem_limit_bytes=1 << 20),
         cost_estimate=pl.CostEstimate(flops=FLOPS_CUT, bytes_accessed=0, transcendentals=0),
-    )(whole)
+    )(part)
 
 
 def halves(refs, rows):
@@ -146,6 +145,11 @@
     (wait_rows, rows_ref), weights = fetches[0], split_parts(parts, fetches[1:])
     count = len(parts)
     wait_rows()
+    if len(rows_ref.shape) == 3:
+        send_rows, flat_ref = emits[2 * count]
+        flat_ref[...] = rows_ref[...].reshape(flat_ref.shape)
+        send_rows()
+        rows_ref = flat_ref
     total = sum(ref[:1] for ref in near_in)
     for b in range(count):
         for wait, _ in weights[b]:
@@ -175,9 +179,10 @@
     gates = slice(0, 2 * units)
     for i in range(2):
         total = sum(dot(d_pre[b], halves(refs[b], gates)[i], PLAIN) for b in range(count))
-        out_ref[:, i * half : (i + 1) * half] = total.astype(jnp.bfloat16)
-    scores = jnp.broadcast_to(d_s, (LANES, d_s.shape[1])).T
-    out_ref[:, width:] = scores.astype(jnp.bfloat16)
+        total = total.astype(jnp.bfloat16).reshape((*out_ref.shape[:2], half))
+        out_ref[:, :, i * half : (i + 1) * half] = total
+    scores = jnp.broadcast_to(d_s, (LANES, d_s.shape[1])).T.astype(jnp.bfloat16)
+    out_ref[:, :, width:] = scores.reshape((*out_ref.shape[:2], LANES))
     send()
 
 
@@ -210,6 +215,61 @@
                 send()
 
 
+def matched(ids, expert_slots, k):
+    return ids[k : k + 1] == expert_slots
+
+
+def dispatch_body(ids_ref, scores_ref, tokens_ref, grad_ref, rows_ref, map_ref):
+    slot_count, width = map_ref.shape[0], tokens_ref.shape[1]
+    tok_count = tokens_ref.shape[0]
+    shape = (slot_count, tok_count)
+    slots = lax.broadcasted_iota(jnp.int32, shape, 0)
+    ids, scores = ids_ref[...], scores_ref[...].astype(jnp.float32)
+    named, weight = jnp.zeros(shape, jnp.float32), jnp.zeros(shape, jnp.float32)
+    for k in range(TOP):
+        hit = matched(ids, slots // CAP, k)
+        named = jnp.where(hit, 1.0, named)
+        weight = jnp.where(hit, scores[k : k + 1], weight)
+    square = (tok_count, tok_count)
+    earlier = lax.broadcasted_iota(jnp.int32, square, 0) < lax.broadcasted_iota(jnp.int32, square, 1)
+    rank = dot(named.astype(jnp.bfloat16), earlier.astype(jnp.bfloat16), PLAIN)
+    placed = jnp.where(rank == (slots % CAP).astype(jnp.float32), named, 0.0)
+    slot_s = jnp.sum(placed * weight, axis=1, keepdims=True)
+    token_map = placed.astype(jnp.bfloat16)
+    map_ref[...] = token_map
+    x = dot(token_map, tokens_ref[...], PLAIN).astype(jnp.bfloat16)
+    rows_ref[:, :, :width] = x.reshape(slot_count // CAP, CAP, width)
+    scaled = slot_s * dot(token_map, grad_ref[...], PLAIN)
+    rows_ref[:, :, width:] = scaled.astype(jnp.bfloat16).reshape(slot_count // CAP, CAP, width)
+
+
+def home_body(home_ref, ids_ref, scores_ref, map_ref, tokens_ref, out_scores_ref):
+    width = tokens_ref.shape[1]
+    token_map = map_ref[...]
+    home = home_ref[...].reshape(token_map.shape[0], width + LANES)
+    tokens_ref[...] = dot(token_map, home[:, :width], ROWS).astype(jnp.bfloat16)
+    slots = lax.broadcasted_iota(jnp.int32, token_map.shape, 0)
+    ids, scores = ids_ref[...], scores_ref[...].astype(jnp.float32)
+    sums = token_map.astype(jnp.float32) * home[:, width : width + 1].astype(jnp.float32)
+    for k in range(TOP):
+        own = jnp.where(matched(ids, slots // CAP, k), sums, 0.0)
+        total = jnp.sum(own, axis=0, keepdims=True) / scores[k : k + 1]
+        out_scores_ref[k : k + 1] = total
+
+
+def simple_call(body, outs, *operands):
+    vmem = pl.BlockSpec(memory_space=pltpu.VMEM)
+    size = sum(v.size * v.dtype.itemsize for v in (*operands, *outs))
+    return pl.pallas_call(
+        body,
+        out_shape=outs,
+        in_specs=[vmem] * len(operands),
+        out_specs=[vmem] * len(outs),
+        compiler_params=pltpu.CompilerParams(vmem_limit_bytes=16 << 20),
+        cost_estimate=pl.CostEstimate(flops=0, bytes_accessed=size, transcendentals=0),
+    )(*operands)
+
+
 def on_device(tokens, grad_out, expert_ids, scores, gate_weight, up_weight, down_weight):
     ring = lax.axis_size("block")
     expert_count = lax.axis_size("node") * lax.axis_size("expert")
@@ -220,54 +280,59 @@
     bf16, f32 = jnp.bfloat16, jnp.float32
     shape = jax.ShapeDtypeStruct
 
-    own = jnp.concatenate([gate_weight[0, 0], up_weight[0, 0], down_weight[0, 0]], axis=0)
-    before = right(own, ring)
-    after = left(own, ring)
-    far_a = right(cut(before, 0), ring)
-    far_b = left(cut(after, 1), ring)
-
-    flat_ids = expert_ids.reshape(-1)
-    expert_iota = jnp.arange(expert_count, dtype=jnp.int32)
-    matches = (flat_ids[:, None] == expert_iota[None, :]).astype(jnp.int32)
-    rank_within = jnp.sum((jnp.cumsum(matches, axis=0) - matches) * matches, axis=1)
-    slot_index = flat_ids * CAP + rank_within
-    placed = jnp.arange(slot_count, dtype=jnp.int32)[:, None] == slot_index[None, :]
-    token_map = placed.reshape(slot_count, tok_count, TOP).sum(axis=2).astype(bf16)
-    slot_s = jnp.sum(jnp.where(placed, scores.reshape(-1)[None, :].astype(f32), 0.0), axis=1)
-    rows = dot(token_map, jnp.concatenate([tokens, grad_out], axis=1), PLAIN)
-    by_slot = jnp.where(jnp.arange(2 * width)[None, :] < width, 1.0, slot_s[:, None])
-    outgoing = (rows * by_slot).astype(bf16)
+    matrices = [gate_weight[0, 0], up_weight[0, 0], down_weight[0, 0]]
+    own_a = jnp.concatenate([w[:, :half] for w in matrices], axis=0)
+    own_b = jnp.concatenate([w[:, half:] for w in matrices], axis=0)
+    before_a, after_b = hold(right(own_a, ring)), hold(left(own_b, ring))
+    before = (before_a, right(own_b, ring))
+    after = (left(own_a, ring), after_b)
+    far_a, far_b = right(before_a, ring), left(after_b, ring)
+
+    ids_t, scores_t = expert_ids.T, scores.T
+    outgoing, token_map = simple_call(
+        dispatch_body,
+        [shape((expert_count, CAP, 2 * width), bf16), shape((slot_count, tok_count), bf16)],
+        ids_t,
+        scores_t,
+        tokens,
+        grad_out,
+    )
     rows = lax.all_to_all(
-        outgoing.reshape(expert_count, CAP, 2 * width), ("node", "expert"), 0, 0, tiled=True
-    ).reshape(slot_count, 2 * width)
+        outgoing, ("node", "expert"), 0, 0, tiled=True
+    )
     half_grad = shape((3 * units, half), bf16)
     near = [shape((slot_count, 2 * units), bf16), shape((SUBLANES, slot_count), f32)]
 
-    def blocks(weights, so_far):
+    def blocks(weights, so_far, rows, extra=()):
         count = len(weights)
         results = on_core(
             functools.partial(blocks_body, width, units, [len(w) for w in weights]),
             [rows, *[w for ws in weights for w in ws]],
             so_far,
-            [half_grad] * (2 * count),
+            [half_grad] * (2 * count) + list(extra),
             [near[0]] * count + [near[1]],
             count * 12 * slot_count * units * width,
         )
-        return results[: 2 * count], results[2 * count : 3 * count], results[3 * count :]
-
-    (far_grad_a, far_grad_b), far_pre, far_s = blocks([(far_a, far_b)], [])
+        sent = 2 * count + len(extra)
+        return results[:sent], results[sent : sent + count], results[sent + count :]
+
+    (far_grad_a, far_grad_b, flat_rows), far_pre, far_s = blocks(
+        [(far_a, far_b)], [], rows, [shape((slot_count, 2 * width), bf16)]
+    )
     passing_a = right(far_grad_a, ring)
     passing_b = left(far_grad_b, ring)
-    (nxt_a, nxt_b, prev_a, prev_b), near_pre, near_s = blocks([(after,), (before,)], far_s)
+    (nxt_a, nxt_b, prev_a, prev_b), near_pre, near_s = blocks(
+        [after, before], far_s, flat_rows
+    )
     left_b = right(nxt_b, ring)
     right_a = left(prev_a, ring)
     left_a = right(added((nxt_a, passing_a))[0], ring)
     right_b = left(added((prev_b, passing_b))[0], ring)
     mine_a, mine_b, returning = on_core(
-        functools.partial(own_body, width, units, [1, 2, 1, 1]),
-        [rows, own, far_a, far_b, after, before],
+        functools.partial(own_body, width, units, [2, 2, 2, 2]),
+        [flat_rows, own_a, own_b, far_a, far_b, *after, *before],
         [*far_pre, *near_pre, *near_s],
-        [half_grad, half_grad, shape((slot_count, width + LANES), bf16)],
+        [half_grad, half_grad, shape((expert_count, CAP, width + LANES), bf16)],
         [],
         28 * slot_count * units * width,
     )
@@ -282,11 +347,17 @@
     )
 
     home = lax.all_to_all(
-        returning.reshape(expert_count, CAP, width + LANES), ("node", "expert"), 0, 0, tiled=True
-    ).reshape(slot_count, width + LANES)
-    d_tokens = dot(token_map, home[:, :width], ROWS).astype(bf16)
-    scaled_sums = jnp.sum(jnp.where(placed, home[:, width].astype(f32)[:, None], 0.0), axis=0)
-    d_scores = (scaled_sums.reshape(tok_count, TOP) / scores.astype(f32)).astype(bf16)
+        returning, ("node", "expert"), 0, 0, tiled=True
+    )
+    d_tokens, d_scores_t = simple_call(
+        home_body,
+        [shape((tok_count, width), bf16), shape((TOP, tok_count), f32)],
+        home,
+        ids_t,
+        scores_t,
+        token_map,
+    )
+    d_scores = d_scores_t.T.astype(bf16)
     return (d_tokens, d_scores, d_gate[None, None], d_up[None, None], d_down[None, None])
 
 

time: 202 us -> 184 us (0.911)
  local copies, waits for them, and re-layouts: 17.5 us -> 4.83 us
  matrix products: 2.93 us -> 0 us
    ppermute x5 -> x6, waiting for transfers between devices: 0.01 us -> 16.4 us  [right(): lax.ppermute(part, 'block', [(i, (i + 1) % ring) for i in range(ring)])]
    ppermute x5 -> x6, waiting for transfers between devices: 23.3 us -> 7.53 us  [left(): lax.ppermute(part, 'block', [(i, (i - 1) % ring) for i in range(ring)])]
    reshape x5 -> x0, local copies, waits for them, and re-layouts: 11.4 us -> none  [the longest x1 4.45 us: on_device(): outgoing.reshape(expert_count, CAP, 2 * width)]
    all_to_all x2, starting transfers between devices: 41.9 us -> 36.1 us  [the longest x1 18.8 us: on_device(): rows = lax.all_to_all(outgoing, ('node', 'expert'), 0, 0, tiled=True)]
    ppermute x5 -> x6, starting transfers between devices: 10.4 us -> 15.7 us  [right(): lax.ppermute(part, 'block', [(i, (i + 1) % ring) for i in range(ring)])]
    dot_general x2 -> x0, matrix products: 2.93 us -> none  [dot(): return lax.dot_general(a, b, dims, preferred_element_type=jnp.float32)]
    unnamed x31 -> x22, local copies, waits for them, and re-layouts: 5.8 us -> 3.42 us
    pallas_call x2 -> x4, Pallas kernels: 4.68 us -> 3.33 us  [the longest x2 3.33 us: simple_call(): pl.pallas_call(body, out_shape=outs, in_specs=[vmem] * len(operands), out...]
  transfers between devices with their start and end apart: 12 -> 14, of which waited for: 4 -> 6; matrix products, arithmetic and copies ran while one was open for 8% -> 1% of each run, Pallas kernels for 16% -> 21%
where the time goes in v3:
time: 184 us; the launch traced here: 182 us
  starting transfers between devices  73.8 us (40%)
  waiting for transfers between devices  58.2 us (32%)
  Pallas kernels  41.5 us (23%)
  local copies, waits for them, and re-layouts  4.83 us (3%)
  other arithmetic  2.81 us (2%)
    pallas_call x7, Pallas kernels, on_core(): pl.pallas_call(kernel, out_shape=[*far_outs, *near_outs], in_specs=[hbm]...  38.1 us
    ppermute x6, starting transfers between devices, left(): lax.ppermute(part, 'block', [(i, (i - 1) % ring) for i in range(ring)])  22 us
    all_to_all x1, waiting for transfers between devices, on_device(): rows = lax.all_to_all(outgoing, ('node', 'expert'), 0, 0, tiled=True)  20.4 us
    all_to_all x1, starting transfers between devices, on_device(): rows = lax.all_to_all(outgoing, ('node', 'expert'), 0, 0, tiled=True)  18.8 us
    all_to_all x1, starting transfers between devices, on_device(): home = lax.all_to_all(returning, ('node', 'expert'), 0, 0, tiled=True)  17.3 us
    ppermute x6, waiting for transfers between devices, right(): lax.ppermute(part, 'block', [(i, (i + 1) % ring) for i in range(ring)])  16.4 us
    ppermute x6, starting transfers between devices, right(): lax.ppermute(part, 'block', [(i, (i + 1) % ring) for i in range(ring)])  15.7 us
    all_to_all x1, waiting for transfers between devices, on_device(): home = lax.all_to_all(returning, ('node', 'expert'), 0, 0, tiled=True)  14 us
  transfers between devices with their start and end apart: 14, of which 6 were waited for; matrix products, arithmetic and copies ran while one was open for 1% of the time, Pallas kernels for 21%

profile of v3, /device:TPU:1, one launch (start us, length us, event | category | flops | bytes accessed | tf_op | source)
XLA Modules:
  0.0 182.3 jit_solution(7770069632966206172)
XLA Ops:
  0.7 1.3 fusion.2
  1.9 0.1 copy-done.10
  2.0 0.2 copy-done.9
  2.2 0.1 fusion
  2.4 1.1 pad_maximum_fusion.refs_1_
  3.5 3.9 %collective-permute-start = (bf16[576,1024]{1,0:T(8,128)(2,1)}, bf16[576,1024]{1,0:T(8,128)(2,1)S(1)}, u32[]{:S(2)}, u32[]{:S(2)}) collective-permute-start(bf16[576,1024]{1,0:T(8,128)(2,1)} %pad_maximum_fusion.refs_1_), channel_id=1, source_target_pairs={{0,1},{1,2},{2,3},{3,0},{4,5},{5,6},{6,7},{7,4},{8,9},{9,10},{10,1... | collective-permute-start | bytes 3538952 | tf_op jit(solution)/shard_map/ppermute | solution.py:31
  7.4 0.0 copy-start.2
  7.4 0.0 copy-start.3
  7.4 0.0 copy-start.4
  7.4 0.0 copy-start.5
  7.5 1.1 pad_maximum_fusion.1.refs_2_
  8.6 3.2 %collective-permute-start.2 = (bf16[576,1024]{1,0:T(8,128)(2,1)}, bf16[576,1024]{1,0:T(8,128)(2,1)S(1)}, u32[]{:S(2)}, u32[]{:S(2)}) collective-permute-start(bf16[576,1024]{1,0:T(8,128)(2,1)} %pad_maximum_fusion.1.refs_2_), channel_id=1, source_target_pairs={{0,3},{1,0},{2,1},{3,2},{4,7},{5,4},{6,5},{7,6},{8,11},{9,8},{10,9... | collective-permute-start | bytes 3538952 | tf_op jit(solution)/shard_map/ppermute | solution.py:35
  11.8 2.3 %shard_map.110 = (bf16[128,2,4096]{2,1,0:T(2,128)(2,1)}, bf16[256,16]{1,0:T(8,128)(2,1)S(1)}) custom-call(s32[8,16]{1,0:T(8,128)S(1)} %bitcast.10, bf16[8,16]{1,0:T(8,128)(2,1)S(1)} %bitcast.12, bf16[16,2048]{1,0:T(8,128)(2,1)S(1)} %copy-done.2, bf16[16,2048]{1,0:T(8,128)(2,1)S(1)} %copy-done.3), custom_call_target="tpu_custom_call" | custom-call | bytes 2237184 | tf_op jit(solution)/shard_map/pallas_call | solution.py:263
  14.1 18.8 %all-to-all-start = ((bf16[128,2,4096]{2,1,0:T(2,128)(2,1)}), bf16[128,2,4096]{2,1,0:T(2,128)(2,1)}, u32[]{:S(2)}, u32[]{:S(2)}) async-start(bf16[128,2,4096]{2,1,0:T(2,128)(2,1)} %get-tuple-element.29), calls=%async_computation | async-start | bytes 4194304 | tf_op jit(solution)/shard_map/all_to_all | solution.py:300
  32.9 2.5 %collective-permute-start.1 = (bf16[576,1024]{1,0:T(8,128)(2,1)S(1)}, bf16[576,1024]{1,0:T(8,128)(2,1)S(1)}, u32[]{:S(2)}, u32[]{:S(2)}) collective-permute-start(bf16[576,1024]{1,0:T(8,128)(2,1)S(1)} %shard_map.111.refs_3_.refs_7_), channel_id=1, source_target_pairs={{0,1},{1,2},{2,3},{3,0},{4,5},{5,6},{6,7},{7,4},{8,9},{9,10},{10,1... | collective-permute-start | bytes 3538952 | tf_op jit(solution)/shard_map/ppermute | solution.py:31
  35.5 0.0 collective-permute-done.2.part_ref
  35.5 4.1 %collective-permute-start.3 = (bf16[576,1024]{1,0:T(8,128)(2,1)S(1)}, bf16[576,1024]{1,0:T(8,128)(2,1)}, u32[]{:S(2)}, u32[]{:S(2)}) collective-permute-start(bf16[576,1024]{1,0:T(8,128)(2,1)S(1)} %shard_map.112.refs_2_.refs_6_), channel_id=1, source_target_pairs={{0,3},{1,0},{2,1},{3,2},{4,7},{5,4},{6,5},{7,6},{8,11},{9,8},{10,9... | collective-permute-start | bytes 3538952 | tf_op jit(solution)/shard_map/ppermute | solution.py:35
  39.6 3.4 %collective-permute-start.4 = (bf16[576,1024]{1,0:T(8,128)(2,1)}, bf16[576,1024]{1,0:T(8,128)(2,1)}, u32[]{:S(2)}, u32[]{:S(2)}) collective-permute-start(bf16[576,1024]{1,0:T(8,128)(2,1)} %pad_maximum_fusion.refs_1_), channel_id=1, source_target_pairs={{0,3},{1,0},{2,1},{3,2},{4,7},{5,4},{6,5},{7,6},{8,11},{9,8},{10,9... | collective-permute-start | bytes 3538952 | tf_op jit(solution)/shard_map/ppermute | solution.py:35
  42.9 1.9 %collective-permute-start.5 = (bf16[576,1024]{1,0:T(8,128)(2,1)}, bf16[576,1024]{1,0:T(8,128)(2,1)}, u32[]{:S(2)}, u32[]{:S(2)}) collective-permute-start(bf16[576,1024]{1,0:T(8,128)(2,1)} %pad_maximum_fusion.1.refs_2_), channel_id=1, source_target_pairs={{0,1},{1,2},{2,3},{3,0},{4,5},{5,6},{6,7},{7,4},{8,9},{9,10},{10,1... | collective-permute-start | bytes 3538952 | tf_op jit(solution)/shard_map/ppermute | solution.py:31
  44.9 16.1 %collective-permute-done.1.refs_1_.refs_3_ = bf16[576,1024]{1,0:T(8,128)(2,1)S(1)} collective-permute-done((bf16[576,1024]{1,0:T(8,128)(2,1)S(1)}, bf16[576,1024]{1,0:T(8,128)(2,1)S(1)}, u32[]{:S(2)}, u32[]{:S(2)}) %collective-permute-start.1) | collective-permute-done | bytes 1179680 | tf_op jit(solution)/shard_map/ppermute | solution.py:31
  60.9 1.0 copy-done.7
  61.9 2.6 %collective-permute-done.3.refs_2_.refs_4_ = bf16[576,1024]{1,0:T(8,128)(2,1)} collective-permute-done((bf16[576,1024]{1,0:T(8,128)(2,1)S(1)}, bf16[576,1024]{1,0:T(8,128)(2,1)}, u32[]{:S(2)}, u32[]{:S(2)}) %collective-permute-start.3) | collective-permute-done | bytes 1179680 | tf_op jit(solution)/shard_map/ppermute | solution.py:35
  64.5 20.4 %all-to-all-done.refs_0_ = bf16[128,2,4096]{2,1,0:T(2,128)(2,1)} async-done(((bf16[128,2,4096]{2,1,0:T(2,128)(2,1)}), bf16[128,2,4096]{2,1,0:T(2,128)(2,1)}, u32[]{:S(2)}, u32[]{:S(2)}) %all-to-all-start) | async-done | bytes 2097184 | tf_op jit(solution)/shard_map/all_to_all | solution.py:300
  84.9 6.2 %shard_map.113 = (bf16[576,1024]{1,0:T(8,128)(2,1)}, bf16[576,1024]{1,0:T(8,128)(2,1)}, bf16[256,4096]{1,0:T(8,128)(2,1)}, bf16[256,384]{1,0:T(8,128)(2,1)}, f32[8,256]{1,0:T(8,128)}) custom-call(bf16[128,2,4096]{2,1,0:T(2,128)(2,1)} %all-to-all-done.refs_0_, bf16[576,1024]{1,0:T(8,128)(2,1)} %copy-done.7, ...), custom_call_target="tpu_custom_call" | custom-call | flops 1207959552 | bytes 9117696 | tf_op jit(solution)/shard_map/pallas_call | solution.py:79
  91.0 1.9 %collective-permute-start.8 = (bf16[576,1024]{1,0:T(8,128)(2,1)}, bf16[576,1024]{1,0:T(8,128)(2,1)}, u32[]{:S(2)}, u32[]{:S(2)}) collective-permute-start(bf16[576,1024]{1,0:T(8,128)(2,1)} %get-tuple-element.46), channel_id=1, source_target_pairs={{0,1},{1,2},{2,3},{3,0},{4,5},{5,6},{6,7},{7,4},{8,9},{9,10},{10,1... | collective-permute-start | bytes 3538952 | tf_op jit(solution)/shard_map/ppermute | solution.py:31
  93.0 4.6 %collective-permute-start.10 = (bf16[576,1024]{1,0:T(8,128)(2,1)}, bf16[576,1024]{1,0:T(8,128)(2,1)S(1)}, u32[]{:S(2)}, u32[]{:S(2)}) collective-permute-start(bf16[576,1024]{1,0:T(8,128)(2,1)} %get-tuple-element.49), channel_id=1, source_target_pairs={{0,3},{1,0},{2,1},{3,2},{4,7},{5,4},{6,5},{7,6},{8,11},{9,8},{10,9... | collective-permute-start | bytes 3538952 | tf_op jit(solution)/shard_map/ppermute | solution.py:35
  97.6 0.0 collective-permute-done.5.refs_4_.refs_8_
  97.6 8.9 %shard_map.114 = (bf16[576,1024]{1,0:T(8,128)(2,1)}, bf16[576,1024]{1,0:T(8,128)(2,1)}, bf16[576,1024]{1,0:T(8,128)(2,1)}, bf16[576,1024]{1,0:T(8,128)(2,1)}, bf...) custom-call(bf16[256,4096]{1,0:T(8,128)(2,1)} %get-tuple-element.30.refs_0_, ...), custom_call_target="tpu_custom_call" | custom-call | flops 2415919104 | bytes 11943936 | tf_op jit(solution)/shard_map/pallas_call | solution.py:79
  106.5 2.0 %collective-permute-start.6 = (bf16[576,1024]{1,0:T(8,128)(2,1)}, bf16[576,1024]{1,0:T(8,128)(2,1)}, u32[]{:S(2)}, u32[]{:S(2)}) collective-permute-start(bf16[576,1024]{1,0:T(8,128)(2,1)} %get-tuple-element.41), channel_id=1, source_target_pairs={{0,3},{1,0},{2,1},{3,2},{4,7},{5,4},{6,5},{7,6},{8,11},{9,8},{10,9... | collective-permute-start | bytes 3538952 | tf_op jit(solution)/shard_map/ppermute | solution.py:35
  108.5 3.5 %collective-permute-start.7 = (bf16[576,1024]{1,0:T(8,128)(2,1)}, bf16[576,1024]{1,0:T(8,128)(2,1)}, u32[]{:S(2)}, u32[]{:S(2)}) collective-permute-start(bf16[576,1024]{1,0:T(8,128)(2,1)} %get-tuple-element.43), channel_id=1, source_target_pairs={{0,1},{1,2},{2,3},{3,0},{4,5},{5,6},{6,7},{7,4},{8,9},{9,10},{10,1... | collective-permute-start | bytes 3538952 | tf_op jit(solution)/shard_map/ppermute | solution.py:31
  112.0 9.3 %shard_map.115 = (bf16[576,1024]{1,0:T(8,128)(2,1)}, bf16[576,1024]{1,0:T(8,128)(2,1)}, bf16[128,2,2176]{2,1,0:T(2,128)(2,1)}) custom-call(bf16[256,4096]{1,0:T(8,128)(2,1)} %get-tuple-element.30.refs_0_, bf16[576,1024]{1,0:T(8,128)(2,1)} %pad_maximum_fusion.refs_1_, bf16[576,1024]{1,0:T(8,128)(2,1)} %pad_maximum_fusion.1.refs_2_, ...), custom_call_target="tpu_custom_call" | custom-call | flops 2818572288 | bytes 15605760 | tf_op jit(solution)/shard_map/pallas_call | solution.py:79
  121.2 17.3 %all-to-all-start.1 = ((bf16[128,2,2176]{2,1,0:T(2,128)(2,1)}), bf16[128,2,2176]{2,1,0:T(2,128)(2,1)S(1)}, u32[]{:S(2)}, u32[]{:S(2)}) async-start(bf16[128,2,2176]{2,1,0:T(2,128)(2,1)} %get-tuple-element.36), calls=%async_computation.1 | async-start | bytes 2228224 | tf_op jit(solution)/shard_map/all_to_all | solution.py:349
  138.6 0.0 collective-permute-done.8.refs_1_
  138.6 3.0 %shard_map.118 = bf16[576,1024]{1,0:T(8,128)(2,1)} custom-call(bf16[576,1024]{1,0:T(8,128)(2,1)} %get-tuple-element.45.refs_0_, bf16[576,1024]{1,0:T(8,128)(2,1)} %collective-permute-done.8.refs_1_), custom_call_target="tpu_custom_call" | custom-call | bytes 3538944 | tf_op jit(solution)/shard_map/pallas_call | solution.py:79
  141.6 1.9 %collective-permute-start.9 = (bf16[576,1024]{1,0:T(8,128)(2,1)}, bf16[576,1024]{1,0:T(8,128)(2,1)}, u32[]{:S(2)}, u32[]{:S(2)}) collective-permute-start(bf16[576,1024]{1,0:T(8,128)(2,1)} %shard_map.118), channel_id=1, source_target_pairs={{0,1},{1,2},{2,3},{3,0},{4,5},{5,6},{6,7},{7,4},{8,9},{9,10},{10,1... | collective-permute-start | bytes 3538952 | tf_op jit(solution)/shard_map/ppermute | solution.py:31
  143.5 0.0 collective-permute-done.10.refs_1_
  143.5 1.0 copy-done.6
  144.6 3.0 %shard_map.119 = bf16[576,1024]{1,0:T(8,128)(2,1)} custom-call(bf16[576,1024]{1,0:T(8,128)(2,1)} %get-tuple-element.48.refs_0_, bf16[576,1024]{1,0:T(8,128)(2,1)} %copy-done.6), custom_call_target="tpu_custom_call" | custom-call | bytes 3538944 | tf_op jit(solution)/shard_map/pallas_call | solution.py:79
  147.6 4.9 %collective-permute-start.11 = (bf16[576,1024]{1,0:T(8,128)(2,1)}, bf16[576,1024]{1,0:T(8,128)(2,1)S(1)}, u32[]{:S(2)}, u32[]{:S(2)}) collective-permute-start(bf16[576,1024]{1,0:T(8,128)(2,1)} %shard_map.119), channel_id=1, source_target_pairs={{0,3},{1,0},{2,1},{3,2},{4,7},{5,4},{6,5},{7,6},{8,11},{9,8},{10,9... | collective-permute-start | bytes 3538952 | tf_op jit(solution)/shard_map/ppermute | solution.py:35
  152.4 0.0 collective-permute-done.6.refs_1_
  152.5 3.8 %shard_map.117 = (bf16[576,1024]{1,0:T(8,128)(2,1)}, bf16[576,1024]{1,0:T(8,128)(2,1)}) custom-call(bf16[576,1024]{1,0:T(8,128)(2,1)} %get-tuple-element.40.refs_0_, bf16[576,1024]{1,0:T(8,128)(2,1)} %collective-permute-done.6.refs_1_, bf16[576,1024]{1,0:T(8,128)(2,1)} %get-tuple-element.42.refs_2_, bf16[576,1024]{1,0:T(8,128)(2,1)} %collective-permute-done.7.refs_3_), custom_call_target="tpu_custom_call" | custom-call | flops 30000001024 | bytes 7077888 | tf_op jit(solution)/shard_map/pallas_call | solution.py:79
  156.3 14.0 %all-to-all-done.1.home_ref = bf16[128,2,2176]{2,1,0:T(2,128)(2,1)S(1)} async-done(((bf16[128,2,2176]{2,1,0:T(2,128)(2,1)}), bf16[128,2,2176]{2,1,0:T(2,128)(2,1)S(1)}, u32[]{:S(2)}, u32[]{:S(2)}) %all-to-all-start.1) | async-done | bytes 1114144 | tf_op jit(solution)/shard_map/all_to_all | solution.py:349
  170.3 1.0 shard_map.116
  171.3 0.6 convert_bitcast_fusion
  171.9 0.3 collective-permute-done.9.refs_1_
  172.2 4.9 %collective-permute-done.11.refs_3_ = bf16[576,1024]{1,0:T(8,128)(2,1)S(1)} collective-permute-done((bf16[576,1024]{1,0:T(8,128)(2,1)}, bf16[576,1024]{1,0:T(8,128)(2,1)S(1)}, u32[]{:S(2)}, u32[]{:S(2)}) %collective-permute-start.11) | collective-permute-done | bytes 1179680 | tf_op jit(solution)/shard_map/ppermute | solution.py:35
  177.1 1.0 copy-done.8
  178.2 4.0 %shard_map.120 = (bf16[192,2048]{1,0:T(8,128)(2,1)}, bf16[192,2048]{1,0:T(8,128)(2,1)}, bf16[192,2048]{1,0:T(8,128)(2,1)}) custom-call(bf16[576,1024]{1,0:T(8,128)(2,1)} %get-tuple-element.44.refs_0_, bf16[576,1024]{1,0:T(8,128)(2,1)} %collective-permute-done.9.refs_1_, bf16[576,1024]{1,0:T(8,128)(2,1)} %get-tuple-element.47.refs_2_, bf16[576,1024]{1,0:T(8,128)(2,1)} %copy-done.8), custom_call_target="tpu_custom_call" | custom-call | bytes 7077888 | tf_op jit(solution)/shard_map/pallas_call | solution.py:79
  (18 shorter events, 0.0 us)
Async XLA Ops:
  0.6 1.4 copy-start.10
  0.6 1.6 copy-start.9
  3.5 29.5 %collective-permute-start = (bf16[576,1024]{1,0:T(8,128)(2,1)}, bf16[576,1024]{1,0:T(8,128)(2,1)S(1)}, u32[]{:S(2)}, u32[]{:S(2)}) collective-permute-start(bf16[576,1024]{1,0:T(8,128)(2,1)} %pad_maximum_fusion.refs_1_), channel_id=1, source_target_pairs={{0,1},{1,2},{2,3},{3,0},{4,5},{5,6},{6,7},{7,4},{8,9},{9,10},{10,1... | collective-permute-start | bytes 3538952 | tf_op jit(solution)/shard_map/ppermute | solution.py:31
  7.4 4.4 %copy-start.2 = (bf16[16,2048]{1,0:T(8,128)(2,1)S(1)}, bf16[16,2048]{1,0:T(8,128)(2,1)}, u32[]{:S(2)}) copy-start(bf16[16,2048]{1,0:T(8,128)(2,1)} %tokens_ref.1) | copy-start | bytes 196612
  7.4 4.4 %copy-start.3 = (bf16[16,2048]{1,0:T(8,128)(2,1)S(1)}, bf16[16,2048]{1,0:T(8,128)(2,1)}, u32[]{:S(2)}) copy-start(bf16[16,2048]{1,0:T(8,128)(2,1)} %grad_ref.1) | copy-start | bytes 196612
  7.4 4.4 %copy-start.4 = (s32[16,8]{0,1:T(8,128)S(1)}, s32[16,8]{0,1:T(8,128)}, u32[]{:S(2)}) copy-start(s32[16,8]{0,1:T(8,128)} %param.9) | copy-start | bytes 1540
  7.4 4.4 %copy-start.5 = (bf16[16,8]{0,1:T(8,128)(2,1)S(1)}, bf16[16,8]{0,1:T(8,128)(2,1)}, u32[]{:S(2)}) copy-start(bf16[16,8]{0,1:T(8,128)(2,1)} %param.10) | copy-start | bytes 772
  8.6 26.9 %collective-permute-start.2 = (bf16[576,1024]{1,0:T(8,128)(2,1)}, bf16[576,1024]{1,0:T(8,128)(2,1)S(1)}, u32[]{:S(2)}, u32[]{:S(2)}) collective-permute-start(bf16[576,1024]{1,0:T(8,128)(2,1)} %pad_maximum_fusion.1.refs_2_), channel_id=1, source_target_pairs={{0,3},{1,0},{2,1},{3,2},{4,7},{5,4},{6,5},{7,6},{8,11},{9,8},{10,9... | collective-permute-start | bytes 3538952 | tf_op jit(solution)/shard_map/ppermute | solution.py:35
  14.1 70.8 %all-to-all-start = ((bf16[128,2,4096]{2,1,0:T(2,128)(2,1)}), bf16[128,2,4096]{2,1,0:T(2,128)(2,1)}, u32[]{:S(2)}, u32[]{:S(2)}) async-start(bf16[128,2,4096]{2,1,0:T(2,128)(2,1)} %get-tuple-element.29), calls=%async_computation | async-start | bytes 4194304 | tf_op jit(solution)/shard_map/all_to_all | solution.py:300
  32.9 2.5 %copy-start = (bf16[576,1024]{1,0:T(8,128)(2,1)}, bf16[576,1024]{1,0:T(8,128)(2,1)S(1)}, u32[]{:S(2)}) copy-start(bf16[576,1024]{1,0:T(8,128)(2,1)S(1)} %shard_map.111.refs_3_.refs_7_) | copy-start | bytes 3538948
  32.9 28.0 %collective-permute-start.1 = (bf16[576,1024]{1,0:T(8,128)(2,1)S(1)}, bf16[576,1024]{1,0:T(8,128)(2,1)S(1)}, u32[]{:S(2)}, u32[]{:S(2)}) collective-permute-start(bf16[576,1024]{1,0:T(8,128)(2,1)S(1)} %shard_map.111.refs_3_.refs_7_), channel_id=1, source_target_pairs={{0,1},{1,2},{2,3},{3,0},{4,5},{5,6},{6,7},{7,4},{8,9},{9,10},{10,1... | collective-permute-start | bytes 3538952 | tf_op jit(solution)/shard_map/ppermute | solution.py:31
  35.5 55.6 %copy-start.1 = (bf16[576,1024]{1,0:T(8,128)(2,1)}, bf16[576,1024]{1,0:T(8,128)(2,1)S(1)}, u32[]{:S(2)}) copy-start(bf16[576,1024]{1,0:T(8,128)(2,1)S(1)} %shard_map.112.refs_2_.refs_6_) | copy-start | bytes 3538948
  35.5 29.0 %collective-permute-start.3 = (bf16[576,1024]{1,0:T(8,128)(2,1)S(1)}, bf16[576,1024]{1,0:T(8,128)(2,1)}, u32[]{:S(2)}, u32[]{:S(2)}) collective-permute-start(bf16[576,1024]{1,0:T(8,128)(2,1)S(1)} %shard_map.112.refs_2_.refs_6_), channel_id=1, source_target_pairs={{0,3},{1,0},{2,1},{3,2},{4,7},{5,4},{6,5},{7,6},{8,11},{9,8},{10,9... | collective-permute-start | bytes 3538952 | tf_op jit(solution)/shard_map/ppermute | solution.py:35
  39.6 58.0 %collective-permute-start.4 = (bf16[576,1024]{1,0:T(8,128)(2,1)}, bf16[576,1024]{1,0:T(8,128)(2,1)}, u32[]{:S(2)}, u32[]{:S(2)}) collective-permute-start(bf16[576,1024]{1,0:T(8,128)(2,1)} %pad_maximum_fusion.refs_1_), channel_id=1, source_target_pairs={{0,3},{1,0},{2,1},{3,2},{4,7},{5,4},{6,5},{7,6},{8,11},{9,8},{10,9... | collective-permute-start | bytes 3538952 | tf_op jit(solution)/shard_map/ppermute | solution.py:35
  42.9 54.6 %collective-permute-start.5 = (bf16[576,1024]{1,0:T(8,128)(2,1)}, bf16[576,1024]{1,0:T(8,128)(2,1)}, u32[]{:S(2)}, u32[]{:S(2)}) collective-permute-start(bf16[576,1024]{1,0:T(8,128)(2,1)} %pad_maximum_fusion.1.refs_2_), channel_id=1, source_target_pairs={{0,1},{1,2},{2,3},{3,0},{4,5},{5,6},{6,7},{7,4},{8,9},{9,10},{10,1... | collective-permute-start | bytes 3538952 | tf_op jit(solution)/shard_map/ppermute | solution.py:31
  60.9 1.0 copy-start.7
  91.0 47.5 %collective-permute-start.8 = (bf16[576,1024]{1,0:T(8,128)(2,1)}, bf16[576,1024]{1,0:T(8,128)(2,1)}, u32[]{:S(2)}, u32[]{:S(2)}) collective-permute-start(bf16[576,1024]{1,0:T(8,128)(2,1)} %get-tuple-element.46), channel_id=1, source_target_pairs={{0,1},{1,2},{2,3},{3,0},{4,5},{5,6},{6,7},{7,4},{8,9},{9,10},{10,1... | collective-permute-start | bytes 3538952 | tf_op jit(solution)/shard_map/ppermute | solution.py:31
  93.0 50.5 %collective-permute-start.10 = (bf16[576,1024]{1,0:T(8,128)(2,1)}, bf16[576,1024]{1,0:T(8,128)(2,1)S(1)}, u32[]{:S(2)}, u32[]{:S(2)}) collective-permute-start(bf16[576,1024]{1,0:T(8,128)(2,1)} %get-tuple-element.49), channel_id=1, source_target_pairs={{0,3},{1,0},{2,1},{3,2},{4,7},{5,4},{6,5},{7,6},{8,11},{9,8},{10,9... | collective-permute-start | bytes 3538952 | tf_op jit(solution)/shard_map/ppermute | solution.py:35
  106.5 46.0 %collective-permute-start.6 = (bf16[576,1024]{1,0:T(8,128)(2,1)}, bf16[576,1024]{1,0:T(8,128)(2,1)}, u32[]{:S(2)}, u32[]{:S(2)}) collective-permute-start(bf16[576,1024]{1,0:T(8,128)(2,1)} %get-tuple-element.41), channel_id=1, source_target_pairs={{0,3},{1,0},{2,1},{3,2},{4,7},{5,4},{6,5},{7,6},{8,11},{9,8},{10,9... | collective-permute-start | bytes 3538952 | tf_op jit(solution)/shard_map/ppermute | solution.py:35
  108.5 44.0 %collective-permute-start.7 = (bf16[576,1024]{1,0:T(8,128)(2,1)}, bf16[576,1024]{1,0:T(8,128)(2,1)}, u32[]{:S(2)}, u32[]{:S(2)}) collective-permute-start(bf16[576,1024]{1,0:T(8,128)(2,1)} %get-tuple-element.43), channel_id=1, source_target_pairs={{0,1},{1,2},{2,3},{3,0},{4,5},{5,6},{6,7},{7,4},{8,9},{9,10},{10,1... | collective-permute-start | bytes 3538952 | tf_op jit(solution)/shard_map/ppermute | solution.py:31
  121.2 49.0 %all-to-all-start.1 = ((bf16[128,2,2176]{2,1,0:T(2,128)(2,1)}), bf16[128,2,2176]{2,1,0:T(2,128)(2,1)S(1)}, u32[]{:S(2)}, u32[]{:S(2)}) async-start(bf16[128,2,2176]{2,1,0:T(2,128)(2,1)} %get-tuple-element.36), calls=%async_computation.1 | async-start | bytes 2228224 | tf_op jit(solution)/shard_map/all_to_all | solution.py:349
  141.6 30.6 %collective-permute-start.9 = (bf16[576,1024]{1,0:T(8,128)(2,1)}, bf16[576,1024]{1,0:T(8,128)(2,1)}, u32[]{:S(2)}, u32[]{:S(2)}) collective-permute-start(bf16[576,1024]{1,0:T(8,128)(2,1)} %shard_map.118), channel_id=1, source_target_pairs={{0,1},{1,2},{2,3},{3,0},{4,5},{5,6},{6,7},{7,4},{8,9},{9,10},{10,1... | collective-permute-start | bytes 3538952 | tf_op jit(solution)/shard_map/ppermute | solution.py:31
  143.5 1.1 copy-start.6
  147.6 29.5 %collective-permute-start.11 = (bf16[576,1024]{1,0:T(8,128)(2,1)}, bf16[576,1024]{1,0:T(8,128)(2,1)S(1)}, u32[]{:S(2)}, u32[]{:S(2)}) collective-permute-start(bf16[576,1024]{1,0:T(8,128)(2,1)} %shard_map.119), channel_id=1, source_target_pairs={{0,3},{1,0},{2,1},{3,2},{4,7},{5,4},{6,5},{7,6},{8,11},{9,8},{10,9... | collective-permute-start | bytes 3538952 | tf_op jit(solution)/shard_map/ppermute | solution.py:35
  177.1 1.0 copy-start.8

commit v4 on v3

--- a/solution.py
+++ b/solution.py
@@ -141,41 +141,35 @@
     return d_pre.T.astype(jnp.bfloat16), d_s
 
 
-def blocks_body(width, units, parts, fetches, near_in, emits, near_out):
+def far_body(width, units, fetches, near_in, emits, near_out):
+    (wait_rows, rows_ref), weights = fetches[0], fetches[1:]
+    wait_rows()
+    send_rows, flat_ref = emits[2]
+    flat_ref[...] = rows_ref[...].reshape(flat_ref.shape)
+    send_rows()
+    for wait, _ in weights:
+        wait()
+    refs = [ref for _, ref in weights]
+    d_pre, d_s = block_grads(width, units, flat_ref, refs, emits[:2])
+    near_out[0][...] = d_pre
+    near_out[1][...] = jnp.broadcast_to(d_s, near_out[1].shape)
+
+
+def rest_body(width, units, parts, fetches, near_in, emits, near_out):
     (wait_rows, rows_ref), weights = fetches[0], split_parts(parts, fetches[1:])
-    count = len(parts)
+    count, half = len(parts), width // 2
+    refs = [[ref for _, ref in pairs] for pairs in weights]
     wait_rows()
-    if len(rows_ref.shape) == 3:
-        send_rows, flat_ref = emits[2 * count]
-        flat_ref[...] = rows_ref[...].reshape(flat_ref.shape)
-        send_rows()
-        rows_ref = flat_ref
-    total = sum(ref[:1] for ref in near_in)
+    d_pre, d_s = [near_in[0][...]], near_in[1][:1]
     for b in range(count):
         for wait, _ in weights[b]:
             wait()
-        refs = [ref for _, ref in weights[b]]
-        out = emits[2 * b : 2 * b + 2]
-        d_pre, d_s = block_grads(width, units, rows_ref, refs, out)
-        near_out[b][...] = d_pre
-        total = total + d_s
-    near_out[count][...] = jnp.broadcast_to(total, near_out[count].shape)
-
-
-def own_body(width, units, parts, fetches, near_in, emits, near_out):
-    (wait_rows, rows_ref), weights = fetches[0], split_parts(parts, fetches[1:])
-    count, half = len(parts), width // 2
-    wait_rows()
-    for wait, _ in weights[0]:
-        wait()
-    refs = [[ref for _, ref in pairs] for pairs in weights]
-    d_pre, d_s = block_grads(width, units, rows_ref, refs[0], emits[:2])
-    d_pre = [d_pre] + [ref[...] for ref in near_in[: count - 1]]
-    d_s = d_s + near_in[count - 1][:1]
-    for pairs in weights[1:]:
-        for wait, _ in pairs:
-            wait()
-    send, out_ref = emits[2]
+        if b > 0:
+            grads = emits[2 * (b - 1) : 2 * b]
+            terms = block_grads(width, units, rows_ref, refs[b], grads)
+            d_pre.append(terms[0])
+            d_s = d_s + terms[1]
+    send, out_ref = emits[-1]
     gates = slice(0, 2 * units)
     for i in range(2):
         total = sum(dot(d_pre[b], halves(refs[b], gates)[i], PLAIN) for b in range(count))
@@ -301,41 +295,30 @@
         outgoing, ("node", "expert"), 0, 0, tiled=True
     )
     half_grad = shape((3 * units, half), bf16)
-    near = [shape((slot_count, 2 * units), bf16), shape((SUBLANES, slot_count), f32)]
-
-    def blocks(weights, so_far, rows, extra=()):
-        count = len(weights)
-        results = on_core(
-            functools.partial(blocks_body, width, units, [len(w) for w in weights]),
-            [rows, *[w for ws in weights for w in ws]],
-            so_far,
-            [half_grad] * (2 * count) + list(extra),
-            [near[0]] * count + [near[1]],
-            count * 12 * slot_count * units * width,
-        )
-        sent = 2 * count + len(extra)
-        return results[:sent], results[sent : sent + count], results[sent + count :]
-
-    (far_grad_a, far_grad_b, flat_rows), far_pre, far_s = blocks(
-        [(far_a, far_b)], [], rows, [shape((slot_count, 2 * width), bf16)]
+    block_flops = 12 * slot_count * units * width
+
+    far_grad_a, far_grad_b, flat_rows, far_pre, far_s = on_core(
+        functools.partial(far_body, width, units),
+        [rows, far_a, far_b],
+        [],
+        [half_grad, half_grad, shape((slot_count, 2 * width), bf16)],
+        [shape((slot_count, 2 * units), bf16), shape((SUBLANES, slot_count), f32)],
+        block_flops,
     )
     passing_a = right(far_grad_a, ring)
     passing_b = left(far_grad_b, ring)
-    (nxt_a, nxt_b, prev_a, prev_b), near_pre, near_s = blocks(
-        [after, before], far_s, flat_rows
+    nxt_a, nxt_b, prev_a, prev_b, mine_a, mine_b, returning = on_core(
+        functools.partial(rest_body, width, units, [2] * ring),
+        [flat_rows, far_a, far_b, *after, *before, own_a, own_b],
+        [far_pre, far_s],
+        [half_grad] * 6 + [shape((expert_count, CAP, width + LANES), bf16)],
+        [],
+        4 * block_flops,
     )
     left_b = right(nxt_b, ring)
     right_a = left(prev_a, ring)
-    left_a = right(added((nxt_a, passing_a))[0], ring)
-    right_b = left(added((prev_b, passing_b))[0], ring)
-    mine_a, mine_b, returning = on_core(
-        functools.partial(own_body, width, units, [2, 2, 2, 2]),
-        [flat_rows, own_a, own_b, far_a, far_b, *after, *before],
-        [*far_pre, *near_pre, *near_s],
-        [half_grad, half_grad, shape((expert_count, CAP, width + LANES), bf16)],
-        [],
-        28 * slot_count * units * width,
-    )
+    left_a = right((nxt_a.astype(f32) + passing_a.astype(f32)).astype(bf16), ring)
+    right_b = left((prev_b.astype(f32) + passing_b.astype(f32)).astype(bf16), ring)
     part_a, part_b = added((mine_a, right_a), (mine_b, left_b), flops=FLOPS_PART)
     d_gate, d_up, d_down = on_core(
         functools.partial(total_body, units),

time: 184 us -> 180 us (0.978)
  Pallas kernels: 41.5 us -> 30.7 us
  waiting for transfers between devices: 58.2 us -> 62.3 us
  other arithmetic: 2.81 us -> 6.16 us
    pallas_call x7 -> x4, Pallas kernels: 38.1 us -> 27.4 us  [on_core(): pl.pallas_call(kernel, out_shape=[*far_outs, *near_outs], in_specs=[hbm]...]
    ppermute x6, waiting for transfers between devices: 16.4 us -> 21 us  [right(): lax.ppermute(part, 'block', [(i, (i + 1) % ring) for i in range(ring)])]
    convert_element_type x0 -> x2, other arithmetic: none -> 3.32 us  [the longest x1 2.86 us: on_device(): (nxt_a.astype(f32) + passing_a.astype(f32)).astype(bf16)]
  transfers between devices with their start and end apart: 14 -> 14, of which waited for: 6 -> 7; matrix products, arithmetic and copies ran while one was open for 1% -> 3% of each run, Pallas kernels for 21% -> 15%
where the time goes in v4:
time: 180 us; the launch traced here: 178 us
  starting transfers between devices  73.6 us (41%)
  waiting for transfers between devices  62.3 us (35%)
  Pallas kernels  30.7 us (17%)
  other arithmetic  6.16 us (3%)
  local copies, waits for them, and re-layouts  3.95 us (2%)
    pallas_call x4, Pallas kernels, on_core(): pl.pallas_call(kernel, out_shape=[*far_outs, *near_outs], in_specs=[hbm]...  27.4 us
    ppermute x6, starting transfers between devices, left(): lax.ppermute(part, 'block', [(i, (i - 1) % ring) for i in range(ring)])  22.2 us
    ppermute x6, waiting for transfers between devices, right(): lax.ppermute(part, 'block', [(i, (i + 1) % ring) for i in range(ring)])  21 us
    all_to_all x1, waiting for transfers between devices, on_device(): rows = lax.all_to_all(outgoing, ('node', 'expert'), 0, 0, tiled=True)  20.4 us
    all_to_all x1, starting transfers between devices, on_device(): rows = lax.all_to_all(outgoing, ('node', 'expert'), 0, 0, tiled=True)  18.8 us
    all_to_all x1, starting transfers between devices, on_device(): home = lax.all_to_all(returning, ('node', 'expert'), 0, 0, tiled=True)  17.1 us
    ppermute x6, starting transfers between devices, right(): lax.ppermute(part, 'block', [(i, (i + 1) % ring) for i in range(ring)])  15.5 us
    all_to_all x1, waiting for transfers between devices, on_device(): home = lax.all_to_all(returning, ('node', 'expert'), 0, 0, tiled=True)  14 us
  transfers between devices with their start and end apart: 14, of which 7 were waited for; matrix products, arithmetic and copies ran while one was open for 3% of the time, Pallas kernels for 15%

profile of v4, /device:TPU:1, one launch (start us, length us, event | category | flops | bytes accessed | tf_op | source)
XLA Modules:
  0.0 177.9 jit_solution(14595480403950691012)
XLA Ops:
  0.7 1.3 fusion.2
  1.9 0.1 copy-done.9
  2.0 0.2 copy-done.8
  2.2 0.1 fusion
  2.4 1.1 pad_maximum_fusion.refs_7_
  3.5 3.9 %collective-permute-start = (bf16[576,1024]{1,0:T(8,128)(2,1)}, bf16[576,1024]{1,0:T(8,128)(2,1)S(1)}, u32[]{:S(2)}, u32[]{:S(2)}) collective-permute-start(bf16[576,1024]{1,0:T(8,128)(2,1)} %pad_maximum_fusion.refs_7_), channel_id=1, source_target_pairs={{0,1},{1,2},{2,3},{3,0},{4,5},{5,6},{6,7},{7,4},{8,9},{9,10},{10,1... | collective-permute-start | bytes 3538952 | tf_op jit(solution)/shard_map/ppermute | solution.py:31
  7.5 0.0 copy-start
  7.5 0.0 copy-start.1
  7.5 0.0 copy-start.2
  7.5 0.0 copy-start.3
  7.5 1.1 pad_maximum_fusion.1.refs_8_
  8.7 3.2 %collective-permute-start.2 = (bf16[576,1024]{1,0:T(8,128)(2,1)}, bf16[576,1024]{1,0:T(8,128)(2,1)S(1)}, u32[]{:S(2)}, u32[]{:S(2)}) collective-permute-start(bf16[576,1024]{1,0:T(8,128)(2,1)} %pad_maximum_fusion.1.refs_8_), channel_id=1, source_target_pairs={{0,3},{1,0},{2,1},{3,2},{4,7},{5,4},{6,5},{7,6},{8,11},{9,8},{10,9... | collective-permute-start | bytes 3538952 | tf_op jit(solution)/shard_map/ppermute | solution.py:35
  11.9 2.3 %shard_map.110 = (bf16[128,2,4096]{2,1,0:T(2,128)(2,1)}, bf16[256,16]{1,0:T(8,128)(2,1)S(1)}) custom-call(s32[8,16]{1,0:T(8,128)S(1)} %bitcast.10, bf16[8,16]{1,0:T(8,128)(2,1)S(1)} %bitcast.12, bf16[16,2048]{1,0:T(8,128)(2,1)S(1)} %copy-done, bf16[16,2048]{1,0:T(8,128)(2,1)S(1)} %copy-done.1), custom_call_target="tpu_custom_call" | custom-call | bytes 2237184 | tf_op jit(solution)/shard_map/pallas_call | solution.py:257
  14.2 18.8 %all-to-all-start = ((bf16[128,2,4096]{2,1,0:T(2,128)(2,1)}), bf16[128,2,4096]{2,1,0:T(2,128)(2,1)}, u32[]{:S(2)}, u32[]{:S(2)}) async-start(bf16[128,2,4096]{2,1,0:T(2,128)(2,1)} %get-tuple-element.26), calls=%async_computation | async-start | bytes 4194304 | tf_op jit(solution)/shard_map/all_to_all | solution.py:294
  33.0 0.0 collective-permute-done.part_ref
  33.0 2.5 %collective-permute-start.1 = (bf16[576,1024]{1,0:T(8,128)(2,1)S(1)}, bf16[576,1024]{1,0:T(8,128)(2,1)S(1)}, u32[]{:S(2)}, u32[]{:S(2)}) collective-permute-start(bf16[576,1024]{1,0:T(8,128)(2,1)S(1)} %shard_map.111.refs_5_), channel_id=1, source_target_pairs={{0,1},{1,2},{2,3},{3,0},{4,5},{5,6},{6,7},{7,4},{8,9},{9,10},{10,1... | collective-permute-start | bytes 3538952 | tf_op jit(solution)/shard_map/ppermute | solution.py:31
  35.5 0.0 collective-permute-done.2.part_ref
  35.6 4.1 %collective-permute-start.3 = (bf16[576,1024]{1,0:T(8,128)(2,1)S(1)}, bf16[576,1024]{1,0:T(8,128)(2,1)}, u32[]{:S(2)}, u32[]{:S(2)}) collective-permute-start(bf16[576,1024]{1,0:T(8,128)(2,1)S(1)} %shard_map.112.refs_4_), channel_id=1, source_target_pairs={{0,3},{1,0},{2,1},{3,2},{4,7},{5,4},{6,5},{7,6},{8,11},{9,8},{10,9... | collective-permute-start | bytes 3538952 | tf_op jit(solution)/shard_map/ppermute | solution.py:35
  39.6 3.4 %collective-permute-start.4 = (bf16[576,1024]{1,0:T(8,128)(2,1)}, bf16[576,1024]{1,0:T(8,128)(2,1)}, u32[]{:S(2)}, u32[]{:S(2)}) collective-permute-start(bf16[576,1024]{1,0:T(8,128)(2,1)} %pad_maximum_fusion.refs_7_), channel_id=1, source_target_pairs={{0,3},{1,0},{2,1},{3,2},{4,7},{5,4},{6,5},{7,6},{8,11},{9,8},{10,9... | collective-permute-start | bytes 3538952 | tf_op jit(solution)/shard_map/ppermute | solution.py:35
  43.0 1.9 %collective-permute-start.5 = (bf16[576,1024]{1,0:T(8,128)(2,1)}, bf16[576,1024]{1,0:T(8,128)(2,1)}, u32[]{:S(2)}, u32[]{:S(2)}) collective-permute-start(bf16[576,1024]{1,0:T(8,128)(2,1)} %pad_maximum_fusion.1.refs_8_), channel_id=1, source_target_pairs={{0,1},{1,2},{2,3},{3,0},{4,5},{5,6},{6,7},{7,4},{8,9},{9,10},{10,1... | collective-permute-start | bytes 3538952 | tf_op jit(solution)/shard_map/ppermute | solution.py:31
  44.9 16.1 %collective-permute-done.1.refs_1_ = bf16[576,1024]{1,0:T(8,128)(2,1)S(1)} collective-permute-done((bf16[576,1024]{1,0:T(8,128)(2,1)S(1)}, bf16[576,1024]{1,0:T(8,128)(2,1)S(1)}, u32[]{:S(2)}, u32[]{:S(2)}) %collective-permute-start.1) | collective-permute-done | bytes 1179680 | tf_op jit(solution)/shard_map/ppermute | solution.py:31
  61.0 1.1 copy-done.10
  62.1 2.5 %collective-permute-done.3.refs_2_ = bf16[576,1024]{1,0:T(8,128)(2,1)} collective-permute-done((bf16[576,1024]{1,0:T(8,128)(2,1)S(1)}, bf16[576,1024]{1,0:T(8,128)(2,1)}, u32[]{:S(2)}, u32[]{:S(2)}) %collective-permute-start.3) | collective-permute-done | bytes 1179680 | tf_op jit(solution)/shard_map/ppermute | solution.py:35
  64.6 20.4 %all-to-all-done.refs_0_ = bf16[128,2,4096]{2,1,0:T(2,128)(2,1)} async-done(((bf16[128,2,4096]{2,1,0:T(2,128)(2,1)}), bf16[128,2,4096]{2,1,0:T(2,128)(2,1)}, u32[]{:S(2)}, u32[]{:S(2)}) %all-to-all-start) | async-done | bytes 2097184 | tf_op jit(solution)/shard_map/all_to_all | solution.py:294
  84.9 6.1 %shard_map.113 = (bf16[576,1024]{1,0:T(8,128)(2,1)}, bf16[576,1024]{1,0:T(8,128)(2,1)}, bf16[256,4096]{1,0:T(8,128)(2,1)}, bf16[256,384]{1,0:T(8,128)(2,1)}, f32[8,256]{1,0:T(8,128)}) custom-call(bf16[128,2,4096]{2,1,0:T(2,128)(2,1)} %all-to-all-done.refs_0_, bf16[576,1024]{1,0:T(8,128)(2,1)} %copy-done.10, bf16[576,1024]{1,0:T(8,128)(2,1)} %collective-permute-done.3.refs_2_), custom_call_target="tpu_custom_call" | custom-call | flops 1207959552 | bytes 9117696 | tf_op jit(solution)/shard_map/pallas_call | solution.py:79
  91.1 1.9 %collective-permute-start.8 = (bf16[576,1024]{1,0:T(8,128)(2,1)}, bf16[576,1024]{1,0:T(8,128)(2,1)S(1)}, u32[]{:S(2)}, u32[]{:S(2)}) collective-permute-start(bf16[576,1024]{1,0:T(8,128)(2,1)} %get-tuple-element.40), channel_id=1, source_target_pairs={{0,1},{1,2},{2,3},{3,0},{4,5},{5,6},{6,7},{7,4},{8,9},{9,10},{10,1... | collective-permute-start | bytes 3538952 | tf_op jit(solution)/shard_map/ppermute | solution.py:31
  93.0 4.8 %collective-permute-start.10 = (bf16[576,1024]{1,0:T(8,128)(2,1)}, bf16[576,1024]{1,0:T(8,128)(2,1)S(1)}, u32[]{:S(2)}, u32[]{:S(2)}) collective-permute-start(bf16[576,1024]{1,0:T(8,128)(2,1)} %get-tuple-element.43), channel_id=1, source_target_pairs={{0,3},{1,0},{2,1},{3,2},{4,7},{5,4},{6,5},{7,6},{8,11},{9,8},{10,9... | collective-permute-start | bytes 3538952 | tf_op jit(solution)/shard_map/ppermute | solution.py:35
  97.8 0.0 collective-permute-done.4.refs_3_
  97.8 0.0 collective-permute-done.5.refs_6_
  97.8 13.4 %shard_map.114 = (bf16[576,1024]{1,0:T(8,128)(2,1)}, bf16[576,1024]{1,0:T(8,128)(2,1)}, bf16[576,1024]{1,0:T(8,128)(2,1)}, bf16[576,1024]{1,0:T(8,128)(2,1)}, bf...) custom-call(bf16[256,4096]{1,0:T(8,128)(2,1)} %get-tuple-element.27.refs_0_, ...), custom_call_target="tpu_custom_call" | custom-call | flops 4831838208 | bytes 19931136 | tf_op jit(solution)/shard_map/pallas_call | solution.py:79
  111.2 2.0 %collective-permute-start.6 = (bf16[576,1024]{1,0:T(8,128)(2,1)}, bf16[576,1024]{1,0:T(8,128)(2,1)}, u32[]{:S(2)}, u32[]{:S(2)}) collective-permute-start(bf16[576,1024]{1,0:T(8,128)(2,1)} %get-tuple-element.35), channel_id=1, source_target_pairs={{0,3},{1,0},{2,1},{3,2},{4,7},{5,4},{6,5},{7,6},{8,11},{9,8},{10,9... | collective-permute-start | bytes 3538952 | tf_op jit(solution)/shard_map/ppermute | solution.py:35
  113.2 3.3 %collective-permute-start.7 = (bf16[576,1024]{1,0:T(8,128)(2,1)}, bf16[576,1024]{1,0:T(8,128)(2,1)}, u32[]{:S(2)}, u32[]{:S(2)}) collective-permute-start(bf16[576,1024]{1,0:T(8,128)(2,1)} %get-tuple-element.37), channel_id=1, source_target_pairs={{0,1},{1,2},{2,3},{3,0},{4,5},{5,6},{6,7},{7,4},{8,9},{9,10},{10,1... | collective-permute-start | bytes 3538952 | tf_op jit(solution)/shard_map/ppermute | solution.py:31
  116.5 17.1 %all-to-all-start.1 = ((bf16[128,2,2176]{2,1,0:T(2,128)(2,1)}), bf16[128,2,2176]{2,1,0:T(2,128)(2,1)S(1)}, u32[]{:S(2)}, u32[]{:S(2)}) async-start(bf16[128,2,2176]{2,1,0:T(2,128)(2,1)} %get-tuple-element.30), calls=%async_computation.1 | async-start | bytes 2228224 | tf_op jit(solution)/shard_map/all_to_all | solution.py:332
  133.6 0.0 collective-permute-done.8
  133.7 2.9 %add_convert_fusion.1 = bf16[576,1024]{1,0:T(8,128)(2,1)} fusion(bf16[576,1024]{1,0:T(8,128)(2,1)S(1)} %collective-permute-done.8, bf16[576,1024]{1,0:T(8,128)(2,1)} %get-tuple-element.39), kind=kLoop, calls=%fused_computation.1 | loop fusion | flops 2359296 | bytes 3538944 | tf_op jit(solution)/shard_map/convert_element_type | solution.py:320
  136.5 1.9 %collective-permute-start.9 = (bf16[576,1024]{1,0:T(8,128)(2,1)}, bf16[576,1024]{1,0:T(8,128)(2,1)}, u32[]{:S(2)}, u32[]{:S(2)}) collective-permute-start(bf16[576,1024]{1,0:T(8,128)(2,1)} %add_convert_fusion.1), channel_id=1, source_target_pairs={{0,1},{1,2},{2,3},{3,0},{4,5},{5,6},{6,7},{7,4},{8,9},{9,10},{10,1... | collective-permute-start | bytes 3538952 | tf_op jit(solution)/shard_map/ppermute | solution.py:31
  138.4 0.0 collective-permute-done.10
  138.5 0.5 add_convert_fusion
  138.9 4.9 %collective-permute-start.11 = (bf16[576,1024]{1,0:T(8,128)(2,1)S(1)}, bf16[576,1024]{1,0:T(8,128)(2,1)S(1)}, u32[]{:S(2)}, u32[]{:S(2)}) collective-permute-start(bf16[576,1024]{1,0:T(8,128)(2,1)S(1)} %add_convert_fusion), channel_id=1, source_target_pairs={{0,3},{1,0},{2,1},{3,2},{4,7},{5,4},{6,5},{7,6},{8,11},{9,8},{10,9... | collective-permute-start | bytes 3538952 | tf_op jit(solution)/shard_map/ppermute | solution.py:35
  143.8 3.7 %collective-permute-done.6.refs_1_ = bf16[576,1024]{1,0:T(8,128)(2,1)} collective-permute-done((bf16[576,1024]{1,0:T(8,128)(2,1)}, bf16[576,1024]{1,0:T(8,128)(2,1)}, u32[]{:S(2)}, u32[]{:S(2)}) %collective-permute-start.6) | collective-permute-done | bytes 1179680 | tf_op jit(solution)/shard_map/ppermute | solution.py:35
  147.5 3.9 %shard_map.116 = (bf16[576,1024]{1,0:T(8,128)(2,1)}, bf16[576,1024]{1,0:T(8,128)(2,1)}) custom-call(bf16[576,1024]{1,0:T(8,128)(2,1)} %get-tuple-element.34.refs_0_, bf16[576,1024]{1,0:T(8,128)(2,1)} %collective-permute-done.6.refs_1_, bf16[576,1024]{1,0:T(8,128)(2,1)} %get-tuple-element.36.refs_2_, bf16[576,1024]{1,0:T(8,128)(2,1)} %collective-permute-done.7.refs_3_), custom_call_target="tpu_custom_call" | custom-call | flops 30000001024 | bytes 7077888 | tf_op jit(solution)/shard_map/pallas_call | solution.py:79
  151.4 14.0 %all-to-all-done.1.home_ref = bf16[128,2,2176]{2,1,0:T(2,128)(2,1)S(1)} async-done(((bf16[128,2,2176]{2,1,0:T(2,128)(2,1)}), bf16[128,2,2176]{2,1,0:T(2,128)(2,1)S(1)}, u32[]{:S(2)}, u32[]{:S(2)}) %all-to-all-start.1) | async-done | bytes 1114144 | tf_op jit(solution)/shard_map/all_to_all | solution.py:332
  165.4 1.0 shard_map.115
  166.4 0.6 convert_bitcast_fusion
  167.0 4.9 %collective-permute-done.9.refs_1_ = bf16[576,1024]{1,0:T(8,128)(2,1)} collective-permute-done((bf16[576,1024]{1,0:T(8,128)(2,1)}, bf16[576,1024]{1,0:T(8,128)(2,1)}, u32[]{:S(2)}, u32[]{:S(2)}) %collective-permute-start.9) | collective-permute-done | bytes 1179680 | tf_op jit(solution)/shard_map/ppermute | solution.py:31
  171.9 0.8 collective-permute-done.11.refs_3_
  172.7 1.1 copy-done.7
  173.8 4.0 %shard_map.117 = (bf16[192,2048]{1,0:T(8,128)(2,1)}, bf16[192,2048]{1,0:T(8,128)(2,1)}, bf16[192,2048]{1,0:T(8,128)(2,1)}) custom-call(bf16[576,1024]{1,0:T(8,128)(2,1)} %get-tuple-element.38.refs_0_, bf16[576,1024]{1,0:T(8,128)(2,1)} %collective-permute-done.9.refs_1_, bf16[576,1024]{1,0:T(8,128)(2,1)} %get-tuple-element.41.refs_2_, bf16[576,1024]{1,0:T(8,128)(2,1)} %copy-done.7), custom_call_target="tpu_custom_call" | custom-call | bytes 7077888 | tf_op jit(solution)/shard_map/pallas_call | solution.py:79
  (17 shorter events, 0.0 us)
Async XLA Ops:
  0.6 1.4 copy-start.9
  0.6 1.6 copy-start.8
  3.5 29.5 %collective-permute-start = (bf16[576,1024]{1,0:T(8,128)(2,1)}, bf16[576,1024]{1,0:T(8,128)(2,1)S(1)}, u32[]{:S(2)}, u32[]{:S(2)}) collective-permute-start(bf16[576,1024]{1,0:T(8,128)(2,1)} %pad_maximum_fusion.refs_7_), channel_id=1, source_target_pairs={{0,1},{1,2},{2,3},{3,0},{4,5},{5,6},{6,7},{7,4},{8,9},{9,10},{10,1... | collective-permute-start | bytes 3538952 | tf_op jit(solution)/shard_map/ppermute | solution.py:31
  7.5 4.4 %copy-start = (bf16[16,2048]{1,0:T(8,128)(2,1)S(1)}, bf16[16,2048]{1,0:T(8,128)(2,1)}, u32[]{:S(2)}) copy-start(bf16[16,2048]{1,0:T(8,128)(2,1)} %tokens_ref.1) | copy-start | bytes 196612
  7.5 4.4 %copy-start.1 = (bf16[16,2048]{1,0:T(8,128)(2,1)S(1)}, bf16[16,2048]{1,0:T(8,128)(2,1)}, u32[]{:S(2)}) copy-start(bf16[16,2048]{1,0:T(8,128)(2,1)} %grad_ref.1) | copy-start | bytes 196612
  7.5 4.4 %copy-start.2 = (s32[16,8]{0,1:T(8,128)S(1)}, s32[16,8]{0,1:T(8,128)}, u32[]{:S(2)}) copy-start(s32[16,8]{0,1:T(8,128)} %param.9) | copy-start | bytes 1540
  7.5 4.4 %copy-start.3 = (bf16[16,8]{0,1:T(8,128)(2,1)S(1)}, bf16[16,8]{0,1:T(8,128)(2,1)}, u32[]{:S(2)}) copy-start(bf16[16,8]{0,1:T(8,128)(2,1)} %param.10) | copy-start | bytes 772
  8.7 26.9 %collective-permute-start.2 = (bf16[576,1024]{1,0:T(8,128)(2,1)}, bf16[576,1024]{1,0:T(8,128)(2,1)S(1)}, u32[]{:S(2)}, u32[]{:S(2)}) collective-permute-start(bf16[576,1024]{1,0:T(8,128)(2,1)} %pad_maximum_fusion.1.refs_8_), channel_id=1, source_target_pairs={{0,3},{1,0},{2,1},{3,2},{4,7},{5,4},{6,5},{7,6},{8,11},{9,8},{10,9... | collective-permute-start | bytes 3538952 | tf_op jit(solution)/shard_map/ppermute | solution.py:35
  14.2 70.8 %all-to-all-start = ((bf16[128,2,4096]{2,1,0:T(2,128)(2,1)}), bf16[128,2,4096]{2,1,0:T(2,128)(2,1)}, u32[]{:S(2)}, u32[]{:S(2)}) async-start(bf16[128,2,4096]{2,1,0:T(2,128)(2,1)} %get-tuple-element.26), calls=%async_computation | async-start | bytes 4194304 | tf_op jit(solution)/shard_map/all_to_all | solution.py:294
  33.0 2.5 %copy-start.4 = (bf16[576,1024]{1,0:T(8,128)(2,1)}, bf16[576,1024]{1,0:T(8,128)(2,1)S(1)}, u32[]{:S(2)}) copy-start(bf16[576,1024]{1,0:T(8,128)(2,1)S(1)} %shard_map.111.refs_5_) | copy-start | bytes 3538948
  33.0 28.0 %collective-permute-start.1 = (bf16[576,1024]{1,0:T(8,128)(2,1)S(1)}, bf16[576,1024]{1,0:T(8,128)(2,1)S(1)}, u32[]{:S(2)}, u32[]{:S(2)}) collective-permute-start(bf16[576,1024]{1,0:T(8,128)(2,1)S(1)} %shard_map.111.refs_5_), channel_id=1, source_target_pairs={{0,1},{1,2},{2,3},{3,0},{4,5},{5,6},{6,7},{7,4},{8,9},{9,10},{10,1... | collective-permute-start | bytes 3538952 | tf_op jit(solution)/shard_map/ppermute | solution.py:31
  35.5 55.5 %copy-start.5 = (bf16[576,1024]{1,0:T(8,128)(2,1)}, bf16[576,1024]{1,0:T(8,128)(2,1)S(1)}, u32[]{:S(2)}) copy-start(bf16[576,1024]{1,0:T(8,128)(2,1)S(1)} %shard_map.112.refs_4_) | copy-start | bytes 3538948
  35.6 29.0 %collective-permute-start.3 = (bf16[576,1024]{1,0:T(8,128)(2,1)S(1)}, bf16[576,1024]{1,0:T(8,128)(2,1)}, u32[]{:S(2)}, u32[]{:S(2)}) collective-permute-start(bf16[576,1024]{1,0:T(8,128)(2,1)S(1)} %shard_map.112.refs_4_), channel_id=1, source_target_pairs={{0,3},{1,0},{2,1},{3,2},{4,7},{5,4},{6,5},{7,6},{8,11},{9,8},{10,9... | collective-permute-start | bytes 3538952 | tf_op jit(solution)/shard_map/ppermute | solution.py:35
  39.6 58.2 %collective-permute-start.4 = (bf16[576,1024]{1,0:T(8,128)(2,1)}, bf16[576,1024]{1,0:T(8,128)(2,1)}, u32[]{:S(2)}, u32[]{:S(2)}) collective-permute-start(bf16[576,1024]{1,0:T(8,128)(2,1)} %pad_maximum_fusion.refs_7_), channel_id=1, source_target_pairs={{0,3},{1,0},{2,1},{3,2},{4,7},{5,4},{6,5},{7,6},{8,11},{9,8},{10,9... | collective-permute-start | bytes 3538952 | tf_op jit(solution)/shard_map/ppermute | solution.py:35
  43.0 54.8 %collective-permute-start.5 = (bf16[576,1024]{1,0:T(8,128)(2,1)}, bf16[576,1024]{1,0:T(8,128)(2,1)}, u32[]{:S(2)}, u32[]{:S(2)}) collective-permute-start(bf16[576,1024]{1,0:T(8,128)(2,1)} %pad_maximum_fusion.1.refs_8_), channel_id=1, source_target_pairs={{0,1},{1,2},{2,3},{3,0},{4,5},{5,6},{6,7},{7,4},{8,9},{9,10},{10,1... | collective-permute-start | bytes 3538952 | tf_op jit(solution)/shard_map/ppermute | solution.py:31
  61.0 1.1 copy-start.10
  91.1 42.5 %collective-permute-start.8 = (bf16[576,1024]{1,0:T(8,128)(2,1)}, bf16[576,1024]{1,0:T(8,128)(2,1)S(1)}, u32[]{:S(2)}, u32[]{:S(2)}) collective-permute-start(bf16[576,1024]{1,0:T(8,128)(2,1)} %get-tuple-element.40), channel_id=1, source_target_pairs={{0,1},{1,2},{2,3},{3,0},{4,5},{5,6},{6,7},{7,4},{8,9},{9,10},{10,1... | collective-permute-start | bytes 3538952 | tf_op jit(solution)/shard_map/ppermute | solution.py:31
  93.0 45.4 %collective-permute-start.10 = (bf16[576,1024]{1,0:T(8,128)(2,1)}, bf16[576,1024]{1,0:T(8,128)(2,1)S(1)}, u32[]{:S(2)}, u32[]{:S(2)}) collective-permute-start(bf16[576,1024]{1,0:T(8,128)(2,1)} %get-tuple-element.43), channel_id=1, source_target_pairs={{0,3},{1,0},{2,1},{3,2},{4,7},{5,4},{6,5},{7,6},{8,11},{9,8},{10,9... | collective-permute-start | bytes 3538952 | tf_op jit(solution)/shard_map/ppermute | solution.py:35
  111.2 36.3 %collective-permute-start.6 = (bf16[576,1024]{1,0:T(8,128)(2,1)}, bf16[576,1024]{1,0:T(8,128)(2,1)}, u32[]{:S(2)}, u32[]{:S(2)}) collective-permute-start(bf16[576,1024]{1,0:T(8,128)(2,1)} %get-tuple-element.35), channel_id=1, source_target_pairs={{0,3},{1,0},{2,1},{3,2},{4,7},{5,4},{6,5},{7,6},{8,11},{9,8},{10,9... | collective-permute-start | bytes 3538952 | tf_op jit(solution)/shard_map/ppermute | solution.py:35
  113.2 34.3 %collective-permute-start.7 = (bf16[576,1024]{1,0:T(8,128)(2,1)}, bf16[576,1024]{1,0:T(8,128)(2,1)}, u32[]{:S(2)}, u32[]{:S(2)}) collective-permute-start(bf16[576,1024]{1,0:T(8,128)(2,1)} %get-tuple-element.37), channel_id=1, source_target_pairs={{0,1},{1,2},{2,3},{3,0},{4,5},{5,6},{6,7},{7,4},{8,9},{9,10},{10,1... | collective-permute-start | bytes 3538952 | tf_op jit(solution)/shard_map/ppermute | solution.py:31
  116.5 48.9 %all-to-all-start.1 = ((bf16[128,2,2176]{2,1,0:T(2,128)(2,1)}), bf16[128,2,2176]{2,1,0:T(2,128)(2,1)S(1)}, u32[]{:S(2)}, u32[]{:S(2)}) async-start(bf16[128,2,2176]{2,1,0:T(2,128)(2,1)} %get-tuple-element.30), calls=%async_computation.1 | async-start | bytes 2228224 | tf_op jit(solution)/shard_map/all_to_all | solution.py:332
  133.7 4.8 %copy-start.6 = (bf16[576,1024]{1,0:T(8,128)(2,1)S(1)}, bf16[576,1024]{1,0:T(8,128)(2,1)}, u32[]{:S(2)}) copy-start(bf16[576,1024]{1,0:T(8,128)(2,1)} %get-tuple-element.42) | copy-start | bytes 3538948
  136.5 35.4 %collective-permute-start.9 = (bf16[576,1024]{1,0:T(8,128)(2,1)}, bf16[576,1024]{1,0:T(8,128)(2,1)}, u32[]{:S(2)}, u32[]{:S(2)}) collective-permute-start(bf16[576,1024]{1,0:T(8,128)(2,1)} %add_convert_fusion.1), channel_id=1, source_target_pairs={{0,1},{1,2},{2,3},{3,0},{4,5},{5,6},{6,7},{7,4},{8,9},{9,10},{10,1... | collective-permute-start | bytes 3538952 | tf_op jit(solution)/shard_map/ppermute | solution.py:31
  138.9 33.7 %collective-permute-start.11 = (bf16[576,1024]{1,0:T(8,128)(2,1)S(1)}, bf16[576,1024]{1,0:T(8,128)(2,1)S(1)}, u32[]{:S(2)}, u32[]{:S(2)}) collective-permute-start(bf16[576,1024]{1,0:T(8,128)(2,1)S(1)} %add_convert_fusion), channel_id=1, source_target_pairs={{0,3},{1,0},{2,1},{3,2},{4,7},{5,4},{6,5},{7,6},{8,11},{9,8},{10,9... | collective-permute-start | bytes 3538952 | tf_op jit(solution)/shard_map/ppermute | solution.py:35
  172.7 1.1 copy-start.7

commit v5 on v4

--- a/solution.py
+++ b/solution.py
@@ -134,10 +134,16 @@
     d_up = d_act * pre_gate * logistic
     d_pre = jnp.concatenate([d_gate, d_up], axis=0)
     d_pre_low = d_pre.astype(jnp.bfloat16)
-    for i, (send, grad) in enumerate(emits):
-        grad[gates] = dot(d_pre_low, x[i], PLAIN).astype(grad.dtype)
-        grad[downs] = dot(act, dy[i], PLAIN).astype(grad.dtype)
+    if len(emits) == 1:
+        ((send, factors),) = emits
+        factors[gates] = d_pre_low
+        factors[downs] = act
         send()
+    else:
+        for i, (send, grad) in enumerate(emits):
+            grad[gates] = dot(d_pre_low, x[i], PLAIN).astype(grad.dtype)
+            grad[downs] = dot(act, dy[i], PLAIN).astype(grad.dtype)
+            send()
     return d_pre.T.astype(jnp.bfloat16), d_s
 
 
@@ -165,7 +171,7 @@
         for wait, _ in weights[b]:
             wait()
         if b > 0:
-            grads = emits[2 * (b - 1) : 2 * b]
+            grads = emits[2 * (b - 1) : 2 * b] if b < count - 1 else emits[-2:-1]
             terms = block_grads(width, units, rows_ref, refs[b], grads)
             d_pre.append(terms[0])
             d_s = d_s + terms[1]
@@ -180,18 +186,19 @@
     send()
 
 
-def add_body(fetches, near_in, emits, near_out):
+def own_body(width, units, fetches, near_in, emits, near_out):
+    (wait_rows, rows_ref), (wait_factors, factors) = fetches[:2]
+    wait_rows()
+    wait_factors()
+    half, gates, downs = width // 2, slice(0, 2 * units), slice(2 * units, 3 * units)
     for i, (send, out) in enumerate(emits):
-        (wait_a, a), (wait_b, b) = fetches[2 * i : 2 * i + 2]
-        wait_a()
-        wait_b()
-        out[...] = (a[...].astype(jnp.float32) + b[...].astype(jnp.float32)).astype(out.dtype)
+        wait, came = fetches[2 + i]
+        wait()
+        for rows, at in ((gates, 0), (downs, width)):
+            side = rows_ref[:, at + i * half : at + (i + 1) * half]
+            grad = dot(factors[rows], side, PLAIN) + came[rows].astype(jnp.float32)
+            out[rows] = grad.astype(out.dtype)
         send()
-
-
-def added(*pairs, flops=0):
-    outs = [jax.ShapeDtypeStruct(a.shape, a.dtype) for a, _ in pairs]
-    return on_core(add_body, [v for pair in pairs for v in pair], [], outs, [], flops)
 
 
 def total_body(units, fetches, near_in, emits, near_out):
@@ -307,11 +314,15 @@
     )
     passing_a = right(far_grad_a, ring)
     passing_b = left(far_grad_b, ring)
-    nxt_a, nxt_b, prev_a, prev_b, mine_a, mine_b, returning = on_core(
+    nxt_a, nxt_b, prev_a, prev_b, factors, returning = on_core(
         functools.partial(rest_body, width, units, [2] * ring),
         [flat_rows, far_a, far_b, *after, *before, own_a, own_b],
         [far_pre, far_s],
-        [half_grad] * 6 + [shape((expert_count, CAP, width + LANES), bf16)],
+        [half_grad] * 4
+        + [
+            shape((3 * units, slot_count), bf16),
+            shape((expert_count, CAP, width + LANES), bf16),
+        ],
         [],
         4 * block_flops,
     )
@@ -319,7 +330,14 @@
     right_a = left(prev_a, ring)
     left_a = right((nxt_a.astype(f32) + passing_a.astype(f32)).astype(bf16), ring)
     right_b = left((prev_b.astype(f32) + passing_b.astype(f32)).astype(bf16), ring)
-    part_a, part_b = added((mine_a, right_a), (mine_b, left_b), flops=FLOPS_PART)
+    part_a, part_b = on_core(
+        functools.partial(own_body, width, units),
+        [flat_rows, factors, right_a, left_b],
+        [],
+        [half_grad, half_grad],
+        [],
+        FLOPS_PART,
+    )
     d_gate, d_up, d_down = on_core(
         functools.partial(total_body, units),
         [part_a, left_a, part_b, right_b],

time: 180 us -> 180 us (level)
  no operation moved by 1% of the time
where the time goes in v5:
time: 180 us; the launch traced here: 178 us
  starting transfers between devices  73.6 us (41%)
  waiting for transfers between devices  61.9 us (34%)
  Pallas kernels  31.1 us (17%)
  other arithmetic  6.21 us (3%)
  local copies, waits for them, and re-layouts  3.86 us (2%)
    pallas_call x4, Pallas kernels, on_core(): pl.pallas_call(kernel, out_shape=[*far_outs, *near_outs], in_specs=[hbm]...  27.7 us
    ppermute x6, starting transfers between devices, left(): lax.ppermute(part, 'block', [(i, (i - 1) % ring) for i in range(ring)])  22.2 us
    ppermute x6, waiting for transfers between devices, right(): lax.ppermute(part, 'block', [(i, (i + 1) % ring) for i in range(ring)])  21 us
    all_to_all x1, waiting for transfers between devices, on_device(): rows = lax.all_to_all(outgoing, ('node', 'expert'), 0, 0, tiled=True)  20.4 us
    all_to_all x1, starting transfers between devices, on_device(): rows = lax.all_to_all(outgoing, ('node', 'expert'), 0, 0, tiled=True)  18.8 us
    all_to_all x1, starting transfers between devices, on_device(): home = lax.all_to_all(returning, ('node', 'expert'), 0, 0, tiled=True)  17.2 us
    ppermute x6, starting transfers between devices, right(): lax.ppermute(part, 'block', [(i, (i + 1) % ring) for i in range(ring)])  15.5 us
    all_to_all x1, waiting for transfers between devices, on_device(): home = lax.all_to_all(returning, ('node', 'expert'), 0, 0, tiled=True)  13.7 us
  transfers between devices with their start and end apart: 14, of which 7 were waited for; matrix products, arithmetic and copies ran while one was open for 3% of the time, Pallas kernels for 15%

profile of v5, /device:TPU:1, one launch (start us, length us, event | category | flops | bytes accessed | tf_op | source)
XLA Modules:
  0.0 177.8 jit_solution(6147397669139253568)
XLA Ops:
  0.7 1.3 fusion.2
  1.9 0.1 copy-done.9
  2.0 0.2 copy-done.8
  2.2 0.1 fusion
  2.4 1.1 pad_maximum_fusion.refs_7_
  3.5 3.9 %collective-permute-start = (bf16[576,1024]{1,0:T(8,128)(2,1)}, bf16[576,1024]{1,0:T(8,128)(2,1)S(1)}, u32[]{:S(2)}, u32[]{:S(2)}) collective-permute-start(bf16[576,1024]{1,0:T(8,128)(2,1)} %pad_maximum_fusion.refs_7_), channel_id=1, source_target_pairs={{0,1},{1,2},{2,3},{3,0},{4,5},{5,6},{6,7},{7,4},{8,9},{9,10},{10,1... | collective-permute-start | bytes 3538952 | tf_op jit(solution)/shard_map/ppermute | solution.py:31
  7.5 0.0 copy-start
  7.5 0.0 copy-start.1
  7.5 0.0 copy-start.2
  7.5 0.0 copy-start.3
  7.5 1.1 pad_maximum_fusion.1.refs_8_
  8.7 3.2 %collective-permute-start.2 = (bf16[576,1024]{1,0:T(8,128)(2,1)}, bf16[576,1024]{1,0:T(8,128)(2,1)S(1)}, u32[]{:S(2)}, u32[]{:S(2)}) collective-permute-start(bf16[576,1024]{1,0:T(8,128)(2,1)} %pad_maximum_fusion.1.refs_8_), channel_id=1, source_target_pairs={{0,3},{1,0},{2,1},{3,2},{4,7},{5,4},{6,5},{7,6},{8,11},{9,8},{10,9... | collective-permute-start | bytes 3538952 | tf_op jit(solution)/shard_map/ppermute | solution.py:35
  11.9 2.3 %shard_map.110 = (bf16[128,2,4096]{2,1,0:T(2,128)(2,1)}, bf16[256,16]{1,0:T(8,128)(2,1)S(1)}) custom-call(s32[8,16]{1,0:T(8,128)S(1)} %bitcast.10, bf16[8,16]{1,0:T(8,128)(2,1)S(1)} %bitcast.12, bf16[16,2048]{1,0:T(8,128)(2,1)S(1)} %copy-done, bf16[16,2048]{1,0:T(8,128)(2,1)S(1)} %copy-done.1), custom_call_target="tpu_custom_call" | custom-call | bytes 2237184 | tf_op jit(solution)/shard_map/pallas_call | solution.py:264
  14.2 18.8 %all-to-all-start = ((bf16[128,2,4096]{2,1,0:T(2,128)(2,1)}), bf16[128,2,4096]{2,1,0:T(2,128)(2,1)}, u32[]{:S(2)}, u32[]{:S(2)}) async-start(bf16[128,2,4096]{2,1,0:T(2,128)(2,1)} %get-tuple-element.25), calls=%async_computation | async-start | bytes 4194304 | tf_op jit(solution)/shard_map/all_to_all | solution.py:301
  33.0 0.0 collective-permute-done.part_ref
  33.0 2.5 %collective-permute-start.1 = (bf16[576,1024]{1,0:T(8,128)(2,1)S(1)}, bf16[576,1024]{1,0:T(8,128)(2,1)S(1)}, u32[]{:S(2)}, u32[]{:S(2)}) collective-permute-start(bf16[576,1024]{1,0:T(8,128)(2,1)S(1)} %shard_map.111.refs_5_), channel_id=1, source_target_pairs={{0,1},{1,2},{2,3},{3,0},{4,5},{5,6},{6,7},{7,4},{8,9},{9,10},{10,1... | collective-permute-start | bytes 3538952 | tf_op jit(solution)/shard_map/ppermute | solution.py:31
  35.5 0.0 collective-permute-done.2.part_ref
  35.6 4.1 %collective-permute-start.3 = (bf16[576,1024]{1,0:T(8,128)(2,1)S(1)}, bf16[576,1024]{1,0:T(8,128)(2,1)}, u32[]{:S(2)}, u32[]{:S(2)}) collective-permute-start(bf16[576,1024]{1,0:T(8,128)(2,1)S(1)} %shard_map.112.refs_4_), channel_id=1, source_target_pairs={{0,3},{1,0},{2,1},{3,2},{4,7},{5,4},{6,5},{7,6},{8,11},{9,8},{10,9... | collective-permute-start | bytes 3538952 | tf_op jit(solution)/shard_map/ppermute | solution.py:35
  39.6 3.4 %collective-permute-start.4 = (bf16[576,1024]{1,0:T(8,128)(2,1)}, bf16[576,1024]{1,0:T(8,128)(2,1)}, u32[]{:S(2)}, u32[]{:S(2)}) collective-permute-start(bf16[576,1024]{1,0:T(8,128)(2,1)} %pad_maximum_fusion.refs_7_), channel_id=1, source_target_pairs={{0,3},{1,0},{2,1},{3,2},{4,7},{5,4},{6,5},{7,6},{8,11},{9,8},{10,9... | collective-permute-start | bytes 3538952 | tf_op jit(solution)/shard_map/ppermute | solution.py:35
  43.0 1.9 %collective-permute-start.5 = (bf16[576,1024]{1,0:T(8,128)(2,1)}, bf16[576,1024]{1,0:T(8,128)(2,1)}, u32[]{:S(2)}, u32[]{:S(2)}) collective-permute-start(bf16[576,1024]{1,0:T(8,128)(2,1)} %pad_maximum_fusion.1.refs_8_), channel_id=1, source_target_pairs={{0,1},{1,2},{2,3},{3,0},{4,5},{5,6},{6,7},{7,4},{8,9},{9,10},{10,1... | collective-permute-start | bytes 3538952 | tf_op jit(solution)/shard_map/ppermute | solution.py:31
  44.9 16.1 %collective-permute-done.1.refs_1_ = bf16[576,1024]{1,0:T(8,128)(2,1)S(1)} collective-permute-done((bf16[576,1024]{1,0:T(8,128)(2,1)S(1)}, bf16[576,1024]{1,0:T(8,128)(2,1)S(1)}, u32[]{:S(2)}, u32[]{:S(2)}) %collective-permute-start.1) | collective-permute-done | bytes 1179680 | tf_op jit(solution)/shard_map/ppermute | solution.py:31
  61.0 1.1 copy-done.10
  62.1 2.5 %collective-permute-done.3.refs_2_ = bf16[576,1024]{1,0:T(8,128)(2,1)} collective-permute-done((bf16[576,1024]{1,0:T(8,128)(2,1)S(1)}, bf16[576,1024]{1,0:T(8,128)(2,1)}, u32[]{:S(2)}, u32[]{:S(2)}) %collective-permute-start.3) | collective-permute-done | bytes 1179680 | tf_op jit(solution)/shard_map/ppermute | solution.py:35
  64.6 20.4 %all-to-all-done.refs_0_ = bf16[128,2,4096]{2,1,0:T(2,128)(2,1)} async-done(((bf16[128,2,4096]{2,1,0:T(2,128)(2,1)}), bf16[128,2,4096]{2,1,0:T(2,128)(2,1)}, u32[]{:S(2)}, u32[]{:S(2)}) %all-to-all-start) | async-done | bytes 2097184 | tf_op jit(solution)/shard_map/all_to_all | solution.py:301
  84.9 6.1 %shard_map.113 = (bf16[576,1024]{1,0:T(8,128)(2,1)}, bf16[576,1024]{1,0:T(8,128)(2,1)}, bf16[256,4096]{1,0:T(8,128)(2,1)}, bf16[256,384]{1,0:T(8,128)(2,1)}, f32[8,256]{1,0:T(8,128)}) custom-call(bf16[128,2,4096]{2,1,0:T(2,128)(2,1)} %all-to-all-done.refs_0_, bf16[576,1024]{1,0:T(8,128)(2,1)} %copy-done.10, bf16[576,1024]{1,0:T(8,128)(2,1)} %collective-permute-done.3.refs_2_), custom_call_target="tpu_custom_call" | custom-call | flops 1207959552 | bytes 9117696 | tf_op jit(solution)/shard_map/pallas_call | solution.py:79
  91.1 1.9 %collective-permute-start.8 = (bf16[576,1024]{1,0:T(8,128)(2,1)}, bf16[576,1024]{1,0:T(8,128)(2,1)S(1)}, u32[]{:S(2)}, u32[]{:S(2)}) collective-permute-start(bf16[576,1024]{1,0:T(8,128)(2,1)} %get-tuple-element.38), channel_id=1, source_target_pairs={{0,1},{1,2},{2,3},{3,0},{4,5},{5,6},{6,7},{7,4},{8,9},{9,10},{10,1... | collective-permute-start | bytes 3538952 | tf_op jit(solution)/shard_map/ppermute | solution.py:31
  93.0 4.8 %collective-permute-start.10 = (bf16[576,1024]{1,0:T(8,128)(2,1)}, bf16[576,1024]{1,0:T(8,128)(2,1)S(1)}, u32[]{:S(2)}, u32[]{:S(2)}) collective-permute-start(bf16[576,1024]{1,0:T(8,128)(2,1)} %get-tuple-element.41), channel_id=1, source_target_pairs={{0,3},{1,0},{2,1},{3,2},{4,7},{5,4},{6,5},{7,6},{8,11},{9,8},{10,9... | collective-permute-start | bytes 3538952 | tf_op jit(solution)/shard_map/ppermute | solution.py:35
  97.8 0.0 collective-permute-done.4.refs_3_
  97.8 0.0 collective-permute-done.5.refs_6_
  97.8 13.4 %shard_map.114 = (bf16[576,1024]{1,0:T(8,128)(2,1)}, bf16[576,1024]{1,0:T(8,128)(2,1)}, bf16[576,1024]{1,0:T(8,128)(2,1)}, bf16[576,1024]{1,0:T(8,128)(2,1)}, bf...) custom-call(bf16[256,4096]{1,0:T(8,128)(2,1)} %get-tuple-element.26.refs_0_, bf16[576,1024]{1,0:T(8,128)(2,1)} %copy-done.10, ...), custom_call_target="tpu_custom_call" | custom-call | flops 4831838208 | bytes 17866752 | tf_op jit(solution)/shard_map/pallas_call | solution.py:79
  111.2 2.0 %collective-permute-start.6 = (bf16[576,1024]{1,0:T(8,128)(2,1)}, bf16[576,1024]{1,0:T(8,128)(2,1)}, u32[]{:S(2)}, u32[]{:S(2)}) collective-permute-start(bf16[576,1024]{1,0:T(8,128)(2,1)} %get-tuple-element.34), channel_id=1, source_target_pairs={{0,3},{1,0},{2,1},{3,2},{4,7},{5,4},{6,5},{7,6},{8,11},{9,8},{10,9... | collective-permute-start | bytes 3538952 | tf_op jit(solution)/shard_map/ppermute | solution.py:35
  113.2 3.3 %collective-permute-start.7 = (bf16[576,1024]{1,0:T(8,128)(2,1)}, bf16[576,1024]{1,0:T(8,128)(2,1)}, u32[]{:S(2)}, u32[]{:S(2)}) collective-permute-start(bf16[576,1024]{1,0:T(8,128)(2,1)} %get-tuple-element.35), channel_id=1, source_target_pairs={{0,1},{1,2},{2,3},{3,0},{4,5},{5,6},{6,7},{7,4},{8,9},{9,10},{10,1... | collective-permute-start | bytes 3538952 | tf_op jit(solution)/shard_map/ppermute | solution.py:31
  116.5 17.2 %all-to-all-start.1 = ((bf16[128,2,2176]{2,1,0:T(2,128)(2,1)}), bf16[128,2,2176]{2,1,0:T(2,128)(2,1)S(1)}, u32[]{:S(2)}, u32[]{:S(2)}) async-start(bf16[128,2,2176]{2,1,0:T(2,128)(2,1)} %get-tuple-element.29), calls=%async_computation.1 | async-start | bytes 2228224 | tf_op jit(solution)/shard_map/all_to_all | solution.py:350
  133.7 0.0 collective-permute-done.8
  133.7 2.9 %add_convert_fusion.1 = bf16[576,1024]{1,0:T(8,128)(2,1)} fusion(bf16[576,1024]{1,0:T(8,128)(2,1)S(1)} %collective-permute-done.8, bf16[576,1024]{1,0:T(8,128)(2,1)} %get-tuple-element.37), kind=kLoop, calls=%fused_computation.1 | loop fusion | flops 2359296 | bytes 3538944 | tf_op jit(solution)/shard_map/convert_element_type | solution.py:331
  136.6 1.9 %collective-permute-start.9 = (bf16[576,1024]{1,0:T(8,128)(2,1)}, bf16[576,1024]{1,0:T(8,128)(2,1)}, u32[]{:S(2)}, u32[]{:S(2)}) collective-permute-start(bf16[576,1024]{1,0:T(8,128)(2,1)} %add_convert_fusion.1), channel_id=1, source_target_pairs={{0,1},{1,2},{2,3},{3,0},{4,5},{5,6},{6,7},{7,4},{8,9},{9,10},{10,1... | collective-permute-start | bytes 3538952 | tf_op jit(solution)/shard_map/ppermute | solution.py:31
  138.5 0.0 collective-permute-done.10
  138.5 0.5 add_convert_fusion
  139.0 4.9 %collective-permute-start.11 = (bf16[576,1024]{1,0:T(8,128)(2,1)S(1)}, bf16[576,1024]{1,0:T(8,128)(2,1)S(1)}, u32[]{:S(2)}, u32[]{:S(2)}) collective-permute-start(bf16[576,1024]{1,0:T(8,128)(2,1)S(1)} %add_convert_fusion), channel_id=1, source_target_pairs={{0,3},{1,0},{2,1},{3,2},{4,7},{5,4},{6,5},{7,6},{8,11},{9,8},{10,9... | collective-permute-start | bytes 3538952 | tf_op jit(solution)/shard_map/ppermute | solution.py:35
  143.9 3.6 %collective-permute-done.6.refs_2_ = bf16[576,1024]{1,0:T(8,128)(2,1)} collective-permute-done((bf16[576,1024]{1,0:T(8,128)(2,1)}, bf16[576,1024]{1,0:T(8,128)(2,1)}, u32[]{:S(2)}, u32[]{:S(2)}) %collective-permute-start.6) | collective-permute-done | bytes 1179680 | tf_op jit(solution)/shard_map/ppermute | solution.py:35
  147.5 4.2 %shard_map.116 = (bf16[576,1024]{1,0:T(8,128)(2,1)}, bf16[576,1024]{1,0:T(8,128)(2,1)}) custom-call(bf16[256,4096]{1,0:T(8,128)(2,1)} %get-tuple-element.26.refs_0_, bf16[576,256]{1,0:T(8,128)(2,1)} %get-tuple-element.33.refs_1_, bf16[576,1024]{1,0:T(8,128)(2,1)} %collective-permute-done.6.refs_2_, bf16[576,1024]{1,0:T(8,128)(2,1)} %collective-permute-done.7.refs_3_), custom_call_target="tpu_custom_call" | custom-call | flops 30000001024 | bytes 7110656 | tf_op jit(solution)/shard_map/pallas_call | solution.py:79
  151.7 13.7 %all-to-all-done.1.home_ref = bf16[128,2,2176]{2,1,0:T(2,128)(2,1)S(1)} async-done(((bf16[128,2,2176]{2,1,0:T(2,128)(2,1)}), bf16[128,2,2176]{2,1,0:T(2,128)(2,1)S(1)}, u32[]{:S(2)}, u32[]{:S(2)}) %all-to-all-start.1) | async-done | bytes 1114144 | tf_op jit(solution)/shard_map/all_to_all | solution.py:350
  165.4 1.0 shard_map.115
  166.4 0.6 convert_bitcast_fusion
  167.0 4.9 %collective-permute-done.9.refs_1_ = bf16[576,1024]{1,0:T(8,128)(2,1)} collective-permute-done((bf16[576,1024]{1,0:T(8,128)(2,1)}, bf16[576,1024]{1,0:T(8,128)(2,1)}, u32[]{:S(2)}, u32[]{:S(2)}) %collective-permute-start.9) | collective-permute-done | bytes 1179680 | tf_op jit(solution)/shard_map/ppermute | solution.py:31
  171.9 0.8 collective-permute-done.11.refs_3_
  172.6 1.0 copy-done.7
  173.7 4.0 %shard_map.117 = (bf16[192,2048]{1,0:T(8,128)(2,1)}, bf16[192,2048]{1,0:T(8,128)(2,1)}, bf16[192,2048]{1,0:T(8,128)(2,1)}) custom-call(bf16[576,1024]{1,0:T(8,128)(2,1)} %get-tuple-element.36.refs_0_, bf16[576,1024]{1,0:T(8,128)(2,1)} %collective-permute-done.9.refs_1_, bf16[576,1024]{1,0:T(8,128)(2,1)} %get-tuple-element.39.refs_2_, bf16[576,1024]{1,0:T(8,128)(2,1)} %copy-done.7), custom_call_target="tpu_custom_call" | custom-call | bytes 7077888 | tf_op jit(solution)/shard_map/pallas_call | solution.py:79
  (17 shorter events, 0.0 us)
Async XLA Ops:
  0.6 1.4 copy-start.9
  0.6 1.6 copy-start.8
  3.5 29.5 %collective-permute-start = (bf16[576,1024]{1,0:T(8,128)(2,1)}, bf16[576,1024]{1,0:T(8,128)(2,1)S(1)}, u32[]{:S(2)}, u32[]{:S(2)}) collective-permute-start(bf16[576,1024]{1,0:T(8,128)(2,1)} %pad_maximum_fusion.refs_7_), channel_id=1, source_target_pairs={{0,1},{1,2},{2,3},{3,0},{4,5},{5,6},{6,7},{7,4},{8,9},{9,10},{10,1... | collective-permute-start | bytes 3538952 | tf_op jit(solution)/shard_map/ppermute | solution.py:31
  7.5 4.4 %copy-start = (bf16[16,2048]{1,0:T(8,128)(2,1)S(1)}, bf16[16,2048]{1,0:T(8,128)(2,1)}, u32[]{:S(2)}) copy-start(bf16[16,2048]{1,0:T(8,128)(2,1)} %tokens_ref.1) | copy-start | bytes 196612
  7.5 4.4 %copy-start.1 = (bf16[16,2048]{1,0:T(8,128)(2,1)S(1)}, bf16[16,2048]{1,0:T(8,128)(2,1)}, u32[]{:S(2)}) copy-start(bf16[16,2048]{1,0:T(8,128)(2,1)} %grad_ref.1) | copy-start | bytes 196612
  7.5 4.4 %copy-start.2 = (s32[16,8]{0,1:T(8,128)S(1)}, s32[16,8]{0,1:T(8,128)}, u32[]{:S(2)}) copy-start(s32[16,8]{0,1:T(8,128)} %param.9) | copy-start | bytes 1540
  7.5 4.4 %copy-start.3 = (bf16[16,8]{0,1:T(8,128)(2,1)S(1)}, bf16[16,8]{0,1:T(8,128)(2,1)}, u32[]{:S(2)}) copy-start(bf16[16,8]{0,1:T(8,128)(2,1)} %param.10) | copy-start | bytes 772
  8.7 26.9 %collective-permute-start.2 = (bf16[576,1024]{1,0:T(8,128)(2,1)}, bf16[576,1024]{1,0:T(8,128)(2,1)S(1)}, u32[]{:S(2)}, u32[]{:S(2)}) collective-permute-start(bf16[576,1024]{1,0:T(8,128)(2,1)} %pad_maximum_fusion.1.refs_8_), channel_id=1, source_target_pairs={{0,3},{1,0},{2,1},{3,2},{4,7},{5,4},{6,5},{7,6},{8,11},{9,8},{10,9... | collective-permute-start | bytes 3538952 | tf_op jit(solution)/shard_map/ppermute | solution.py:35
  14.2 70.8 %all-to-all-start = ((bf16[128,2,4096]{2,1,0:T(2,128)(2,1)}), bf16[128,2,4096]{2,1,0:T(2,128)(2,1)}, u32[]{:S(2)}, u32[]{:S(2)}) async-start(bf16[128,2,4096]{2,1,0:T(2,128)(2,1)} %get-tuple-element.25), calls=%async_computation | async-start | bytes 4194304 | tf_op jit(solution)/shard_map/all_to_all | solution.py:301
  33.0 2.5 %copy-start.4 = (bf16[576,1024]{1,0:T(8,128)(2,1)}, bf16[576,1024]{1,0:T(8,128)(2,1)S(1)}, u32[]{:S(2)}) copy-start(bf16[576,1024]{1,0:T(8,128)(2,1)S(1)} %shard_map.111.refs_5_) | copy-start | bytes 3538948
  33.0 28.0 %collective-permute-start.1 = (bf16[576,1024]{1,0:T(8,128)(2,1)S(1)}, bf16[576,1024]{1,0:T(8,128)(2,1)S(1)}, u32[]{:S(2)}, u32[]{:S(2)}) collective-permute-start(bf16[576,1024]{1,0:T(8,128)(2,1)S(1)} %shard_map.111.refs_5_), channel_id=1, source_target_pairs={{0,1},{1,2},{2,3},{3,0},{4,5},{5,6},{6,7},{7,4},{8,9},{9,10},{10,1... | collective-permute-start | bytes 3538952 | tf_op jit(solution)/shard_map/ppermute | solution.py:31
  35.6 55.5 %copy-start.5 = (bf16[576,1024]{1,0:T(8,128)(2,1)}, bf16[576,1024]{1,0:T(8,128)(2,1)S(1)}, u32[]{:S(2)}) copy-start(bf16[576,1024]{1,0:T(8,128)(2,1)S(1)} %shard_map.112.refs_4_) | copy-start | bytes 3538948
  35.6 29.0 %collective-permute-start.3 = (bf16[576,1024]{1,0:T(8,128)(2,1)S(1)}, bf16[576,1024]{1,0:T(8,128)(2,1)}, u32[]{:S(2)}, u32[]{:S(2)}) collective-permute-start(bf16[576,1024]{1,0:T(8,128)(2,1)S(1)} %shard_map.112.refs_4_), channel_id=1, source_target_pairs={{0,3},{1,0},{2,1},{3,2},{4,7},{5,4},{6,5},{7,6},{8,11},{9,8},{10,9... | collective-permute-start | bytes 3538952 | tf_op jit(solution)/shard_map/ppermute | solution.py:35
  39.6 58.1 %collective-permute-start.4 = (bf16[576,1024]{1,0:T(8,128)(2,1)}, bf16[576,1024]{1,0:T(8,128)(2,1)}, u32[]{:S(2)}, u32[]{:S(2)}) collective-permute-start(bf16[576,1024]{1,0:T(8,128)(2,1)} %pad_maximum_fusion.refs_7_), channel_id=1, source_target_pairs={{0,3},{1,0},{2,1},{3,2},{4,7},{5,4},{6,5},{7,6},{8,11},{9,8},{10,9... | collective-permute-start | bytes 3538952 | tf_op jit(solution)/shard_map/ppermute | solution.py:35
  43.0 54.8 %collective-permute-start.5 = (bf16[576,1024]{1,0:T(8,128)(2,1)}, bf16[576,1024]{1,0:T(8,128)(2,1)}, u32[]{:S(2)}, u32[]{:S(2)}) collective-permute-start(bf16[576,1024]{1,0:T(8,128)(2,1)} %pad_maximum_fusion.1.refs_8_), channel_id=1, source_target_pairs={{0,1},{1,2},{2,3},{3,0},{4,5},{5,6},{6,7},{7,4},{8,9},{9,10},{10,1... | collective-permute-start | bytes 3538952 | tf_op jit(solution)/shard_map/ppermute | solution.py:31
  61.0 1.1 copy-start.10
  91.1 42.6 %collective-permute-start.8 = (bf16[576,1024]{1,0:T(8,128)(2,1)}, bf16[576,1024]{1,0:T(8,128)(2,1)S(1)}, u32[]{:S(2)}, u32[]{:S(2)}) collective-permute-start(bf16[576,1024]{1,0:T(8,128)(2,1)} %get-tuple-element.38), channel_id=1, source_target_pairs={{0,1},{1,2},{2,3},{3,0},{4,5},{5,6},{6,7},{7,4},{8,9},{9,10},{10,1... | collective-permute-start | bytes 3538952 | tf_op jit(solution)/shard_map/ppermute | solution.py:31
  93.0 45.5 %collective-permute-start.10 = (bf16[576,1024]{1,0:T(8,128)(2,1)}, bf16[576,1024]{1,0:T(8,128)(2,1)S(1)}, u32[]{:S(2)}, u32[]{:S(2)}) collective-permute-start(bf16[576,1024]{1,0:T(8,128)(2,1)} %get-tuple-element.41), channel_id=1, source_target_pairs={{0,3},{1,0},{2,1},{3,2},{4,7},{5,4},{6,5},{7,6},{8,11},{9,8},{10,9... | collective-permute-start | bytes 3538952 | tf_op jit(solution)/shard_map/ppermute | solution.py:35
  111.2 36.3 %collective-permute-start.6 = (bf16[576,1024]{1,0:T(8,128)(2,1)}, bf16[576,1024]{1,0:T(8,128)(2,1)}, u32[]{:S(2)}, u32[]{:S(2)}) collective-permute-start(bf16[576,1024]{1,0:T(8,128)(2,1)} %get-tuple-element.34), channel_id=1, source_target_pairs={{0,3},{1,0},{2,1},{3,2},{4,7},{5,4},{6,5},{7,6},{8,11},{9,8},{10,9... | collective-permute-start | bytes 3538952 | tf_op jit(solution)/shard_map/ppermute | solution.py:35
  113.2 34.3 %collective-permute-start.7 = (bf16[576,1024]{1,0:T(8,128)(2,1)}, bf16[576,1024]{1,0:T(8,128)(2,1)}, u32[]{:S(2)}, u32[]{:S(2)}) collective-permute-start(bf16[576,1024]{1,0:T(8,128)(2,1)} %get-tuple-element.35), channel_id=1, source_target_pairs={{0,1},{1,2},{2,3},{3,0},{4,5},{5,6},{6,7},{7,4},{8,9},{9,10},{10,1... | collective-permute-start | bytes 3538952 | tf_op jit(solution)/shard_map/ppermute | solution.py:31
  116.5 48.9 %all-to-all-start.1 = ((bf16[128,2,2176]{2,1,0:T(2,128)(2,1)}), bf16[128,2,2176]{2,1,0:T(2,128)(2,1)S(1)}, u32[]{:S(2)}, u32[]{:S(2)}) async-start(bf16[128,2,2176]{2,1,0:T(2,128)(2,1)} %get-tuple-element.29), calls=%async_computation.1 | async-start | bytes 2228224 | tf_op jit(solution)/shard_map/all_to_all | solution.py:350
  133.7 4.8 %copy-start.6 = (bf16[576,1024]{1,0:T(8,128)(2,1)S(1)}, bf16[576,1024]{1,0:T(8,128)(2,1)}, u32[]{:S(2)}) copy-start(bf16[576,1024]{1,0:T(8,128)(2,1)} %get-tuple-element.40) | copy-start | bytes 3538948
  136.6 35.3 %collective-permute-start.9 = (bf16[576,1024]{1,0:T(8,128)(2,1)}, bf16[576,1024]{1,0:T(8,128)(2,1)}, u32[]{:S(2)}, u32[]{:S(2)}) collective-permute-start(bf16[576,1024]{1,0:T(8,128)(2,1)} %add_convert_fusion.1), channel_id=1, source_target_pairs={{0,1},{1,2},{2,3},{3,0},{4,5},{5,6},{6,7},{7,4},{8,9},{9,10},{10,1... | collective-permute-start | bytes 3538952 | tf_op jit(solution)/shard_map/ppermute | solution.py:31
  139.0 33.6 %collective-permute-start.11 = (bf16[576,1024]{1,0:T(8,128)(2,1)S(1)}, bf16[576,1024]{1,0:T(8,128)(2,1)S(1)}, u32[]{:S(2)}, u32[]{:S(2)}) collective-permute-start(bf16[576,1024]{1,0:T(8,128)(2,1)S(1)} %add_convert_fusion), channel_id=1, source_target_pairs={{0,3},{1,0},{2,1},{3,2},{4,7},{5,4},{6,5},{7,6},{8,11},{9,8},{10,9... | collective-permute-start | bytes 3538952 | tf_op jit(solution)/shard_map/ppermute | solution.py:35
  172.6 1.0 copy-start.7
